TPU v7x, 32 devices: a whole 2x2x4 slice. The times are simulated.
32 devices in a mesh: dp: 8 (over y, x, core), rows: 4 (over z).
Axes of the slice: x: 2, y: 2, z: 4, core: 2. Of those that a mesh axis runs over, the one named last changes fastest.
Arguments:
- features: bfloat16 [8, 36, 48, 2048], P('dp', 'rows'), may hold values from -6 to 6
- extent: int32 [8, 2], P('dp'), may hold values from 18 to 48, as said below
- pointwise_weight: bfloat16 [2048, 256], P('dp', 'rows'), may hold values from -0.125 to 0.125
- pooling_weight: bfloat16 [2048, 256], P('dp', 'rows'), may hold values from -0.125 to 0.125
- dilated_weight: bfloat16 [55296, 256], P('dp', 'rows'), may hold values from -0.046875 to 0.046875
- projection_weight: bfloat16 [1280, 256], P('dp', 'rows'), may hold values from -0.15625 to 0.15625
- norm_gain: float32 [6, 256], replicated, may hold values from 0.5 to 1.5
- norm_bias: float32 [6, 256], replicated, may hold values from -3 to 3
- cotangent: bfloat16 [8, 36, 48, 256], P('dp', 'rows'), may hold values from -6 to 6
Outputs:
- output: bfloat16 [8, 36, 48, 256], P('dp', 'rows')
- feature_input_gradient: bfloat16 [8, 36, 48, 2048], P('dp', 'rows')
- pointwise_gradient: float32 [2048, 256], P('dp', 'rows')
- pooling_gradient: float32 [2048, 256], P('dp', 'rows')
- dilated_gradient: float32 [55296, 256], P('dp', 'rows')
- projection_gradient: float32 [1280, 256], P('dp', 'rows')
- norm_gain_gradient: float32 [6, 256], replicated
- norm_bias_gradient: float32 [6, 256], replicated
Inputs may be any that keep to these rules, and one draw needn't show every extreme that they name: `extent`: column 0 lies between 18 and 36, column 1 between 24 and 48; the first image fills its whole frame and the last has exactly 18 rows and 24 columns.
All inputs are finite; a program needn't handle non-finite values.
Results may differ from a plain program's by a relative error of at most 0.015.
Values may be sent and summed in bfloat16 or wider, within the bound.
No kernel may reach another device: no remote copies, remote signals or barrier semaphores. Data moves between devices by JAX's collectives and lax.ppermute only.
A program may use at most 384 MiB of HBM per device.

v0:
```python
import jax
import jax.numpy as jnp
from jax import lax
from jax.sharding import PartitionSpec as P

FEATURE_WIDTH = 2048
BRANCH_WIDTH = 256


epsilon = 1e-05
dilations = (6, 12, 18)


def passed_along(x, axis, by):
    size = lax.axis_size(axis)
    pairs = [(i, i + by) for i in range(size) if 0 <= i + by < size]
    return lax.ppermute(x, axis, pairs)


def silu_slope(values):
    sigma = jax.nn.sigmoid(values)
    return sigma * (1.0 + values * (1.0 - sigma))


def collect_weights(pointwise_weight, pooling_weight, dilated_weight, projection_weight):
    partial_pointwise, partial_pooling, partial_dilated, partial_projection = (
        lax.all_gather(pointwise_weight, "rows", axis=1, tiled=True),
        lax.all_gather(pooling_weight, "rows", axis=1, tiled=True),
        lax.all_gather(dilated_weight, "rows", axis=1, tiled=True),
        lax.all_gather(projection_weight, "rows", axis=1, tiled=True),
    )
    return (
        lax.all_gather(partial_pointwise, "dp", axis=0, tiled=True),
        lax.all_gather(partial_pooling, "dp", axis=0, tiled=True),
        lax.all_gather(partial_dilated, "dp", axis=0, tiled=True),
        lax.all_gather(partial_projection, "dp", axis=0, tiled=True),
    )


def stack_bands(values, band_depth):
    pieces = []
    for offset in list(range(band_depth, 0, -1)) + list(range(-1, -band_depth - 1, -1)):
        pieces.append(passed_along(values, "rows", offset))
    pieces.insert(band_depth, values)
    return jnp.concatenate(pieces, axis=1)


def stack_grad_bands(values, band_depth):
    pieces = []
    for offset in list(range(band_depth, 0, -1)) + list(range(-1, -band_depth - 1, -1)):
        pieces.append(passed_along(values, "rows", offset))
    pieces.insert(band_depth, values)
    return jnp.concatenate(pieces, axis=1)


def pad_columns(values, col_pad):
    return jnp.pad(values, ((0, 0), (0, 0), (col_pad, col_pad), (0, 0)))


def global_sums(parts):
    return lax.psum(parts, ("dp", "rows"))


def back_totals(parts):
    return lax.psum(parts, ("dp", "rows"))


def image_sums(values):
    return lax.psum(values, "rows")


def pixel_product(first_op, second_op):
    return lax.dot_general(
        first_op.reshape(-1, first_op.shape[-1]),
        second_op.reshape(-1, second_op.shape[-1]),
        (((0,), (0,)), ((), ())),
        preferred_element_type=jnp.float32,
    )


def on_device(
    features,
    extent,
    pointwise_weight,
    pooling_weight,
    dilated_weight,
    projection_weight,
    norm_gain,
    norm_bias,
    cotangent,
):
    images, band_rows, columns, channels = features.shape
    total_images = images * lax.axis_size("dp")
    col_pad = max(dilations)
    band_depth = -(-col_pad // band_rows)
    margin = band_depth * band_rows
    row_ids = lax.axis_index("rows") * band_rows + jnp.arange(band_rows, dtype=jnp.int32)
    col_ids = jnp.arange(columns, dtype=jnp.int32)
    validity_mask = (
        (row_ids[None, :, None] < extent[:, 0][:, None, None])
        & (col_ids[None, None, :] < extent[:, 1][:, None, None])
    ).astype(jnp.float32)
    valid_low = validity_mask.astype(jnp.bfloat16)
    pixel_mask = validity_mask[None, ..., None]
    image_region_sizes = (extent[:, 0] * extent[:, 1]).astype(jnp.float32)
    leader = (lax.axis_index("rows") == 0).astype(jnp.float32)
    masked = features * valid_low[..., None]
    complete_pointwise, complete_pooling, complete_dilated, complete_projection = collect_weights(
        pointwise_weight, pooling_weight, dilated_weight, projection_weight
    )
    padded = pad_columns(stack_bands(masked, band_depth), col_pad)
    branch_pre = [
        jnp.einsum("ihwc,ca->ihwa", masked, complete_pointwise, preferred_element_type=jnp.float32)
    ]
    for branch_index, dilation in enumerate(dilations):
        running = jnp.zeros((images, band_rows, columns, BRANCH_WIDTH), jnp.float32)
        for row_tap in range(3):
            for col_tap in range(3):
                leading_row = (branch_index * 9 + row_tap * 3 + col_tap) * FEATURE_WIDTH
                kernel_tap_weight = complete_dilated[leading_row : leading_row + FEATURE_WIDTH]
                row_first = margin + (row_tap - 1) * dilation
                col_first = col_pad + (col_tap - 1) * dilation
                window_in = padded[
                    :, row_first : row_first + band_rows, col_first : col_first + columns, :
                ]
                running = running + jnp.einsum(
                    "ihwc,ca->ihwa",
                    window_in,
                    kernel_tap_weight,
                    preferred_element_type=jnp.float32,
                )
        branch_pre.append(running)
    stacked = jnp.stack(branch_pre)
    local_pool = jnp.einsum("ihwc,ihw->ic", masked, valid_low, preferred_element_type=jnp.float32)
    pooled = image_sums(local_pool) / image_region_sizes[:, None]
    pooled_low = pooled.astype(jnp.bfloat16)
    pool_pre = jnp.dot(pooled_low, complete_pooling, preferred_element_type=jnp.float32)
    weighted = stacked * pixel_mask
    branch_sums, pool_total, pixel_count = global_sums(
        (
            jnp.sum(weighted, axis=(1, 2, 3)),
            leader * jnp.sum(pool_pre, axis=0),
            jnp.sum(validity_mask),
        )
    )
    average = branch_sums / pixel_count
    pool_average = pool_total / total_images
    centred = (stacked - average[:, None, None, None, :]) * pixel_mask
    pool_centred = pool_pre - pool_average
    squares, pool_squares = global_sums(
        (
            jnp.sum(centred * centred, axis=(1, 2, 3)),
            leader * jnp.sum(pool_centred * pool_centred, axis=0),
        )
    )
    spread = squares / pixel_count
    pool_spread = pool_squares / total_images
    inv_std = lax.rsqrt(spread + epsilon)
    normed = (stacked - average[:, None, None, None, :]) * inv_std[:, None, None, None, :]
    gain_four = norm_gain[:4, None, None, None, :]
    pre_act = gain_four * normed + norm_bias[:4, None, None, None, :]
    branch_acts = jax.nn.silu(pre_act) * pixel_mask
    pool_inv = lax.rsqrt(pool_spread + epsilon)
    pool_normed = (pool_pre - pool_average) * pool_inv
    pool_lift = norm_gain[4] * pool_normed + norm_bias[4]
    pool_act = jax.nn.silu(pool_lift)
    concat = jnp.concatenate(
        [
            branch_acts[0],
            branch_acts[1],
            branch_acts[2],
            branch_acts[3],
            pool_act[:, None, None, :] * validity_mask[..., None],
        ],
        axis=-1,
    ).astype(jnp.bfloat16)
    proj_pre = jnp.einsum(
        "ihwk,ka->ihwa", concat, complete_projection, preferred_element_type=jnp.float32
    )
    proj_weighted = proj_pre * validity_mask[..., None]
    (proj_sum,) = global_sums((jnp.sum(proj_weighted, axis=(0, 1, 2)),))
    proj_average = proj_sum / pixel_count
    proj_centred = (proj_pre - proj_average) * validity_mask[..., None]
    (proj_squares,) = global_sums((jnp.sum(proj_centred * proj_centred, axis=(0, 1, 2)),))
    proj_spread = proj_squares / pixel_count
    proj_inv = lax.rsqrt(proj_spread + epsilon)
    proj_normed = (proj_pre - proj_average) * proj_inv
    proj_lift = norm_gain[5] * proj_normed + norm_bias[5]
    output = (jax.nn.silu(proj_lift) * validity_mask[..., None]).astype(jnp.bfloat16)
    complete_pointwise, complete_pooling, complete_dilated, complete_projection = collect_weights(
        pointwise_weight, pooling_weight, dilated_weight, projection_weight
    )
    upstream = cotangent.astype(jnp.float32) * validity_mask[..., None] * silu_slope(proj_lift)
    proj_gain_grad, proj_bias_grad = back_totals(
        (jnp.sum(upstream * proj_normed, axis=(0, 1, 2)), jnp.sum(upstream, axis=(0, 1, 2)))
    )
    proj_delta = (
        validity_mask[..., None]
        * proj_inv
        * (
            norm_gain[5] * upstream
            - norm_gain[5] * proj_bias_grad / pixel_count
            - proj_normed * norm_gain[5] * proj_gain_grad / pixel_count
        )
    ).astype(jnp.bfloat16)
    concat_grad = jnp.einsum(
        "ihwa,ka->ihwk", proj_delta, complete_projection, preferred_element_type=jnp.float32
    )
    proj_weight_grad = pixel_product(concat, proj_delta)
    branch_grads = jnp.moveaxis(
        concat_grad[..., : 4 * BRANCH_WIDTH].reshape(images, band_rows, columns, 4, BRANCH_WIDTH),
        3,
        0,
    )
    pool_act_grad = image_sums(
        jnp.einsum("ihwa,ihw->ia", concat_grad[..., 4 * BRANCH_WIDTH :], validity_mask)
    )
    pool_up = pool_act_grad * silu_slope(pool_lift)
    branch_up = branch_grads * pixel_mask * silu_slope(pre_act)
    branch_gain_grad, branch_bias_grad, pool_gain_grad, pool_bias_grad = back_totals(
        (
            jnp.sum(branch_up * normed, axis=(1, 2, 3)),
            jnp.sum(branch_up, axis=(1, 2, 3)),
            leader * jnp.sum(pool_up * pool_normed, axis=0),
            leader * jnp.sum(pool_up, axis=0),
        )
    )
    deltas = (
        pixel_mask
        * inv_std[:, None, None, None, :]
        * (
            gain_four * branch_up
            - gain_four * branch_bias_grad[:, None, None, None, :] / pixel_count
            - normed * gain_four * branch_gain_grad[:, None, None, None, :] / pixel_count
        )
    ).astype(jnp.bfloat16)
    pool_delta = (
        pool_inv
        * (
            norm_gain[4] * pool_up
            - norm_gain[4] * pool_bias_grad / total_images
            - pool_normed * norm_gain[4] * pool_gain_grad / total_images
        )
    ).astype(jnp.bfloat16)
    one_weight_grad = pixel_product(masked, deltas[0])
    pool_weight_grad = leader * pixel_product(pooled_low, pool_delta)
    pool_input = (
        jnp.einsum("ia,ca->ic", pool_delta, complete_pooling, preferred_element_type=jnp.float32)
        / image_region_sizes[:, None]
    )
    input_sum = (
        jnp.einsum(
            "ihwa,ca->ihwc", deltas[0], complete_pointwise, preferred_element_type=jnp.float32
        )
        + pool_input[:, None, None, :]
    )
    grad_stack = jnp.concatenate([deltas[1], deltas[2], deltas[3]], axis=-1)
    grad_padded = pad_columns(stack_grad_bands(grad_stack, band_depth), col_pad)
    kernel_tap_gradients = []
    for branch_index, dilation in enumerate(dilations):
        for row_tap in range(3):
            for col_tap in range(3):
                leading_row = (branch_index * 9 + row_tap * 3 + col_tap) * FEATURE_WIDTH
                kernel_tap_weight = complete_dilated[leading_row : leading_row + FEATURE_WIDTH]
                row_back = margin - (row_tap - 1) * dilation
                col_back = col_pad - (col_tap - 1) * dilation
                source = grad_padded[
                    :,
                    row_back : row_back + band_rows,
                    col_back : col_back + columns,
                    branch_index * BRANCH_WIDTH : (branch_index + 1) * BRANCH_WIDTH,
                ]
                input_sum = input_sum + jnp.einsum(
                    "ihwa,ca->ihwc", source, kernel_tap_weight, preferred_element_type=jnp.float32
                )
                row_first = margin + (row_tap - 1) * dilation
                col_first = col_pad + (col_tap - 1) * dilation
                window_in = padded[
                    :, row_first : row_first + band_rows, col_first : col_first + columns, :
                ]
                kernel_tap_gradients.append(pixel_product(window_in, deltas[branch_index + 1]))
    dilated_weight_gradient = jnp.concatenate(kernel_tap_gradients, axis=0)
    feature_input_gradient = (input_sum * validity_mask[..., None]).astype(jnp.bfloat16)
    partial_pointwise, partial_pooling, partial_dilated, partial_projection = (
        lax.psum_scatter(
            one_weight_grad.astype(jnp.bfloat16), "dp", scatter_dimension=0, tiled=True
        ).astype(jnp.float32),
        lax.psum_scatter(
            pool_weight_grad.astype(jnp.bfloat16), "dp", scatter_dimension=0, tiled=True
        ).astype(jnp.float32),
        lax.psum_scatter(
            dilated_weight_gradient.astype(jnp.bfloat16), "dp", scatter_dimension=0, tiled=True
        ).astype(jnp.float32),
        lax.psum_scatter(
            proj_weight_grad.astype(jnp.bfloat16), "dp", scatter_dimension=0, tiled=True
        ).astype(jnp.float32),
    )
    pointwise_gradient, pooling_gradient, dilated_gradient, projection_gradient = (
        lax.psum_scatter(
            partial_pointwise.astype(jnp.bfloat16), "rows", scatter_dimension=1, tiled=True
        ).astype(jnp.float32),
        lax.psum_scatter(
            partial_pooling.astype(jnp.bfloat16), "rows", scatter_dimension=1, tiled=True
        ).astype(jnp.float32),
        lax.psum_scatter(
            partial_dilated.astype(jnp.bfloat16), "rows", scatter_dimension=1, tiled=True
        ).astype(jnp.float32),
        lax.psum_scatter(
            partial_projection.astype(jnp.bfloat16), "rows", scatter_dimension=1, tiled=True
        ).astype(jnp.float32),
    )
    norm_gain_gradient = jnp.concatenate(
        [branch_gain_grad, pool_gain_grad[None, :], proj_gain_grad[None, :]], axis=0
    )
    norm_bias_gradient = jnp.concatenate(
        [branch_bias_grad, pool_bias_grad[None, :], proj_bias_grad[None, :]], axis=0
    )
    return (
        output,
        feature_input_gradient,
        pointwise_gradient,
        pooling_gradient,
        dilated_gradient,
        projection_gradient,
        norm_gain_gradient,
        norm_bias_gradient,
    )


def solution(mesh):
    in_specs = (
        P("dp", "rows", None, None),
        P("dp", None),
        P("dp", "rows"),
        P("dp", "rows"),
        P("dp", "rows"),
        P("dp", "rows"),
        P(),
        P(),
        P("dp", "rows", None, None),
    )
    out_specs = (
        P("dp", "rows", None, None),
        P("dp", "rows", None, None),
        P("dp", "rows"),
        P("dp", "rows"),
        P("dp", "rows"),
        P("dp", "rows"),
        P(),
        P(),
    )
    return jax.shard_map(
        on_device, mesh=mesh, in_specs=in_specs, out_specs=out_specs, check_vma=False
    )
```

profile of v0, /device:TPU:0, one launch (start us, length us, event | category | flops | bytes accessed | tf_op | source)
XLA Modules:
  0.0 1057.3 jit_solution(4558801012944083468)
XLA Ops:
  7.9 17.0 %all_gather.36 = bf16[256,256]{0,1:T(8,128)(2,1)} all-gather(bf16[256,64]{0,1:T(8,128)(2,1)} %param.12), channel_id=1, replica_groups=mesh['dp'=8,'rows'=4] {'rows'}, dimensions={1}, use_global_device_ids=true | all-gather | bytes 163840 | tf_op jit(solution)/shard_map/all_gather | solution.py:28
  25.0 14.6 %all_gather.32 = bf16[256,256]{0,1:T(8,128)(2,1)S(1)} all-gather(bf16[256,64]{0,1:T(8,128)(2,1)} %param.11), channel_id=1, replica_groups=mesh['dp'=8,'rows'=4] {'rows'}, dimensions={1}, use_global_device_ids=true | all-gather | bytes 163840 | tf_op jit(solution)/shard_map/all_gather | solution.py:27
  40.4 44.0 %all-gather.7.cloned.1.call-done = bf16[6912,256]{0,1:T(8,128)(2,1)} async-done(((bf16[6912,64]{0,1:T(8,128)(2,1)}), bf16[6912,256]{0,1:T(8,128)(2,1)}) %all-gather.7.cloned.1.call-update) | async-done | bytes 3538960 | tf_op jit(solution)/shard_map/all_gather | solution.py:29
  84.4 5.9 copy.38
  94.9 6.8 collective-permute-start
  108.7 113.1 %all_gather.38 = bf16[160,256]{0,1:T(8,128)(2,1)} all-gather(bf16[160,64]{0,1:T(8,128)(2,1)} %param.14), channel_id=1, replica_groups=mesh['dp'=8,'rows'=4] {'rows'}, dimensions={1}, use_global_device_ids=true | all-gather | bytes 102400 | tf_op jit(solution)/shard_map/all_gather | solution.py:30
  225.7 8.6 psum.108
  236.4 14.8 %all_gather.39 = bf16[1280,256]{1,0:T(8,128)(2,1)} all-gather(bf16[160,256]{1,0:T(8,128)(2,1)} %copy.39), channel_id=1, replica_groups=mesh['dp'=8,'rows'=4] {'dp'}, dimensions={0}, use_global_device_ids=true | all-gather | bytes 737280 | tf_op jit(solution)/shard_map/all_gather | solution.py:36
  251.2 6.1 pad_maximum_fusion.3
  261.4 3.5 copy-done
  264.9 13.4 %pad_slice_fusion.5 = (bf16[1,9,48,2048]{3,2,1,0:T(8,128)(2,1)}, bf16[1,9,48,2048]{3,2,1,0:T(8,128)(2,1)}, bf16[1,9,48,2048]{3,2,1,0:T(8,128)(2,1)}, bf16[1,9,48...) fusion(bf16[1,45,48,2048]{3,2,1,0:T(8,128)(2,1)S(1)} %constant_, ...), kind=kLoop, calls=%fused_computation.5 | loop fusion | bytes 40697856 | tf_op jit(solution)/shard_map/slice | solution.py:123
  286.8 3.8 fusion.32
  290.6 3.9 fusion.42
  297.2 3.2 fusion.62
  300.3 3.3 fusion.66
  303.6 3.3 fusion.68
  334.1 39.9 %all-reduce.5 = (f32[4,256]{1,0:T(4,128)}, f32[]{:T(128)}, f32[256]{0:T(256)}) all-reduce(f32[4,256]{1,0:T(4,128)S(1)} %multiply_reduce_fusion.2, f32[]{:T(128)} %fusion.276, f32[256]{0:T(256)} %broadcast_multiply_fusion.2), channel_id=1, replica_groups=mesh['dp'=8,'rows'=4] {'dp','rows'}, use_global_device_ids=true, to_apply=%region_1.2 | all-reduce | flops 1281 | bytes 10248 | tf_op jit(solution)/shard_map/psum | solution.py:61
  377.5 39.3 %all-reduce.4 = (f32[4,256]{1,0:T(4,128)}, f32[256]{0:T(256)}) all-reduce(f32[4,256]{1,0:T(4,128)} %multiply_reduce_fusion.1, f32[256]{0:T(256)} %multiply_multiply_fusion.5), channel_id=1, replica_groups=mesh['dp'=8,'rows'=4] {'dp','rows'}, use_global_device_ids=true, to_apply=%region_5.6 | all-reduce | flops 1280 | bytes 10240 | tf_op jit(solution)/shard_map/psum | solution.py:61
  423.6 41.7 %psum.111 = f32[256]{0:T(256)} all-reduce(f32[256]{0:T(256)} %get-tuple-element.104), channel_id=1, replica_groups=mesh['dp'=8,'rows'=4] {'dp','rows'}, use_global_device_ids=true, to_apply=%region_10.11 | all-reduce | flops 256 | bytes 2048 | tf_op jit(solution)/shard_map/psum | solution.py:61
  468.9 39.2 %psum.112 = f32[256]{0:T(256)} all-reduce(f32[256]{0:T(256)} %multiply_reduce_fusion.3), channel_id=1, replica_groups=mesh['dp'=8,'rows'=4] {'dp','rows'}, use_global_device_ids=true, to_apply=%region_12.13 | all-reduce | flops 256 | bytes 2048 | tf_op jit(solution)/shard_map/psum | solution.py:61
  511.9 41.7 %all-reduce.3 = (f32[256]{0:T(256)}, f32[256]{0:T(256)}) all-reduce(f32[256]{0:T(256)} %get-tuple-element.43, f32[256]{0:T(256)} %get-tuple-element.42), channel_id=1, replica_groups=mesh['dp'=8,'rows'=4] {'dp','rows'}, use_global_device_ids=true, to_apply=%region_16.17 | all-reduce | flops 512 | bytes 4096 | tf_op jit(solution)/shard_map/psum | solution.py:65
  555.5 3.7 fusion.27
  559.2 4.0 convolution_bitcast_fusion
  568.0 10.6 psum.117
  581.7 4.4 fusion.312
  586.1 39.7 %all-reduce.2 = (f32[4,256]{1,0:T(4,128)}, f32[4,256]{1,0:T(4,128)}, f32[1,256]{1,0:T(1,128)}, f32[256]{0:T(256)}) all-reduce(f32[4,256]{1,0:T(4,128)} %get-tuple-element.41, f32[4,256]{1,0:T(4,128)} %get-tuple-element.40, f32[1,256]{1,0:T(1,128)} %multiply_multiply_fusion.2, ...), channel_id=1, replica_groups=mesh['dp'=8,'rows'=4] {'dp','rows'}, use_global_device_ids=true, to_apply=%region_20.21 | all-reduce | flops 2560 | bytes 20480 | tf_op jit(solution)/shard_map/psum | solution.py:65
  658.3 3.4 fusion.14
  665.4 3.4 fusion.17
  670.6 3.4 fusion.19
  677.1 3.3 fusion.21
  690.9 4.6 collective-permute-start.5
  696.8 5.9 collective-permute-start.4
  702.7 3.7 fusion.179
  706.4 3.8 fusion.188
  710.2 3.8 fusion.197
  718.3 4.7 collective-permute-done.4
  723.3 13.9 %collective-permute-done.7 = bf16[1,9,48,768]{3,2,1,0:T(8,128)(2,1)S(1)} collective-permute-done((bf16[1,9,48,768]{3,2,1,0:T(8,128)(2,1)S(1)}, bf16[1,9,48,768]{3,2,1,0:T(8,128)(2,1)S(1)}, u32[]{:S(2)}, u32[]{:S(2)}) %collective-permute-start.7) | collective-permute-done | bytes 663584 | tf_op jit(solution)/shard_map/ppermute | solution.py:17
  737.2 3.8 fusion.176
  741.1 3.8 fusion.182
  744.8 3.8 fusion.185
  748.6 3.6 fusion.191
  752.3 4.2 fusion.175
  756.4 4.2 fusion.177
  760.6 4.3 fusion.178
  765.0 4.3 fusion.180
  769.2 4.2 fusion.181
  773.5 4.3 fusion.183
  779.5 4.0 fusion.184
  785.2 3.7 fusion.186
  789.2 3.9 fusion.187
  793.0 125.6 %reduce-scatter.21.cloned.1.call-done = bf16[6912,256]{1,0:T(8,128)(2,1)} async-done(((bf16[55296,256]{1,0:T(8,128)(2,1)}), bf16[6912,256]{1,0:T(8,128)(2,1)}) %reduce-scatter.21.cloned.1.call-update) | async-done | bytes 3538960 | tf_op jit(solution)/shard_map/reduce_scatter | solution.py:291
  918.6 6.0 copy.48
  924.6 3.7 fusion.189
  928.3 3.7 fusion.190
  931.9 3.7 fusion.192
  935.6 3.7 fusion.193
  939.3 3.7 fusion.195
  943.0 3.7 fusion.196
  946.7 3.6 fusion.198
  950.3 3.7 fusion.199
  954.0 3.9 fusion.194
  957.9 3.8 fusion.200
  961.7 32.1 %fusion.87 = bf16[1,9,48,2048]{3,2,1,0:T(8,128)(2,1)} fusion(f32[9,48]{1,0:T(8,128)S(1)} %get-tuple-element.101, f32[9,48,2048]{2,1,0:T(8,128)} %fusion.200, f32[9,48,2048]{2,1,0:T(8,128)} %fusion.199, f32[9,48,2048]{2,1,0:T(8,128)} %fusion.198, f32[9,48,2048]{2,1,0:T(8,128)} %fusion.197, f32[9,48,2048]{2,1,0:T(8,128)} %fusion.196, ...), kind=kOutput, calls=%fused_computation.168 | convolution fusion | flops 479526912 | bytes 101697216 | tf_op jit(solution)/shard_map/ihwa,ca->ihwc/dot_general | solution.py:273
  998.4 48.3 %reduce-scatter.27.cloned.1.call-done = bf16[64,6912]{1,0:T(8,128)(2,1)} async-done(((bf16[256,6912]{1,0:T(8,128)(2,1)}), bf16[64,6912]{1,0:T(8,128)(2,1)}) %reduce-scatter.27.cloned.1.call-update) | async-done | bytes 884752
  (365 shorter events, 156.3 us)
Async XLA Ops:
  7.2 77.2 %all-gather.7.cloned.1.call-start = ((), (), s32[]{:S(2)}) async-start(), calls=%async_computation.9 | async-start | bytes 4423680 | tf_op jit(solution)/shard_map/all_gather | solution.py:29
  7.9 270.5 %all-gather.11.cloned.1.call-start = ((), (), s32[]{:S(2)}) async-start(), calls=%async_computation.11 | async-start | bytes 1179648 | tf_op jit(solution)/shard_map/all_gather | solution.py:34
  24.9 255.6 %all-gather.5.cloned.1.call-start = ((), (), s32[]{:S(2)}) async-start(), calls=%async_computation.8 | async-start | bytes 1179648 | tf_op jit(solution)/shard_map/all_gather | solution.py:33
  40.3 242.1 %all-gather.9.cloned.1.call-start = ((), (), s32[]{:S(2)}) async-start(), calls=%async_computation.10 | async-start | bytes 31850496 | tf_op jit(solution)/shard_map/all_gather | solution.py:35
  90.3 3.1 copy-start.6
  90.3 16.5 %copy-start.81 = (f32[6,256]{1,0:T(8,128)S(1)}, f32[6,256]{1,0:T(8,128)}, u32[]{:S(2)}) copy-start(f32[6,256]{1,0:T(8,128)} %param.15) | copy-start | bytes 18436
  90.3 687.4 %reduce-scatter.23.cloned.1.call-start = ((), (), s32[]{:S(2)}) async-start(), calls=%async_computation.16 | async-start | bytes 737280 | tf_op jit(solution)/shard_map/reduce_scatter | solution.py:294
  93.4 8.3 copy-start.68
  93.6 157.5 %collective-permute-start.3 = (bf16[1,9,48,2048]{3,2,1,0:T(8,128)(2,1)S(1)}, bf16[1,9,48,2048]{3,2,1,0:T(8,128)(2,1)S(1)}, u32[]{:S(2)}, u32[]{:S(2)}) collective-permute-start(bf16[1,9,48,2048]{3,2,1,0:T(8,128)(2,1)S(1)} %broadcast_multiply_fusion), channel_id=1, source_target_pairs={{2,0},{3,1},{6,4},{7,5},{10,8},{11,9},{14,12},{15,13},{18,16},{19,... | collective-permute-start | bytes 5308424 | tf_op jit(solution)/shard_map/ppermute | solution.py:17
  94.9 156.2 %collective-permute-start = (bf16[1,9,48,2048]{3,2,1,0:T(8,128)(2,1)S(1)}, bf16[1,9,48,2048]{3,2,1,0:T(8,128)(2,1)}, u32[]{:S(2)}, u32[]{:S(2)}) collective-permute-start(bf16[1,9,48,2048]{3,2,1,0:T(8,128)(2,1)S(1)} %broadcast_multiply_fusion), channel_id=1, source_target_pairs={{0,2},{1,3},{4,6},{5,7},{8,10},{9,11},{12,14},{13,15},{16,18},{17,... | collective-permute-start | bytes 5308424 | tf_op jit(solution)/shard_map/ppermute | solution.py:17
  101.7 149.4 %collective-permute-start.1 = (bf16[1,9,48,2048]{3,2,1,0:T(8,128)(2,1)S(1)}, bf16[1,9,48,2048]{3,2,1,0:T(8,128)(2,1)}, u32[]{:S(2)}, u32[]{:S(2)}) collective-permute-start(bf16[1,9,48,2048]{3,2,1,0:T(8,128)(2,1)S(1)} %broadcast_multiply_fusion), channel_id=1, source_target_pairs={{0,1},{1,2},{2,3},{4,5},{5,6},{6,7},{8,9},{9,10},{10,11},{12,13},{... | collective-permute-start | bytes 5308424 | tf_op jit(solution)/shard_map/ppermute | solution.py:17
  104.2 146.9 %collective-permute-start.2 = (bf16[1,9,48,2048]{3,2,1,0:T(8,128)(2,1)S(1)}, bf16[1,9,48,2048]{3,2,1,0:T(8,128)(2,1)}, u32[]{:S(2)}, u32[]{:S(2)}) collective-permute-start(bf16[1,9,48,2048]{3,2,1,0:T(8,128)(2,1)S(1)} %broadcast_multiply_fusion), channel_id=1, source_target_pairs={{1,0},{2,1},{3,2},{5,4},{6,5},{7,6},{9,8},{10,9},{11,10},{13,12},{... | collective-permute-start | bytes 5308424 | tf_op jit(solution)/shard_map/ppermute | solution.py:17
  251.2 10.1 copy-start.4
  261.4 3.5 copy-start
  280.0 4.5 copy-start.75
  282.5 24.4 %copy-start.1 = (bf16[55296,256]{1,0:T(8,128)(2,1)S(1)}, bf16[55296,256]{1,0:T(8,128)(2,1)}, u32[]{:S(2)}) copy-start(bf16[55296,256]{1,0:T(8,128)(2,1)} %all-gather.9.cloned.1.call-done) | copy-start | bytes 84934656
  300.3 6.6 copy-start.46
  303.6 4.7 copy-start.48
  306.9 2.8 copy-start.20
  308.3 2.8 copy-start.22
  315.3 2.8 copy-start.40
  316.7 2.8 copy-start.16
  319.5 2.8 copy-start.24
  320.9 2.8 copy-start.26
  322.3 2.8 copy-start.28
  322.3 5.9 slice-start
  323.7 3.2 copy-start.30
  323.7 4.5 slice-start.1
  333.9 84.3 %copy-start.65 = (f32[4,256]{1,0:T(4,128)S(1)}, f32[4,256]{1,0:T(4,128)}, u32[]{:S(2)}) copy-start(f32[4,256]{1,0:T(4,128)} %slice.405) | copy-start | bytes 12292
  416.8 2.8 copy-start.76
  416.8 2.8 copy-start.91
  416.8 2.8 copy-start.97
  416.8 4.9 copy-start.52
  418.2 5.4 copy-start.66
  563.2 220.2 %reduce-scatter.15.cloned.1.call-start = ((), (), s32[]{:S(2)}) async-start(), calls=%async_computation.12 | async-start | bytes 1179648 | tf_op jit(solution)/shard_map/reduce_scatter | solution.py:285
  563.3 2.9 copy-start.71
  627.2 3.1 copy-start.50
  630.2 59.2 %copy-start.8 = (bf16[1,9,48,256]{3,2,1,0:T(8,128)(2,1)}, bf16[1,9,48,256]{3,2,1,0:T(8,128)(2,1)S(1)}, u32[]{:S(2)}) copy-start(bf16[1,9,48,256]{3,2,1,0:T(8,128)(2,1)S(1)} %get-tuple-element.88) | copy-start | bytes 663556
  630.2 59.2 %copy-start.10 = (bf16[1,9,48,256]{3,2,1,0:T(8,128)(2,1)}, bf16[1,9,48,256]{3,2,1,0:T(8,128)(2,1)S(1)}, u32[]{:S(2)}) copy-start(bf16[1,9,48,256]{3,2,1,0:T(8,128)(2,1)S(1)} %get-tuple-element.89) | copy-start | bytes 663556
  658.3 3.4 copy-start.36
  665.3 123.6 %reduce-scatter.17.cloned.1.call-start = ((), (), s32[]{:S(2)}) async-start(), calls=%async_computation.13 | async-start | bytes 1179648 | tf_op jit(solution)/shard_map/reduce_scatter | solution.py:288
  665.4 3.4 copy-start.33
  670.6 3.4 copy-start.32
  677.0 241.6 %reduce-scatter.21.cloned.1.call-start = ((), (), s32[]{:S(2)}) async-start(), calls=%async_computation.15 | async-start | bytes 31850496 | tf_op jit(solution)/shard_map/reduce_scatter | solution.py:291
  689.3 13.4 %copy-start.3 = (bf16[4,1,9,48,256]{4,3,2,1,0:T(8,128)(2,1)S(1)}, bf16[4,1,9,48,256]{4,3,2,1,0:T(8,128)(2,1)}, u32[]{:S(2)}) copy-start(bf16[4,1,9,48,256]{4,3,2,1,0:T(8,128)(2,1)} %copy-done.2) | copy-start | bytes 2654212
  689.3 304.5 %reduce-scatter.29.cloned.1.call-start = ((), (), s32[]{:S(2)}) async-start(), calls=%async_computation.19 | async-start | bytes 163840
  689.5 33.8 %collective-permute-start.6 = (bf16[1,9,48,768]{3,2,1,0:T(8,128)(2,1)S(1)}, bf16[1,9,48,768]{3,2,1,0:T(8,128)(2,1)S(1)}, u32[]{:S(2)}, u32[]{:S(2)}) collective-permute-start(bf16[1,9,48,768]{3,2,1,0:T(8,128)(2,1)S(1)} %pad_maximum_fusion.5), channel_id=1, source_target_pairs={{1,0},{2,1},{3,2},{5,4},{6,5},{7,6},{9,8},{10,9},{11,10},{13,12},{... | collective-permute-start | bytes 1990664 | tf_op jit(solution)/shard_map/ppermute | solution.py:17
  690.9 32.2 %collective-permute-start.5 = (bf16[1,9,48,768]{3,2,1,0:T(8,128)(2,1)S(1)}, bf16[1,9,48,768]{3,2,1,0:T(8,128)(2,1)S(1)}, u32[]{:S(2)}, u32[]{:S(2)}) collective-permute-start(bf16[1,9,48,768]{3,2,1,0:T(8,128)(2,1)S(1)} %pad_maximum_fusion.5), channel_id=1, source_target_pairs={{0,1},{1,2},{2,3},{4,5},{5,6},{6,7},{8,9},{9,10},{10,11},{12,13},{... | collective-permute-start | bytes 1990664 | tf_op jit(solution)/shard_map/ppermute | solution.py:17
  695.5 41.7 %collective-permute-start.7 = (bf16[1,9,48,768]{3,2,1,0:T(8,128)(2,1)S(1)}, bf16[1,9,48,768]{3,2,1,0:T(8,128)(2,1)S(1)}, u32[]{:S(2)}, u32[]{:S(2)}) collective-permute-start(bf16[1,9,48,768]{3,2,1,0:T(8,128)(2,1)S(1)} %pad_maximum_fusion.5), channel_id=1, source_target_pairs={{2,0},{3,1},{6,4},{7,5},{10,8},{11,9},{14,12},{15,13},{18,16},{19,... | collective-permute-start | bytes 1990664 | tf_op jit(solution)/shard_map/ppermute | solution.py:17
  696.8 26.3 %collective-permute-start.4 = (bf16[1,9,48,768]{3,2,1,0:T(8,128)(2,1)S(1)}, bf16[1,9,48,768]{3,2,1,0:T(8,128)(2,1)S(1)}, u32[]{:S(2)}, u32[]{:S(2)}) collective-permute-start(bf16[1,9,48,768]{3,2,1,0:T(8,128)(2,1)S(1)} %pad_maximum_fusion.5), channel_id=1, source_target_pairs={{0,2},{1,3},{4,6},{5,7},{8,10},{9,11},{12,14},{13,15},{16,18},{17,... | collective-permute-start | bytes 1990664 | tf_op jit(solution)/shard_map/ppermute | solution.py:17
  710.2 3.8 copy-start.51
  714.0 2.8 copy-start.13
  714.0 2.8 copy-start.73
  714.0 3.7 copy-start.77
  714.0 3.7 copy-start.80
  714.1 3.6 copy-start.87
  714.1 3.6 copy-start.96
  716.5 6.6 copy-start.9
  716.6 6.6 copy-start.11
  723.1 25.5 %copy-start.15 = (bf16[1,9,48,768]{3,2,1,0:T(8,128)(2,1)}, bf16[1,9,48,768]{3,2,1,0:T(8,128)(2,1)S(1)}, u32[]{:S(2)}) copy-start(bf16[1,9,48,768]{3,2,1,0:T(8,128)(2,1)S(1)} %collective-permute-done.4) | copy-start | bytes 1990660
  737.2 7.6 copy-start.14
  779.5 216.0 %reduce-scatter.25.cloned.1.call-start = ((), (), s32[]{:S(2)}) async-start(), calls=%async_computation.17 | async-start | bytes 163840
  785.2 211.9 %reduce-scatter.19.cloned.1.call-start = ((), (), s32[]{:S(2)}) async-start(), calls=%async_computation.14 | async-start | bytes 163840 | tf_op jit(solution)/shard_map/reduce_scatter | solution.py:302
  788.9 257.8 %reduce-scatter.27.cloned.1.call-start = ((), (), s32[]{:S(2)}) async-start(), calls=%async_computation.18 | async-start | bytes 4423680
  (58 other events, 111.1 us)
Sparse Core Ops, SparseCore 0:
  9.6 74.7 all-gather.6
  86.3 22.1 all-gather.10
  110.9 23.4 all-gather.4
  136.1 141.2 all-gather.8
  563.4 33.8 reduce-scatter.22
  665.4 36.3 reduce-scatter.14
  705.6 35.9 reduce-scatter.16
  745.3 173.2 reduce-scatter.20
  920.9 19.1 reduce-scatter.28
  942.8 17.2 reduce-scatter.24
  962.4 17.3 reduce-scatter.18
  982.0 64.6 reduce-scatter.26
where the time goes:
time: 1070 us; the launch traced here: 1060 us
  blocking collectives  420 us (39%)
  matrix products  259 us (24%)
  waiting for transfers between devices  237 us (22%)
  local copies, waits for them, and re-layouts  54.7 us (5%)
  other arithmetic  44 us (4%)
  starting transfers between devices  25.8 us (2%)
  between operations  16.7 us (2%)
    psum x4, blocking collectives, global_sums(): return lax.psum(parts, ('dp', 'rows'))  160 us
    dot_general x27, matrix products, on_device(): jnp.einsum('ihwa,ca->ihwc', source, kernel_tap_weight, preferred_element_...  132 us
    reduce_scatter x1, waiting for transfers between devices, on_device(): lax.psum_scatter(dilated_weight_gradient.astype(jnp.bfloat16), 'dp', scat...  126 us
    all_gather x1, blocking collectives, collect_weights(): lax.all_gather(projection_weight, 'rows', axis=1, tiled=True)  113 us
    psum x2, blocking collectives, back_totals(): return lax.psum(parts, ('dp', 'rows'))  81.5 us
    dot_general x29, matrix products, pixel_product(): lax.dot_general(first_op.reshape(-1, first_op.shape[-1]), second_op.resha...  60.5 us
    dot_general x27, matrix products, on_device(): jnp.einsum('ihwc,ca->ihwa', window_in, kernel_tap_weight, preferred_eleme...  50.8 us
    unnamed x15, waiting for transfers between devices  49.1 us
  transfers between devices with their start and end apart: 20, of which 5 were waited for; matrix products, arithmetic and copies ran while one was open for 25% of the time, Pallas kernels for 0%

commit v1 on v0

v1 whole, which is shorter than its diff:
```python
import jax
import jax.numpy as jnp
from jax import lax
from jax.experimental import pallas as pl
from jax.experimental.pallas import tpu as pltpu
from jax.sharding import PartitionSpec as P

epsilon = 1e-05
dilations = (6, 12, 18)
LANES = 128
BLOCK_ROWS = 6
AXES = ("dp", "rows")
FULL, SHORT, PER_CHIP = 14, 13, 27
NT = (((1,), (1,)), ((), ()))
TN = (((0,), (0,)), ((), ()))
NN = (((1,), (0,)), ((), ()))


def dot(first, second, dims):
    return lax.dot_general(first, second, dims, preferred_element_type=jnp.float32)


def silu_slope(values):
    sigma = jax.nn.sigmoid(values)
    return sigma * (1.0 + values * (1.0 - sigma))


class Place:
    def __init__(self):
        self.nd, self.nr = lax.axis_size("dp"), lax.axis_size("rows")
        self.nzl = self.nr // 2
        d, z = lax.axis_index("dp"), lax.axis_index("rows")
        self.d, self.z = d, z
        self.m, self.c = d // 2, d % 2
        self.zh, self.zl = z // self.nzl, z % self.nzl
        self.part = self.c * self.nzl + self.zl
        self.image = 2 * self.m + self.zh

    def send(self, x, target):
        nzl = self.nzl
        pairs = []
        for flat in range(self.nd * self.nr):
            d, z = divmod(flat, self.nr)
            m, c, zh, zl = target(d // 2, d % 2, z // nzl, z % nzl)
            pairs.append((flat, (2 * m + c) * self.nr + zh * nzl + zl))
        return lax.ppermute(x, AXES, pairs)

    def swap(self, x, m=0, c=0, zh=0, zl=0):
        return self.send(x, lambda a, b, e, f: (a ^ m, b ^ c, e ^ zh, f ^ zl))


def by_xor(items, index):
    items = list(items)
    bit = 1
    while bit < len(items):
        flip = (index & bit) != 0
        items = [jnp.where(flip, items[k ^ bit], items[k]) for k in range(len(items))]
        bit *= 2
    return items


def tree(items):
    items = list(items)
    while len(items) > 1:
        items = [items[i] + items[i + 1] for i in range(0, len(items), 2)]
    return items[0]


def exchange_stages(place):
    return (
        [dict(c=1)],
        [dict(m=k) for k in range(1, place.nd // 2)],
        [dict(zh=k // place.nzl, zl=k % place.nzl) for k in range(1, place.nr)],
    )


def total(place, x):
    for stage in exchange_stages(place):
        x = tree([x] + [place.swap(x, **s) for s in stage])
    return x


def moments(place, sums, squares, count, extra=None):
    width = sums.shape[1]
    k = sums.shape[0]
    rows = [sums, squares, jnp.full((1, width), count, jnp.float32)]
    if extra is not None:
        rows.append(extra)
    x = jnp.concatenate(rows, axis=0)
    for stage in exchange_stages(place):
        xs = [x] + [place.swap(x, **s) for s in stage]
        whole = tree(xs)
        n = whole[2 * k : 2 * k + 1]
        mean = whole[:k] / jnp.maximum(n, 1.0)
        between = []
        for y in xs:
            own = y[2 * k : 2 * k + 1]
            gap = y[:k] / jnp.maximum(own, 1.0) - mean
            between.append(own * gap * gap)
        x = jnp.concatenate([whole[:k], whole[k : 2 * k] + tree(between), whole[2 * k :]], axis=0)
    n = x[2 * k : 2 * k + 1]
    return x[:k] / n, x[k : 2 * k] / n, n, x[2 * k + 1 :]


def local_moments(values, mask, count):
    sums = jnp.sum(values * mask, axis=0, keepdims=True)
    centred = (values - sums / jnp.maximum(count, 1.0)) * mask
    return sums, jnp.sum(centred * centred, axis=0, keepdims=True)


def line_pieces(place, dilated, pointwise, pooling):
    tiles = lambda w: jnp.transpose(w.T.reshape(w.shape[1], w.shape[0] // LANES, LANES), (1, 0, 2))
    dil, one, pool = tiles(dilated), tiles(pointwise), tiles(pooling)
    same = [jnp.concatenate([dil[r::4][:FULL], one[r : r + 1], pool[r : r + 1]], axis=0) for r in range(2)]
    other = [dil[2 + r :: 4][:SHORT] for r in range(2)]
    same, other = by_xor(same, place.zl), by_xor(other, place.zl)
    halves = []
    for kh in range(2):
        got = []
        for kc, source in ((0, same), (1, other)):
            for kl in range(2):
                piece = source[kl]
                if (kc, kh, kl) != (0, 0, 0):
                    piece = place.swap(piece, c=kc, zh=kh, zl=kl)
                got.append(piece)
        halves.append(jnp.concatenate(got, axis=0))
    return halves


def plane_gather(place, halves):
    own, far = halves
    own_x, own_y = place.swap(own, m=1), place.swap(own, m=2)
    far_x, far_y = place.swap(far, m=1), place.swap(far, m=2)
    own_d, far_d = place.swap(own_x, m=2), place.swap(far_y, m=1)
    return [[own, far], [own_x, far_x], [own_y, far_y], [own_d, far_d]]


def add_low(first, *others):
    out = first.astype(jnp.float32)
    for o in others:
        out = out + o.astype(jnp.float32)
    return out.astype(jnp.bfloat16)


def plane_scatter(place, pieces):
    own_d, far_d = place.swap(pieces[3][0], m=2), place.swap(pieces[3][1], m=1)
    own_y, far_x = place.swap(pieces[2][0], m=2), place.swap(pieces[1][1], m=1)
    own_x = place.swap(add_low(pieces[1][0], own_d), m=1)
    far_y = place.swap(add_low(pieces[2][1], far_d), m=2)
    return [add_low(pieces[0][0], own_x, own_y), add_low(pieces[0][1], far_x, far_y)]


def line_back(place, halves):
    sums = {}
    for kc in range(2):
        for kl in range(2):
            start = kl * (FULL + 2) if kc == 0 else 2 * (FULL + 2) + kl * SHORT
            size = FULL + 2 if kc == 0 else SHORT
            got = None
            for kh in range(2):
                piece = halves[kh][start : start + size]
                if (kc, kh, kl) != (0, 0, 0):
                    piece = place.swap(piece, c=kc, zh=kh, zl=kl)
                piece = piece.astype(jnp.float32)
                got = piece if got is None else got + piece
            sums[kc, kl] = got
    same = by_xor([sums[0, 0], sums[0, 1]], place.zl)
    other = by_xor([sums[1, 0], sums[1, 1]], place.zl)
    gap = jnp.zeros((FULL - SHORT,) + other[0].shape[1:], jnp.float32)
    dil = jnp.stack([s[:FULL] for s in same] + [jnp.concatenate([o, gap], axis=0) for o in other], axis=1)
    dil = dil.reshape((4 * FULL,) + dil.shape[2:])[: 2 * PER_CHIP]
    rows = lambda t: jnp.transpose(t, (1, 0, 2)).reshape(t.shape[1], t.shape[0] * LANES).T
    one = jnp.stack([s[FULL] for s in same])
    pool = jnp.stack([s[FULL + 1] for s in same])
    return rows(dil), rows(one), rows(pool)


def gathered_tiles(place, dilated, pointwise, pooling):
    whole = []
    for w in (dilated, pointwise, pooling):
        w = lax.all_gather(w, "rows", axis=1, tiled=True)
        w = lax.all_gather(w, "dp", axis=0, tiled=True)
        channels = pointwise.shape[0] * place.nd
        taps = w.shape[0] // channels
        w = w.reshape(taps, channels // (LANES * place.nr), place.nr, LANES, w.shape[1])
        w = lax.dynamic_index_in_dim(w, place.part, 2, keepdims=False)
        whole.append(jnp.transpose(w.reshape(taps, channels // place.nr, w.shape[-1]), (0, 2, 1)))
    return jnp.concatenate(whole, axis=0)


def scattered_tiles(place, gradients):
    outs = []
    taps, columns, width = gradients.shape
    for g in (gradients[: taps - 2], gradients[taps - 2 : taps - 1], gradients[taps - 1 :]):
        g = jnp.transpose(g, (0, 2, 1)).reshape(g.shape[0], width // LANES, 1, LANES, columns)
        spread = jnp.zeros((g.shape[0], width // LANES, place.nr, LANES, columns), g.dtype)
        g = lax.dynamic_update_slice_in_dim(spread, g, place.part, 2).reshape(-1, columns)
        g = lax.psum_scatter(g, "dp", scatter_dimension=0, tiled=True)
        outs.append(lax.psum_scatter(g, "rows", scatter_dimension=1, tiled=True).astype(jnp.float32))
    return outs


class Shape:
    def __init__(self, band_rows, columns, nr, width, out, pieces):
        self.band_rows, self.columns, self.nr, self.width, self.out = band_rows, columns, nr, width, out
        self.rows = band_rows * nr
        self.band, self.pixels = band_rows * columns, band_rows * columns * nr
        self.block = BLOCK_ROWS * columns
        self.blocks = self.rows // BLOCK_ROWS
        self.pieces = pieces
        self.n_weights = 8 if pieces else 1


ANY = pl.BlockSpec(memory_space=pl.ANY)
SMEM = pl.BlockSpec(memory_space=pltpu.SMEM)
VMEM = pl.BlockSpec(memory_space=pltpu.VMEM)
PARAMS = pltpu.CompilerParams(vmem_limit_bytes=58 * 2**20)


def start_bands(shape, refs, scratch, sem, part):
    for k, ref in enumerate(refs):
        pltpu.make_async_copy(ref, scratch.at[pl.ds((part ^ k) * shape.band, shape.band), :], sem.at[k]).start()


def wait_bands(shape, refs, scratch, sem):
    for k, ref in enumerate(refs):
        pltpu.make_async_copy(ref, scratch.at[pl.ds(k * shape.band, shape.band), :], sem.at[k]).wait()


def piece_of(t, kl, c):
    same = jnp.where(c == 0, t < FULL, t >= SHORT)
    return jnp.where(same, (FULL + 2) * kl + t - SHORT * c, 2 * (FULL + 2) + SHORT * kl + t - FULL * (1 - c))


def for_tiles(shape, info, first_tap, n_taps, visit):
    m, c, zh, zl = info[0], info[1], info[2], info[3]

    def column(kh, kl):
        return ((zh ^ kh) * 2 + (zl ^ kl)) * (shape.out // shape.nr)

    if first_tap < 27:

        def body(v, carry):
            chip = v // PER_CHIP
            t = v - chip * PER_CHIP
            for rel in range(4):

                @pl.when((chip ^ m) == rel)
                def _():
                    for kl in range(2):
                        slot = piece_of(t, kl, c)
                        for kh in range(2):
                            visit(rel, kh, slot, v // 4 - first_tap, (v % 4) * LANES, column(kh, kl))

            return carry

        lax.fori_loop(4 * first_tap, 4 * min(first_tap + n_taps, 27), body, 0)
    for tap in range(max(first_tap, 27), first_tap + n_taps):
        for rel in range(4):
            for kl in range(2):
                for kh in range(2):
                    lane = pl.multiple_of((rel ^ m) * LANES, LANES)
                    visit(rel, kh, (FULL + 2) * kl + FULL + tap - 27, tap - first_tap, lane, column(kh, kl))


def start_weights(shape, refs, scratch, sem, info, first_tap, n_taps):
    if not shape.pieces:
        pltpu.make_async_copy(refs[0].at[pl.ds(first_tap, n_taps)], scratch, sem).start()
        return
    part = shape.out // shape.nr

    def visit(rel, kh, slot, tap, lane, column):
        place = scratch.at[tap, pl.ds(pl.multiple_of(column, part), part), pl.ds(pl.multiple_of(lane, LANES), LANES)]
        pltpu.make_async_copy(refs[2 * rel + kh].at[slot], place, sem).start()

    for_tiles(shape, info, first_tap, n_taps, visit)


def wait_weights(scratch, sem):
    pltpu.make_async_copy(scratch, scratch, sem).wait()


def shifted(values, by, columns):
    if by == 0:
        return values
    pixels = values.shape[0]
    source = lax.broadcasted_iota(jnp.int32, (pixels, 1), 0) % columns - by
    return jnp.where((source >= 0) & (source < columns), pltpu.roll(values, by % pixels, 0), 0.0)


def put_halves(shape, c, blk, value, keep, sent):
    half = shape.blocks // 2
    at = pl.ds((blk % half) * shape.block, shape.block)

    @pl.when(c == blk // half)
    def _():
        keep[at, :] = value

    @pl.when(c != blk // half)
    def _():
        sent[at, :] = value.astype(sent.dtype)


def half_shapes(shape):
    half = shape.pixels // 2
    return [jax.ShapeDtypeStruct((half, shape.out), jnp.float32), jax.ShapeDtypeStruct((half, shape.out), jnp.bfloat16)]


def dilated_kernel(shape, branch, info, *refs):
    dilation = dilations[branch]
    bands, weights = refs[: shape.nr], refs[shape.nr : shape.nr + shape.n_weights]
    keep, sent, x, w, y, band_sem, w_sem = refs[shape.nr + shape.n_weights :]
    start_bands(shape, bands, x, band_sem, info[4])
    start_weights(shape, weights, w, w_sem, info, 9 * branch, 9)
    wait_bands(shape, bands, x, band_sem)
    wait_weights(w, w_sem)
    move = dilation * shape.columns
    for s in range(3):
        y[s] = dot(x[...], w[3 + s], NT)
        y[s, move:, :] += dot(x[: shape.pixels - move, :], w[s], NT)
        y[s, : shape.pixels - move, :] += dot(x[move:, :], w[6 + s], NT)
    for blk in range(shape.blocks):
        at = slice(blk * shape.block, (blk + 1) * shape.block)
        z = y[1, at, :] + shifted(y[0, at, :], dilation, shape.columns) + shifted(y[2, at, :], -dilation, shape.columns)
        put_halves(shape, info[1], blk, z, keep, sent)


def dilated_sums(shape, branch, info, bands, weights):
    macs = shape.pixels * shape.width * shape.out * 7
    return pl.pallas_call(
        lambda *refs: dilated_kernel(shape, branch, *refs),
        out_shape=half_shapes(shape),
        in_specs=[SMEM] + [ANY] * (shape.nr + shape.n_weights),
        out_specs=[VMEM] * 2,
        scratch_shapes=[
            pltpu.VMEM((shape.pixels, shape.width), jnp.bfloat16),
            pltpu.VMEM((9, shape.out, shape.width), jnp.bfloat16),
            pltpu.VMEM((3, shape.pixels, shape.out), jnp.float32),
            pltpu.SemaphoreType.DMA((shape.nr,)),
            pltpu.SemaphoreType.DMA,
        ],
        compiler_params=PARAMS,
        cost_estimate=pl.CostEstimate(flops=2 * macs, bytes_accessed=2**23, transcendentals=0),
        name=f"branch{branch}",
    )(info, *bands, *weights)


def one_kernel(shape, info, area, *refs):
    bands, weights = refs[: shape.nr], refs[shape.nr : shape.nr + shape.n_weights]
    keep, sent, pooled, lifted, x, w, band_sem, w_sem = refs[shape.nr + shape.n_weights :]
    start_bands(shape, bands, x, band_sem, info[4])
    start_weights(shape, weights, w, w_sem, info, 27, 2)
    wait_bands(shape, bands, x, band_sem)
    wait_weights(w, w_sem)
    sums = jnp.zeros((1, shape.width), jnp.float32)
    for blk in range(shape.blocks):
        at = slice(blk * shape.block, (blk + 1) * shape.block)
        values = x[at, :]
        sums = sums + jnp.sum(values.astype(jnp.float32), axis=0, keepdims=True)
        put_halves(shape, info[1], blk, dot(values, w[0], NT), keep, sent)
    low = jnp.broadcast_to(sums / area[0], pooled.shape).astype(jnp.bfloat16)
    first = lax.broadcasted_iota(jnp.int32, pooled.shape, 0) == 0
    pooled[...] = jnp.where(first, low.astype(jnp.float32), 0.0).astype(jnp.bfloat16)
    lifted[...] = dot(pooled[...], w[1], NT)


def one_sums(shape, info, area, bands, weights):
    return pl.pallas_call(
        lambda *refs: one_kernel(shape, *refs),
        out_shape=half_shapes(shape)
        + [jax.ShapeDtypeStruct((16, shape.width), jnp.bfloat16), jax.ShapeDtypeStruct((16, shape.out), jnp.float32)],
        in_specs=[SMEM, SMEM] + [ANY] * (shape.nr + shape.n_weights),
        out_specs=[VMEM] * 4,
        scratch_shapes=[
            pltpu.VMEM((shape.pixels, shape.width), jnp.bfloat16),
            pltpu.VMEM((2, shape.out, shape.width), jnp.bfloat16),
            pltpu.SemaphoreType.DMA((shape.nr,)),
            pltpu.SemaphoreType.DMA,
        ],
        compiler_params=PARAMS,
        cost_estimate=pl.CostEstimate(
            flops=2 * shape.pixels * shape.width * shape.out, bytes_accessed=2**22, transcendentals=0
        ),
        name="one_by_one",
    )(info, area, *bands, *weights)


def moved_deltas(shape, delta, moved, branch):
    for blk in range(shape.blocks):
        at = slice(blk * shape.block, (blk + 1) * shape.block)
        values = delta[at, (branch + 1) * shape.out : (branch + 2) * shape.out].astype(jnp.float32)
        for s in range(3):
            moved[s, at, :] = shifted(values, (s - 1) * dilations[branch], shape.columns).astype(jnp.bfloat16)


def weight_kernel(shape, info, *refs):
    nr = shape.nr
    bands, deltas, pool_delta, pooled = refs[:nr], refs[nr : 2 * nr], refs[2 * nr], refs[2 * nr + 1]
    outs = refs[2 * nr + 2 : 2 * nr + 2 + shape.n_weights]
    x, delta, moved, grads, band_sem, delta_sem = refs[2 * nr + 2 + shape.n_weights :]
    start_bands(shape, deltas, delta, delta_sem, info[4])
    start_bands(shape, bands, x, band_sem, info[4])
    wait_bands(shape, deltas, delta, delta_sem)
    wait_bands(shape, bands, x, band_sem)
    part = shape.out // nr

    def put(first_tap, n_taps):
        if not shape.pieces:
            outs[0][first_tap : first_tap + n_taps] = grads[:n_taps]
            return

        def visit(rel, kh, slot, tap, lane, column):
            rows, lanes = pl.ds(pl.multiple_of(column, part), part), pl.ds(pl.multiple_of(lane, LANES), LANES)
            outs[2 * rel + kh][slot] = grads[tap, rows, lanes]

        for_tiles(shape, info, first_tap, n_taps, visit)

    for branch in range(3):
        moved_deltas(shape, delta, moved, branch)
        move = dilations[branch] * shape.columns
        for s in range(3):
            grads[s] = dot(moved[s, move:, :], x[: shape.pixels - move, :], TN).astype(jnp.bfloat16)
            grads[3 + s] = dot(moved[s], x[...], TN).astype(jnp.bfloat16)
            grads[6 + s] = dot(moved[s, : shape.pixels - move, :], x[move:, :], TN).astype(jnp.bfloat16)
        put(9 * branch, 9)
    grads[0] = dot(delta[:, : shape.out], x[...], TN).astype(jnp.bfloat16)
    grads[1] = dot(pool_delta[...], pooled[...], TN).astype(jnp.bfloat16)
    put(27, 2)


def weight_gradients(shape, info, bands, deltas, pool_delta, pooled):
    if shape.pieces:
        slots = 2 * (FULL + 2) + 2 * SHORT
        out_shape = [jax.ShapeDtypeStruct((slots, shape.out // shape.nr, LANES), jnp.bfloat16)] * 8
    else:
        out_shape = [jax.ShapeDtypeStruct((29, shape.out, shape.width), jnp.bfloat16)]
    return pl.pallas_call(
        lambda *refs: weight_kernel(shape, *refs),
        out_shape=out_shape,
        in_specs=[SMEM] + [ANY] * (2 * shape.nr) + [VMEM] * 2,
        out_specs=[VMEM] * len(out_shape),
        scratch_shapes=[
            pltpu.VMEM((shape.pixels, shape.width), jnp.bfloat16),
            pltpu.VMEM((shape.pixels, 4 * shape.out), jnp.bfloat16),
            pltpu.VMEM((3, shape.pixels, shape.out), jnp.bfloat16),
            pltpu.VMEM((9, shape.out, shape.width), jnp.bfloat16),
            pltpu.SemaphoreType.DMA((shape.nr,)),
            pltpu.SemaphoreType.DMA((shape.nr,)),
        ],
        compiler_params=PARAMS,
        cost_estimate=pl.CostEstimate(
            flops=44 * shape.pixels * shape.width * shape.out, bytes_accessed=2**24, transcendentals=0
        ),
        name="weight_gradients",
    )(info, *bands, *deltas, pool_delta, pooled)


def input_kernel(shape, info, area, *refs):
    nr, n = shape.nr, shape.n_weights
    deltas, pool_delta, mask, weights = refs[:nr], refs[nr], refs[nr + 1], refs[nr + 2 : nr + 2 + n]
    outs = refs[nr + 2 + n : 2 * nr + 2 + n]
    delta, moved, w, acc, delta_sem, w_sem = refs[2 * nr + 2 + n :]
    start_bands(shape, deltas, delta, delta_sem, info[4])
    start_weights(shape, weights, w, w_sem, info, 0, 29)
    wait_bands(shape, deltas, delta, delta_sem)
    wait_weights(w, w_sem)
    pool = dot(pool_delta[...], w[28], NN)[0:1] / area[0]
    acc[...] = dot(delta[:, : shape.out], w[27], NN) + pool
    for branch in range(3):
        moved_deltas(shape, delta, moved, branch)
        move = dilations[branch] * shape.columns
        for s in range(3):
            acc[...] += dot(moved[s], w[9 * branch + 3 + s], NN)
            acc[: shape.pixels - move, :] += dot(moved[s, move:, :], w[9 * branch + s], NN)
            acc[move:, :] += dot(moved[s, : shape.pixels - move, :], w[9 * branch + 6 + s], NN)
    for k in range(nr):
        at = pl.ds(pl.multiple_of((info[4] ^ k) * shape.band, shape.band), shape.band)
        outs[k][...] = (acc[at, :] * mask[at, :]).astype(jnp.bfloat16)


def input_gradient(shape, info, area, deltas, pool_delta, mask, weights):
    return pl.pallas_call(
        lambda *refs: input_kernel(shape, *refs),
        out_shape=[jax.ShapeDtypeStruct((shape.band, shape.width), jnp.bfloat16)] * shape.nr,
        in_specs=[SMEM, SMEM] + [ANY] * shape.nr + [VMEM] * 2 + [ANY] * shape.n_weights,
        out_specs=[VMEM] * shape.nr,
        scratch_shapes=[
            pltpu.VMEM((shape.pixels, 4 * shape.out), jnp.bfloat16),
            pltpu.VMEM((3, shape.pixels, shape.out), jnp.bfloat16),
            pltpu.VMEM((29, shape.out, shape.width), jnp.bfloat16),
            pltpu.VMEM((shape.pixels, shape.width), jnp.float32),
            pltpu.SemaphoreType.DMA((shape.nr,)),
            pltpu.SemaphoreType.DMA,
        ],
        compiler_params=PARAMS,
        cost_estimate=pl.CostEstimate(
            flops=44 * shape.pixels * shape.width * shape.out, bytes_accessed=2**24, transcendentals=0
        ),
        name="input_gradient",
    )(info, area, *deltas, pool_delta, mask, *weights)


def valid_pixels(extent, first_row, rows, columns):
    r = first_row + lax.broadcasted_iota(jnp.int32, (rows, columns), 0)
    w = lax.broadcasted_iota(jnp.int32, (rows, columns), 1)
    return ((r < extent[0]) & (w < extent[1])).astype(jnp.float32).reshape(rows * columns, 1)


def to_logical(place, x):
    return place.send(x, lambda m, c, zh, zl: (m, zh, c, zl))


def on_device(
    features, extent, pointwise_weight, pooling_weight, dilated_weight, projection_weight, norm_gain, norm_bias, cotangent
):
    place = Place()
    nr, nzl = place.nr, place.nzl
    _, band_rows, columns, channels = features.shape
    width, out = channels // nr, norm_gain.shape[1]
    band = band_rows * columns
    pieces = nr == 4 and place.nd == 8 and dilated_weight.shape[0] == 2 * PER_CHIP * LANES
    shape = Shape(band_rows, columns, nr, width, out, pieces)
    images = place.nd

    if pieces:
        weights = [w for pair in plane_gather(place, line_pieces(place, dilated_weight, pointwise_weight, pooling_weight)) for w in pair]
    else:
        weights = [gathered_tiles(place, dilated_weight, pointwise_weight, pooling_weight)]
    projection = lax.all_gather(projection_weight, "rows", axis=1, tiled=True)
    projection = lax.all_gather(projection, "dp", axis=0, tiled=True)

    partner = place.swap(extent, c=1)
    extent_here = jnp.where(place.zh == place.c, extent, partner)[0]
    area = (extent_here[0] * extent_here[1]).astype(jnp.float32)
    mask = valid_pixels(extent_here, place.part * band_rows, band_rows, columns)
    whole_mask = valid_pixels(extent_here, 0, shape.rows, columns)
    own_mask = valid_pixels(extent[0], place.z * band_rows, band_rows, columns)
    info = jnp.stack([place.m, place.c, place.zh, place.zl, place.part]).astype(jnp.int32)
    areas = area.reshape(1)

    masked = (features.reshape(band, channels) * own_mask.astype(jnp.bfloat16)).reshape(band, channels // (LANES * nr), nr, LANES)
    parts = by_xor([masked[:, :, q].reshape(band, width) for q in range(nr)], place.z)
    bands = []
    for k in range(nr):
        k0, k1 = divmod(k, nzl)
        bands.append(place.send(parts[k], lambda m, c, zh, zl: (m, zh ^ k0, c, zl ^ k1)))
    upstream_low = to_logical(place, cotangent.reshape(band, out))

    def reduce(keep, sent):
        half = keep + place.swap(sent, c=1).astype(jnp.float32)
        rows = half.reshape(nzl, band, out)
        mine = lax.dynamic_index_in_dim(rows, place.zl, 0, keepdims=False)
        for k in range(1, nzl):
            other = lax.dynamic_index_in_dim(rows, place.zl ^ k, 0, keepdims=False).astype(jnp.bfloat16)
            mine = mine + place.swap(other, zl=k).astype(jnp.float32)
        return mine

    keep, sent, pooled, lifted = one_sums(shape, info, areas, bands, weights)
    z = [reduce(keep, sent)]
    for branch in range(3):
        z.append(reduce(*dilated_sums(shape, branch, info, bands, weights)))

    local_count = jnp.sum(mask)
    stats = [local_moments(v, mask, local_count) for v in z]
    table = (lax.broadcasted_iota(jnp.int32, (images, 1), 0) == place.image).astype(jnp.float32) * lifted[0:1]
    average, spread, count, pool_pre = moments(
        place,
        jnp.concatenate([s for s, _ in stats], axis=0),
        jnp.concatenate([q for _, q in stats], axis=0),
        local_count,
        table,
    )
    inv_std = lax.rsqrt(spread + epsilon)
    normed = [(z[k] - average[k : k + 1]) * inv_std[k : k + 1] for k in range(4)]
    pre_act = [norm_gain[k : k + 1] * normed[k] + norm_bias[k : k + 1] for k in range(4)]

    pool_average = jnp.mean(pool_pre, axis=0, keepdims=True)
    pool_centred = pool_pre - pool_average
    pool_inv = lax.rsqrt(jnp.mean(pool_centred * pool_centred, axis=0, keepdims=True) + epsilon)
    pool_normed = pool_centred * pool_inv
    pool_lift = norm_gain[4:5] * pool_normed + norm_bias[4:5]
    here = lambda rows: lax.dynamic_slice_in_dim(rows, place.image, 1, axis=0)
    pool_act = here(jax.nn.silu(pool_lift))

    concat = jnp.concatenate([jax.nn.silu(u) * mask for u in pre_act] + [pool_act * mask], axis=1).astype(jnp.bfloat16)
    proj_pre = dot(concat, projection, NN)
    proj_sums, proj_squares = local_moments(proj_pre, mask, local_count)
    proj_average, proj_spread, _, _ = moments(place, proj_sums, proj_squares, local_count)
    proj_inv = lax.rsqrt(proj_spread + epsilon)
    proj_normed = (proj_pre - proj_average) * proj_inv
    proj_lift = norm_gain[5:6] * proj_normed + norm_bias[5:6]
    output = to_logical(place, (jax.nn.silu(proj_lift) * mask).astype(jnp.bfloat16))

    upstream = upstream_low.astype(jnp.float32) * mask * silu_slope(proj_lift)
    sums = jnp.concatenate(
        [jnp.sum(upstream * proj_normed, axis=0, keepdims=True), jnp.sum(upstream, axis=0, keepdims=True)], axis=0
    )
    proj_totals = total(place, sums)
    proj_gain_grad, proj_bias_grad = proj_totals[0:1], proj_totals[1:2]
    gain = norm_gain[5:6]
    proj_delta = (
        mask
        * proj_inv
        * (gain * upstream - gain * proj_bias_grad / count - proj_normed * gain * proj_gain_grad / count)
    ).astype(jnp.bfloat16)
    concat_grad = dot(proj_delta, projection, NT)
    projection_partial = dot(concat, proj_delta, TN).astype(jnp.bfloat16)
    branch_up = [
        concat_grad[:, k * out : (k + 1) * out] * mask * silu_slope(pre_act[k]) for k in range(4)
    ]
    pool_part = jnp.sum(concat_grad[:, 4 * out :] * mask, axis=0, keepdims=True)
    table = (lax.broadcasted_iota(jnp.int32, (images, 1), 0) == place.image).astype(jnp.float32) * pool_part
    totals = total(
        place,
        jnp.concatenate(
            [jnp.sum(branch_up[k] * normed[k], axis=0, keepdims=True) for k in range(4)]
            + [jnp.sum(branch_up[k], axis=0, keepdims=True) for k in range(4)]
            + [table],
            axis=0,
        ),
    )
    branch_gain_grad, branch_bias_grad = totals[:4], totals[4:8]
    pool_up = totals[8:] * silu_slope(pool_lift)
    pool_gain_grad = jnp.sum(pool_up * pool_normed, axis=0, keepdims=True)
    pool_bias_grad = jnp.sum(pool_up, axis=0, keepdims=True)
    pool_delta = here(
        pool_inv
        * (
            norm_gain[4:5] * pool_up
            - norm_gain[4:5] * pool_bias_grad / images
            - pool_normed * norm_gain[4:5] * pool_gain_grad / images
        )
    )
    pool_delta = jnp.pad(pool_delta, ((0, 15), (0, 0))).astype(jnp.bfloat16)
    deltas = []
    for k in range(4):
        gain = norm_gain[k : k + 1]
        deltas.append(
            mask
            * inv_std[k : k + 1]
            * (
                gain * branch_up[k]
                - gain * branch_bias_grad[k : k + 1] / count
                - normed[k] * gain * branch_gain_grad[k : k + 1] / count
            )
        )
    delta = jnp.concatenate(deltas, axis=1).astype(jnp.bfloat16)
    near = [delta] + [place.swap(delta, zl=k) for k in range(1, nzl)]
    spread_deltas = near + [place.swap(v, c=1) for v in near]

    grads = weight_gradients(shape, info, bands, spread_deltas, pool_delta, pooled)
    inputs = input_gradient(shape, info, areas, spread_deltas, pool_delta, whole_mask, weights)

    returned = []
    for k in range(nr):
        k0, k1 = divmod(k, nzl)
        returned.append(place.send(inputs[k], lambda m, c, zh, zl: (m, zh, c ^ k0, zl ^ k1)))
    returned = by_xor(returned, place.z)
    feature_gradient = jnp.stack([r.reshape(band, channels // (LANES * nr), LANES) for r in returned], axis=2)

    if pieces:
        pairs = [[grads[2 * rel], grads[2 * rel + 1]] for rel in range(4)]
        dilated_gradient, pointwise_gradient, pooling_gradient = line_back(place, plane_scatter(place, pairs))
    else:
        dilated_gradient, pointwise_gradient, pooling_gradient = scattered_tiles(place, grads[0])
    projection_gradient = lax.psum_scatter(projection_partial, "dp", scatter_dimension=0, tiled=True)
    projection_gradient = lax.psum_scatter(projection_gradient, "rows", scatter_dimension=1, tiled=True)

    return (
        output.reshape(cotangent.shape),
        feature_gradient.reshape(features.shape),
        pointwise_gradient,
        pooling_gradient,
        dilated_gradient,
        projection_gradient.astype(jnp.float32),
        jnp.concatenate([branch_gain_grad, pool_gain_grad, proj_gain_grad], axis=0),
        jnp.concatenate([branch_bias_grad, pool_bias_grad, proj_bias_grad], axis=0),
    )


def solution(mesh):
    banded = P("dp", "rows", None, None)
    blocks = P("dp", "rows")
    return jax.shard_map(
        on_device,
        mesh=mesh,
        in_specs=(banded, P("dp", None), blocks, blocks, blocks, blocks, P(), P(), banded),
        out_specs=(banded, banded, blocks, blocks, blocks, blocks, P(), P()),
        check_vma=False,
    )
```

time: 1070 us -> 494 us (0.46)
  the two profiles are of different devices: /device:TPU:0 before, /device:TPU:9 now
where the time goes in v1:
time: 494 us; the launch traced here: 486 us
  waiting for transfers between devices  184 us (37%)
  starting transfers between devices  102 us (21%)
  Pallas kernels  78.3 us (16%)
  other arithmetic  41.3 us (8%)
  local copies, waits for them, and re-layouts  31.1 us (6%)
  blocking collectives  26.7 us (5%)
  between operations  18.1 us (4%)
    ppermute x76, waiting for transfers between devices, send(): return lax.ppermute(x, AXES, pairs)  180 us
    ppermute x76, starting transfers between devices, send(): return lax.ppermute(x, AXES, pairs)  102 us
    pallas_call x3, Pallas kernels, dilated_sums(): pl.pallas_call(lambda *refs: dilated_kernel(shape, branch, *refs), out_sh...  27.1 us
    pallas_call x1, Pallas kernels, weight_gradients(): pl.pallas_call(lambda *refs: weight_kernel(shape, *refs), out_shape=out_s...  25.2 us
    pallas_call x1, Pallas kernels, input_gradient(): pl.pallas_call(lambda *refs: input_kernel(shape, *refs), out_shape=[jax.S...  20.4 us
    all_gather x1, blocking collectives, on_device(): projection = lax.all_gather(projection, 'dp', axis=0, tiled=True)  15 us
    unnamed x157, local copies, waits for them, and re-layouts  12.6 us
    all_gather x1, blocking collectives, on_device(): projection = lax.all_gather(projection_weight, 'rows', axis=1, tiled=True)  11.7 us
  transfers between devices with their start and end apart: 78, of which 37 were waited for; matrix products, arithmetic and copies ran while one was open for 10% of the time, Pallas kernels for 14%

profile of v1, /device:TPU:9, one launch (start us, length us, event | category | flops | bytes accessed | tf_op | source)
XLA Modules:
  0.0 485.7 jit_solution(8814263912738982968)
XLA Ops:
  9.4 2.9 collective-permute-start.10
  13.3 2.6 collective-permute-start.8
  19.4 28.7 %collective-permute-done.8 = bf16[16,64,128]{2,1,0:T(8,128)(2,1)} collective-permute-done((bf16[16,64,128]{2,1,0:T(8,128)(2,1)}, bf16[16,64,128]{2,1,0:T(8,128)(2,1)}, u32[]{:S(2)}, u32[]{:S(2)}) %collective-permute-start.8) | collective-permute-done | bytes 262176 | tf_op jit(solution)/shard_map/ppermute | solution.py:46
  49.7 1.7 constant_dynamic-update-slice_fusion.3
  51.4 2.4 collective-permute-done.9
  53.7 1.7 constant_dynamic-update-slice_fusion.2
  55.4 1.6 constant_dynamic-update-slice_fusion.1
  57.0 1.6 constant_dynamic-update-slice_fusion.refs_7_.refs_6_.refs_9_
  61.4 2.1 pad_maximum_fusion.2.refs_6_.refs_5_.refs_8_
  64.8 2.9 copy_multiply_fusion
  68.7 5.6 %collective-permute-start.1 = (bf16[432,512]{1,0:T(8,128)(2,1)S(1)}, bf16[432,512]{1,0:T(8,128)(2,1)}, u32[]{:S(2)}, u32[]{:S(2)}) collective-permute-start(bf16[432,512]{1,0:T(8,128)(2,1)S(1)} %bitcast.219), channel_id=1, source_target_pairs={{0,0},{1,1},{2,4},{3,5},{4,2},{5,3},{6,6},{7,7},{8,8},{9,9},{10,12... | collective-permute-start | bytes 1327112 | tf_op jit(solution)/shard_map/ppermute | solution.py:46
  76.4 12.6 %collective-permute-done.1.refs_2_.refs_1_ = bf16[432,512]{1,0:T(8,128)(2,1)} collective-permute-done((bf16[432,512]{1,0:T(8,128)(2,1)S(1)}, bf16[432,512]{1,0:T(8,128)(2,1)}, u32[]{:S(2)}, u32[]{:S(2)}) %collective-permute-start.1) | collective-permute-done | bytes 442400 | tf_op jit(solution)/shard_map/ppermute | solution.py:46
  96.8 8.6 %collective-permute-done.2.refs_3_.refs_2_ = bf16[432,512]{1,0:T(8,128)(2,1)S(1)} collective-permute-done((bf16[432,512]{1,0:T(8,128)(2,1)S(1)}, bf16[432,512]{1,0:T(8,128)(2,1)S(1)}, u32[]{:S(2)}, u32[]{:S(2)}) %collective-permute-start.2) | collective-permute-done | bytes 442400 | tf_op jit(solution)/shard_map/ppermute | solution.py:46
  105.4 1.9 collective-permute-start.4
  109.5 10.0 %collective-permute-done.4.refs_5_.refs_4_ = bf16[432,512]{1,0:T(8,128)(2,1)S(1)} collective-permute-done((bf16[432,512]{1,0:T(8,128)(2,1)}, bf16[432,512]{1,0:T(8,128)(2,1)S(1)}, u32[]{:S(2)}, u32[]{:S(2)}) %collective-permute-start.4) | collective-permute-done | bytes 442400 | tf_op jit(solution)/shard_map/ppermute | solution.py:46
  119.5 6.4 %collective-permute-done.17.refs_13_.refs_12_.refs_15_ = bf16[58,64,128]{2,1,0:T(8,128)(2,1)} collective-permute-done((bf16[58,64,128]{2,1,0:T(8,128)(2,1)}, bf16[58,64,128]{2,1,0:T(8,128)(2,1)}, u32[]{:S(2)}, u32[]{:S(2)}) %collective-permute-start.17) | collective-permute-done | bytes 950304 | tf_op jit(solution)/shard_map/ppermute | solution.py:46
  126.0 8.7 %branch2.1 = (f32[864,256]{1,0:T(8,128)}, bf16[864,256]{1,0:T(8,128)(2,1)}) custom-call(s32[5]{0:T(128)} %stack.47.refs_0_, bf16[432,512]{1,0:T(8,128)(2,1)} %collective-permute-done.1.refs_2_.refs_1_, bf16[432,512]{1,0:T(8,128)(2,1)} %copy-done.15, bf16[432,512]{1,0:T(8,128)(2,1)} %collective-permute-done.3.refs_4_.refs_3_, bf16[432,512]{1,0:T(8,128)(2,1)} %copy-done.16, ...), custom_call_target="tpu_custom_call" | custom-call | flops 3170893824 | bytes 8388608 | tf_op jit(solution)/shard_map/branch2/pallas_call | solution.py:330
  134.7 2.2 collective-permute-start.24
  136.9 9.0 %branch1.1 = (f32[864,256]{1,0:T(8,128)}, bf16[864,256]{1,0:T(8,128)(2,1)}) custom-call(s32[5]{0:T(128)} %stack.47.refs_0_, bf16[432,512]{1,0:T(8,128)(2,1)} %collective-permute-done.1.refs_2_.refs_1_, bf16[432,512]{1,0:T(8,128)(2,1)} %copy-done.15, bf16[432,512]{1,0:T(8,128)(2,1)} %collective-permute-done.3.refs_4_.refs_3_, bf16[432,512]{1,0:T(8,128)(2,1)} %copy-done.16, ...), custom_call_target="tpu_custom_call" | custom-call | flops 3170893824 | bytes 8388608 | tf_op jit(solution)/shard_map/branch1/pallas_call | solution.py:330
  145.9 9.4 %branch0.1 = (f32[864,256]{1,0:T(8,128)}, bf16[864,256]{1,0:T(8,128)(2,1)}) custom-call(s32[5]{0:T(128)} %stack.47.refs_0_, bf16[432,512]{1,0:T(8,128)(2,1)} %collective-permute-done.1.refs_2_.refs_1_, bf16[432,512]{1,0:T(8,128)(2,1)} %copy-done.15, bf16[432,512]{1,0:T(8,128)(2,1)} %collective-permute-done.3.refs_4_.refs_3_, bf16[432,512]{1,0:T(8,128)(2,1)} %copy-done.16, ...), custom_call_target="tpu_custom_call" | custom-call | flops 3170893824 | bytes 8388608 | tf_op jit(solution)/shard_map/branch0/pallas_call | solution.py:330
  155.9 5.6 %one_by_one.1 = (f32[864,256]{1,0:T(8,128)}, bf16[864,256]{1,0:T(8,128)(2,1)}, bf16[16,512]{1,0:T(8,128)(2,1)}, f32[16,256]{1,0:T(8,128)}) custom-call(s32[5]{0:T(128)} %stack.47.refs_0_, f32[1]{0:T(128)} %bitcast.9.refs_1_, bf16[432,512]{1,0:T(8,128)(2,1)} %collective-permute-done.1.refs_2_.refs_1_, bf16[432,512]{1,0:T(8,128)(2,1)} %copy-done.15, ...), custom_call_target="tpu_custom_call" | custom-call | flops 452984832 | bytes 4194304 | tf_op jit(solution)/shard_map/one_by_one/pallas_call | solution.py:368
  166.2 2.9 collective-permute-done.25
  169.2 9.5 %collective-permute-done.19 = bf16[432,256]{1,0:T(8,128)(2,1)S(1)} collective-permute-done((bf16[432,256]{1,0:T(8,128)(2,1)S(1)}, bf16[432,256]{1,0:T(8,128)(2,1)S(1)}, u32[]{:S(2)}, u32[]{:S(2)}) %collective-permute-start.19) | collective-permute-done | bytes 221216 | tf_op jit(solution)/shard_map/ppermute | solution.py:46
  178.8 4.5 collective-permute-done.21
  190.4 11.7 %all_gather.6 = bf16[160,256]{0,1:T(8,128)(2,1)S(1)} all-gather(bf16[160,64]{0,1:T(8,128)(2,1)S(1)} %copy-done.23), channel_id=1, replica_groups=mesh['dp'=8,'rows'=4] {'rows'}, dimensions={1}, use_global_device_ids=true | all-gather | bytes 102400 | tf_op jit(solution)/shard_map/all_gather | solution.py:529
  202.4 2.2 collective-permute-start.31
  206.0 15.0 %all_gather.7 = bf16[1280,256]{1,0:T(8,128)(2,1)S(1)} all-gather(bf16[160,256]{1,0:T(8,128)(2,1)S(1)} %copy.59), channel_id=1, replica_groups=mesh['dp'=8,'rows'=4] {'dp'}, dimensions={0}, use_global_device_ids=true | all-gather | bytes 737280 | tf_op jit(solution)/shard_map/all_gather | solution.py:530
  228.2 1.9 collective-permute-done.36
  231.7 2.3 collective-permute-start.37
  234.0 4.8 collective-permute-start.41
  238.9 5.1 %collective-permute-done.41 = bf16[432,256]{1,0:T(8,128)(2,1)S(1)} collective-permute-done((bf16[432,256]{1,0:T(8,128)(2,1)S(1)}, bf16[432,256]{1,0:T(8,128)(2,1)S(1)}, u32[]{:S(2)}, u32[]{:S(2)}) %collective-permute-start.41) | collective-permute-done | bytes 221216 | tf_op jit(solution)/shard_map/ppermute | solution.py:46
  250.7 3.2 collective-permute-start.47
  261.8 2.6 concatenate.73
  264.5 3.6 collective-permute-start.49
  275.0 2.3 collective-permute-start.55
  278.8 2.0 collective-permute-done.54
  281.5 1.9 multiply_reduce_fusion.15
  287.2 3.6 collective-permute-start.57
  290.8 14.1 %collective-permute-done.56.refs_3_.refs_6_ = bf16[432,1024]{1,0:T(8,128)(2,1)S(1)} collective-permute-done((bf16[432,1024]{1,0:T(8,128)(2,1)S(1)}, bf16[432,1024]{1,0:T(8,128)(2,1)S(1)}, u32[]{:S(2)}, u32[]{:S(2)}) %collective-permute-start.56) | collective-permute-done | bytes 884768 | tf_op jit(solution)/shard_map/ppermute | solution.py:46
  304.9 4.4 collective-permute-start.58
  311.4 2.7 collective-permute-start.40
  314.1 2.6 convolution_convert_fusion
  318.4 25.2 %weight_gradients.1 = (bf16[58,64,128]{2,1,0:T(8,128)(2,1)}, bf16[58,64,128]{2,1,0:T(8,128)(2,1)}, bf16[58,64,128]{2,1,0:T(8,128)(2,1)}, bf16[58,64,128]{2,1,0:T...) custom-call(s32[5]{0:T(128)} %stack.47.refs_0_, ...), custom_call_target="tpu_custom_call" | custom-call | flops 9965666304 | bytes 16777216 | tf_op jit(solution)/shard_map/weight_gradients/pallas_call | solution.py:437
  345.2 20.4 %input_gradient.1 = (bf16[432,512]{1,0:T(8,128)(2,1)}, bf16[432,512]{1,0:T(8,128)(2,1)}, bf16[432,512]{1,0:T(8,128)(2,1)}, bf16[432,512]{1,0:T(8,128)(2,1)}) custom-call(s32[5]{0:T(128)} %stack.47.refs_0_, f32[1]{0:T(128)} %bitcast.9.refs_1_, bf16[432,1024]{1,0:T(8,128)(2,1)} %copy-done.8, bf16[432,1024]{1,0:T(8,128)(2,1)} %copy-done.71, ...), custom_call_target="tpu_custom_call" | custom-call | flops 9965666304 | bytes 16777216 | tf_op jit(solution)/shard_map/input_gradient/pallas_call | solution.py:482
  366.4 1.7 copy.67
  368.0 1.7 collective-permute-start.60
  369.9 6.4 %collective-permute-start.62 = (bf16[432,512]{1,0:T(8,128)(2,1)}, bf16[432,512]{1,0:T(8,128)(2,1)}, u32[]{:S(2)}, u32[]{:S(2)}) collective-permute-start(bf16[432,512]{1,0:T(8,128)(2,1)} %get-tuple-element.42), channel_id=1, source_target_pairs={{0,0},{1,1},{2,4},{3,5},{4,2},{5,3},{6,6},{7,7},{8,8},{9,9},{10,12... | collective-permute-start | bytes 1327112 | tf_op jit(solution)/shard_map/ppermute | solution.py:46
  376.4 2.6 add_convert_fusion.3
  378.9 12.1 %collective-permute-done.59 = bf16[432,512]{1,0:T(8,128)(2,1)S(1)} collective-permute-done((bf16[432,512]{1,0:T(8,128)(2,1)}, bf16[432,512]{1,0:T(8,128)(2,1)S(1)}, u32[]{:S(2)}, u32[]{:S(2)}) %collective-permute-start.59) | collective-permute-done | bytes 442400 | tf_op jit(solution)/shard_map/ppermute | solution.py:46
  393.4 4.1 reduce-scatter.7.cloned.1.call-done
  399.7 2.3 collective-permute-done.61
  402.5 5.9 %collective-permute-done.62 = bf16[432,512]{1,0:T(8,128)(2,1)} collective-permute-done((bf16[432,512]{1,0:T(8,128)(2,1)}, bf16[432,512]{1,0:T(8,128)(2,1)}, u32[]{:S(2)}, u32[]{:S(2)}) %collective-permute-start.62) | collective-permute-done | bytes 442400 | tf_op jit(solution)/shard_map/ppermute | solution.py:46
  410.3 1.9 pad_maximum_fusion.1
  412.2 2.3 copy.61
  414.5 2.5 reshape.225
  417.0 2.4 add_convert_fusion.2
  420.7 3.8 collective-permute-start.74
  424.6 1.7 collective-permute-start.72
  426.3 2.6 collective-permute-done.67
  428.8 2.0 add_convert_fusion
  431.5 5.5 %collective-permute-start.73 = (bf16[13,64,128]{2,1,0:T(8,128)(2,1)S(1)}, bf16[13,64,128]{2,1,0:T(8,128)(2,1)S(1)}, u32[]{:S(2)}, u32[]{:S(2)}) collective-permute-start(bf16[13,64,128]{2,1,0:T(8,128)(2,1)S(1)} %get-tuple-element.146), channel_id=1, source_target_pairs={{0,7},{1,6},{2,5},{3,4},{4,3},{5,2},{6,1},{7,0},{8,15},{9,14},{10,... | collective-permute-start | bytes 638984 | tf_op jit(solution)/shard_map/ppermute | solution.py:46
  437.0 3.3 collective-permute-start.71
  440.3 23.0 %collective-permute-done.73 = bf16[13,64,128]{2,1,0:T(8,128)(2,1)S(1)} collective-permute-done((bf16[13,64,128]{2,1,0:T(8,128)(2,1)S(1)}, bf16[13,64,128]{2,1,0:T(8,128)(2,1)S(1)}, u32[]{:S(2)}, u32[]{:S(2)}) %collective-permute-start.73) | collective-permute-done | bytes 213024 | tf_op jit(solution)/shard_map/ppermute | solution.py:46
  464.8 9.7 %collective-permute-done.70 = bf16[16,64,128]{2,1,0:T(8,128)(2,1)S(1)} collective-permute-done((bf16[16,64,128]{2,1,0:T(8,128)(2,1)S(1)}, bf16[16,64,128]{2,1,0:T(8,128)(2,1)S(1)}, u32[]{:S(2)}, u32[]{:S(2)}) %collective-permute-start.70) | collective-permute-done | bytes 262176 | tf_op jit(solution)/shard_map/ppermute | solution.py:46
  (410 shorter events, 93.5 us)
Async XLA Ops:
  7.2 359.2 %reduce-scatter.5.cloned.1.call-start = ((), (), s32[]{:S(2)}) async-start(), calls=%async_computation.2 | async-start | bytes 737280 | tf_op jit(solution)/shard_map/reduce_scatter | solution.py:666
  9.4 46.0 %collective-permute-start.10 = (bf16[13,64,128]{2,1,0:T(8,128)(2,1)}, bf16[13,64,128]{2,1,0:T(8,128)(2,1)}, u32[]{:S(2)}, u32[]{:S(2)}) collective-permute-start(bf16[13,64,128]{2,1,0:T(8,128)(2,1)} %get-tuple-element.151), channel_id=1, source_target_pairs={{0,6},{1,7},{2,4},{3,5},{4,2},{5,3},{6,0},{7,1},{8,14},{9,15},{10,... | collective-permute-start | bytes 638984 | tf_op jit(solution)/shard_map/ppermute | solution.py:46
  12.3 47.6 %collective-permute-start.6 = (bf16[13,64,128]{2,1,0:T(8,128)(2,1)}, bf16[13,64,128]{2,1,0:T(8,128)(2,1)}, u32[]{:S(2)}, u32[]{:S(2)}) collective-permute-start(bf16[13,64,128]{2,1,0:T(8,128)(2,1)} %get-tuple-element.151), channel_id=1, source_target_pairs={{0,4},{1,5},{2,6},{3,7},{4,0},{5,1},{6,2},{7,3},{8,12},{9,13},{10,... | collective-permute-start | bytes 638984 | tf_op jit(solution)/shard_map/ppermute | solution.py:46
  12.3 44.7 %collective-permute-start.11 = (bf16[13,64,128]{2,1,0:T(8,128)(2,1)}, bf16[13,64,128]{2,1,0:T(8,128)(2,1)}, u32[]{:S(2)}, u32[]{:S(2)}) collective-permute-start(bf16[13,64,128]{2,1,0:T(8,128)(2,1)} %get-tuple-element.152), channel_id=1, source_target_pairs={{0,7},{1,6},{2,5},{3,4},{4,3},{5,2},{6,1},{7,0},{8,15},{9,14},{10,... | collective-permute-start | bytes 638984 | tf_op jit(solution)/shard_map/ppermute | solution.py:46
  13.3 34.9 %collective-permute-start.8 = (bf16[16,64,128]{2,1,0:T(8,128)(2,1)}, bf16[16,64,128]{2,1,0:T(8,128)(2,1)}, u32[]{:S(2)}, u32[]{:S(2)}) collective-permute-start(bf16[16,64,128]{2,1,0:T(8,128)(2,1)} %get-tuple-element.159), channel_id=1, source_target_pairs={{0,2},{1,3},{2,0},{3,1},{4,6},{5,7},{6,4},{7,5},{8,10},{9,11},{10,... | collective-permute-start | bytes 786440 | tf_op jit(solution)/shard_map/ppermute | solution.py:46
  15.9 37.8 %collective-permute-start.9 = (bf16[16,64,128]{2,1,0:T(8,128)(2,1)}, bf16[16,64,128]{2,1,0:T(8,128)(2,1)}, u32[]{:S(2)}, u32[]{:S(2)}) collective-permute-start(bf16[16,64,128]{2,1,0:T(8,128)(2,1)} %get-tuple-element.160), channel_id=1, source_target_pairs={{0,3},{1,2},{2,1},{3,0},{4,7},{5,6},{6,5},{7,4},{8,11},{9,10},{10,... | collective-permute-start | bytes 786440 | tf_op jit(solution)/shard_map/ppermute | solution.py:46
  48.1 11.8 %collective-permute-start.7 = (bf16[13,64,128]{2,1,0:T(8,128)(2,1)}, bf16[13,64,128]{2,1,0:T(8,128)(2,1)S(1)}, u32[]{:S(2)}, u32[]{:S(2)}) collective-permute-start(bf16[13,64,128]{2,1,0:T(8,128)(2,1)} %get-tuple-element.152), channel_id=1, source_target_pairs={{0,5},{1,4},{2,7},{3,6},{4,1},{5,0},{6,3},{7,2},{8,13},{9,12},{10,... | collective-permute-start | bytes 638984 | tf_op jit(solution)/shard_map/ppermute | solution.py:46
  53.7 7.7 %collective-permute-start.5 = (bf16[16,64,128]{2,1,0:T(8,128)(2,1)}, bf16[16,64,128]{2,1,0:T(8,128)(2,1)S(1)}, u32[]{:S(2)}, u32[]{:S(2)}) collective-permute-start(bf16[16,64,128]{2,1,0:T(8,128)(2,1)} %get-tuple-element.160), channel_id=1, source_target_pairs={{0,1},{1,0},{2,3},{3,2},{4,5},{5,4},{6,7},{7,6},{8,9},{9,8},{10,11... | collective-permute-start | bytes 786440 | tf_op jit(solution)/shard_map/ppermute | solution.py:46
  58.7 31.6 %collective-permute-start.15 = (bf16[58,64,128]{2,1,0:T(8,128)(2,1)}, bf16[58,64,128]{2,1,0:T(8,128)(2,1)}, u32[]{:S(2)}, u32[]{:S(2)}) collective-permute-start(bf16[58,64,128]{2,1,0:T(8,128)(2,1)} %constant_dynamic-update-slice_fusion.refs_7_.refs_6_.refs_9_), channel_id=1, source_target_pairs={{0,16},{1,17},{2,18},{3,19},{4,20},{5,21},{6,22},{7,23},{8,24},{9,... | collective-permute-start | bytes 2850824 | tf_op jit(solution)/shard_map/ppermute | solution.py:46
  63.6 26.9 %collective-permute-start.12 = (bf16[58,64,128]{2,1,0:T(8,128)(2,1)}, bf16[58,64,128]{2,1,0:T(8,128)(2,1)}, u32[]{:S(2)}, u32[]{:S(2)}) collective-permute-start(bf16[58,64,128]{2,1,0:T(8,128)(2,1)} %pad_maximum_fusion.2.refs_6_.refs_5_.refs_8_), channel_id=1, source_target_pairs={{0,8},{1,9},{2,10},{3,11},{4,12},{5,13},{6,14},{7,15},{8,0},{9,1},... | collective-permute-start | bytes 2850824 | tf_op jit(solution)/shard_map/ppermute | solution.py:46
  68.7 20.3 %collective-permute-start.1 = (bf16[432,512]{1,0:T(8,128)(2,1)S(1)}, bf16[432,512]{1,0:T(8,128)(2,1)}, u32[]{:S(2)}, u32[]{:S(2)}) collective-permute-start(bf16[432,512]{1,0:T(8,128)(2,1)S(1)} %bitcast.219), channel_id=1, source_target_pairs={{0,0},{1,1},{2,4},{3,5},{4,2},{5,3},{6,6},{7,7},{8,8},{9,9},{10,12... | collective-permute-start | bytes 1327112 | tf_op jit(solution)/shard_map/ppermute | solution.py:46
  74.4 19.4 %collective-permute-start.3 = (bf16[432,512]{1,0:T(8,128)(2,1)S(1)}, bf16[432,512]{1,0:T(8,128)(2,1)}, u32[]{:S(2)}, u32[]{:S(2)}) collective-permute-start(bf16[432,512]{1,0:T(8,128)(2,1)S(1)} %bitcast.218), channel_id=1, source_target_pairs={{0,4},{1,5},{2,0},{3,1},{4,6},{5,7},{6,2},{7,3},{8,12},{9,13},{10,... | collective-permute-start | bytes 1327112 | tf_op jit(solution)/shard_map/ppermute | solution.py:46
  76.2 43.3 %collective-permute-start.13 = (bf16[58,64,128]{2,1,0:T(8,128)(2,1)}, bf16[58,64,128]{2,1,0:T(8,128)(2,1)S(1)}, u32[]{:S(2)}, u32[]{:S(2)}) collective-permute-start(bf16[58,64,128]{2,1,0:T(8,128)(2,1)} %constant_dynamic-update-slice_fusion.refs_7_.refs_6_.refs_9_), channel_id=1, source_target_pairs={{0,8},{1,9},{2,10},{3,11},{4,12},{5,13},{6,14},{7,15},{8,0},{9,1},... | collective-permute-start | bytes 2850824 | tf_op jit(solution)/shard_map/ppermute | solution.py:46
  89.0 30.5 %collective-permute-start.14 = (bf16[58,64,128]{2,1,0:T(8,128)(2,1)}, bf16[58,64,128]{2,1,0:T(8,128)(2,1)S(1)}, u32[]{:S(2)}, u32[]{:S(2)}) collective-permute-start(bf16[58,64,128]{2,1,0:T(8,128)(2,1)} %pad_maximum_fusion.2.refs_6_.refs_5_.refs_8_), channel_id=1, source_target_pairs={{0,16},{1,17},{2,18},{3,19},{4,20},{5,21},{6,22},{7,23},{8,24},{9,... | collective-permute-start | bytes 2850824 | tf_op jit(solution)/shard_map/ppermute | solution.py:46
  90.3 35.7 %collective-permute-start.17 = (bf16[58,64,128]{2,1,0:T(8,128)(2,1)}, bf16[58,64,128]{2,1,0:T(8,128)(2,1)}, u32[]{:S(2)}, u32[]{:S(2)}) collective-permute-start(bf16[58,64,128]{2,1,0:T(8,128)(2,1)} %collective-permute-done.15.refs_11_.refs_10_.refs_13_), channel_id=1, source_target_pairs={{0,8},{1,9},{2,10},{3,11},{4,12},{5,13},{6,14},{7,15},{8,0},{9,1},... | collective-permute-start | bytes 2850824 | tf_op jit(solution)/shard_map/ppermute | solution.py:46
  90.5 35.4 %collective-permute-start.16 = (bf16[58,64,128]{2,1,0:T(8,128)(2,1)}, bf16[58,64,128]{2,1,0:T(8,128)(2,1)}, u32[]{:S(2)}, u32[]{:S(2)}) collective-permute-start(bf16[58,64,128]{2,1,0:T(8,128)(2,1)} %collective-permute-done.12.refs_8_.refs_7_.refs_10_), channel_id=1, source_target_pairs={{0,16},{1,17},{2,18},{3,19},{4,20},{5,21},{6,22},{7,23},{8,24},{9,... | collective-permute-start | bytes 2850824 | tf_op jit(solution)/shard_map/ppermute | solution.py:46
  93.7 11.7 %collective-permute-start.2 = (bf16[432,512]{1,0:T(8,128)(2,1)S(1)}, bf16[432,512]{1,0:T(8,128)(2,1)S(1)}, u32[]{:S(2)}, u32[]{:S(2)}) collective-permute-start(bf16[432,512]{1,0:T(8,128)(2,1)S(1)} %bitcast.221), channel_id=1, source_target_pairs={{0,1},{1,0},{2,5},{3,4},{4,3},{5,2},{6,7},{7,6},{8,9},{9,8},{10,13... | collective-permute-start | bytes 1327112 | tf_op jit(solution)/shard_map/ppermute | solution.py:46
  105.4 14.0 %collective-permute-start.4 = (bf16[432,512]{1,0:T(8,128)(2,1)}, bf16[432,512]{1,0:T(8,128)(2,1)S(1)}, u32[]{:S(2)}, u32[]{:S(2)}) collective-permute-start(bf16[432,512]{1,0:T(8,128)(2,1)} %bitcast.220), channel_id=1, source_target_pairs={{0,5},{1,4},{2,1},{3,0},{4,7},{5,6},{6,3},{7,2},{8,13},{9,12},{10,... | collective-permute-start | bytes 1327112 | tf_op jit(solution)/shard_map/ppermute | solution.py:46
  134.7 27.8 %collective-permute-start.24 = (bf16[864,256]{1,0:T(8,128)(2,1)}, bf16[864,256]{1,0:T(8,128)(2,1)S(1)}, u32[]{:S(2)}, u32[]{:S(2)}) collective-permute-start(bf16[864,256]{1,0:T(8,128)(2,1)} %get-tuple-element.37), channel_id=1, source_target_pairs={{0,4},{1,5},{2,6},{3,7},{4,0},{5,1},{6,2},{7,3},{8,12},{9,13},{10,... | collective-permute-start | bytes 1327112 | tf_op jit(solution)/shard_map/ppermute | solution.py:46
  145.8 17.4 %collective-permute-start.22 = (bf16[864,256]{1,0:T(8,128)(2,1)}, bf16[864,256]{1,0:T(8,128)(2,1)S(1)}, u32[]{:S(2)}, u32[]{:S(2)}) collective-permute-start(bf16[864,256]{1,0:T(8,128)(2,1)} %get-tuple-element.35), channel_id=1, source_target_pairs={{0,4},{1,5},{2,6},{3,7},{4,0},{5,1},{6,2},{7,3},{8,12},{9,13},{10,... | collective-permute-start | bytes 1327112 | tf_op jit(solution)/shard_map/ppermute | solution.py:46
  155.3 9.9 %collective-permute-start.20 = (bf16[864,256]{1,0:T(8,128)(2,1)}, bf16[864,256]{1,0:T(8,128)(2,1)S(1)}, u32[]{:S(2)}, u32[]{:S(2)}) collective-permute-start(bf16[864,256]{1,0:T(8,128)(2,1)} %get-tuple-element.33), channel_id=1, source_target_pairs={{0,4},{1,5},{2,6},{3,7},{4,0},{5,1},{6,2},{7,3},{8,12},{9,13},{10,... | collective-permute-start | bytes 1327112 | tf_op jit(solution)/shard_map/ppermute | solution.py:46
  162.6 6.6 %collective-permute-start.25 = (bf16[432,256]{1,0:T(8,128)(2,1)S(1)}, bf16[432,256]{1,0:T(8,128)(2,1)S(1)}, u32[]{:S(2)}, u32[]{:S(2)}) collective-permute-start(bf16[432,256]{1,0:T(8,128)(2,1)S(1)} %fusion.21), channel_id=1, source_target_pairs={{0,1},{1,0},{2,3},{3,2},{4,5},{5,4},{6,7},{7,6},{8,9},{9,8},{10,11... | collective-permute-start | bytes 663560 | tf_op jit(solution)/shard_map/ppermute | solution.py:46
  163.4 15.4 %collective-permute-start.23 = (bf16[432,256]{1,0:T(8,128)(2,1)S(1)}, bf16[432,256]{1,0:T(8,128)(2,1)S(1)}, u32[]{:S(2)}, u32[]{:S(2)}) collective-permute-start(bf16[432,256]{1,0:T(8,128)(2,1)S(1)} %fusion.20), channel_id=1, source_target_pairs={{0,1},{1,0},{2,3},{3,2},{4,5},{5,4},{6,7},{7,6},{8,9},{9,8},{10,11... | collective-permute-start | bytes 663560 | tf_op jit(solution)/shard_map/ppermute | solution.py:46
  164.5 14.2 %collective-permute-start.19 = (bf16[432,256]{1,0:T(8,128)(2,1)S(1)}, bf16[432,256]{1,0:T(8,128)(2,1)S(1)}, u32[]{:S(2)}, u32[]{:S(2)}) collective-permute-start(bf16[432,256]{1,0:T(8,128)(2,1)S(1)} %fusion.18), channel_id=1, source_target_pairs={{0,1},{1,0},{2,3},{3,2},{4,5},{5,4},{6,7},{7,6},{8,9},{9,8},{10,11... | collective-permute-start | bytes 663560 | tf_op jit(solution)/shard_map/ppermute | solution.py:46
  165.3 18.1 %collective-permute-start.21 = (bf16[432,256]{1,0:T(8,128)(2,1)S(1)}, bf16[432,256]{1,0:T(8,128)(2,1)S(1)}, u32[]{:S(2)}, u32[]{:S(2)}) collective-permute-start(bf16[432,256]{1,0:T(8,128)(2,1)S(1)} %fusion.19), channel_id=1, source_target_pairs={{0,1},{1,0},{2,3},{3,2},{4,5},{5,4},{6,7},{7,6},{8,9},{9,8},{10,11... | collective-permute-start | bytes 663560 | tf_op jit(solution)/shard_map/ppermute | solution.py:46
  187.7 14.6 %collective-permute-start.28 = (f32[17,256]{1,0:T(8,128)S(1)}, f32[17,256]{1,0:T(8,128)S(1)}, u32[]{:S(2)}, u32[]{:S(2)}) collective-permute-start(f32[17,256]{1,0:T(8,128)S(1)} %pad_maximum_fusion.6), channel_id=1, source_target_pairs={{0,16},{1,17},{2,18},{3,19},{4,20},{5,21},{6,22},{7,23},{8,24},{9,... | collective-permute-start | bytes 52232 | tf_op jit(solution)/shard_map/ppermute | solution.py:46
  189.0 13.3 %collective-permute-start.29 = (f32[17,256]{1,0:T(8,128)S(1)}, f32[17,256]{1,0:T(8,128)S(1)}, u32[]{:S(2)}, u32[]{:S(2)}) collective-permute-start(f32[17,256]{1,0:T(8,128)S(1)} %pad_maximum_fusion.6), channel_id=1, source_target_pairs={{0,24},{1,25},{2,26},{3,27},{4,28},{5,29},{6,30},{7,31},{8,16},{9,... | collective-permute-start | bytes 52232 | tf_op jit(solution)/shard_map/ppermute | solution.py:46
  190.1 12.1 %collective-permute-start.27 = (f32[17,256]{1,0:T(8,128)S(1)}, f32[17,256]{1,0:T(8,128)S(1)}, u32[]{:S(2)}, u32[]{:S(2)}) collective-permute-start(f32[17,256]{1,0:T(8,128)S(1)} %pad_maximum_fusion.6), channel_id=1, source_target_pairs={{0,8},{1,9},{2,10},{3,11},{4,12},{5,13},{6,14},{7,15},{8,0},{9,1},... | collective-permute-start | bytes 52232 | tf_op jit(solution)/shard_map/ppermute | solution.py:46
  202.4 18.6 %collective-permute-start.31 = (f32[17,256]{1,0:T(8,128)S(1)}, f32[17,256]{1,0:T(8,128)S(1)}, u32[]{:S(2)}, u32[]{:S(2)}) collective-permute-start(f32[17,256]{1,0:T(8,128)S(1)} %pad_maximum_fusion.7), channel_id=1, source_target_pairs={{0,2},{1,3},{2,0},{3,1},{4,6},{5,7},{6,4},{7,5},{8,10},{9,11},{10,... | collective-permute-start | bytes 52232 | tf_op jit(solution)/shard_map/ppermute | solution.py:46
  204.6 16.4 %collective-permute-start.32 = (f32[17,256]{1,0:T(8,128)S(1)}, f32[17,256]{1,0:T(8,128)S(1)}, u32[]{:S(2)}, u32[]{:S(2)}) collective-permute-start(f32[17,256]{1,0:T(8,128)S(1)} %pad_maximum_fusion.7), channel_id=1, source_target_pairs={{0,3},{1,2},{2,1},{3,0},{4,7},{5,6},{6,5},{7,4},{8,11},{9,10},{10,... | collective-permute-start | bytes 52232 | tf_op jit(solution)/shard_map/ppermute | solution.py:46
  204.6 16.4 %collective-permute-start.30 = (f32[17,256]{1,0:T(8,128)S(1)}, f32[17,256]{1,0:T(8,128)S(1)}, u32[]{:S(2)}, u32[]{:S(2)}) collective-permute-start(f32[17,256]{1,0:T(8,128)S(1)} %pad_maximum_fusion.7), channel_id=1, source_target_pairs={{0,1},{1,0},{2,3},{3,2},{4,5},{5,4},{6,7},{7,6},{8,9},{9,8},{10,11... | collective-permute-start | bytes 52232 | tf_op jit(solution)/shard_map/ppermute | solution.py:46
  226.7 3.4 collective-permute-start.36
  230.4 8.4 %collective-permute-start.38 = (f32[3,256]{1,0:T(4,128)S(1)}, f32[3,256]{1,0:T(4,128)S(1)}, u32[]{:S(2)}, u32[]{:S(2)}) collective-permute-start(f32[3,256]{1,0:T(4,128)S(1)} %pad_maximum_fusion.12), channel_id=1, source_target_pairs={{0,2},{1,3},{2,0},{3,1},{4,6},{5,7},{6,4},{7,5},{8,10},{9,11},{10,... | collective-permute-start | bytes 9224 | tf_op jit(solution)/shard_map/ppermute | solution.py:46
  231.7 7.2 %collective-permute-start.39 = (f32[3,256]{1,0:T(4,128)S(1)}, f32[3,256]{1,0:T(4,128)S(1)}, u32[]{:S(2)}, u32[]{:S(2)}) collective-permute-start(f32[3,256]{1,0:T(4,128)S(1)} %pad_maximum_fusion.12), channel_id=1, source_target_pairs={{0,3},{1,2},{2,1},{3,0},{4,7},{5,6},{6,5},{7,4},{8,11},{9,10},{10,... | collective-permute-start | bytes 9224 | tf_op jit(solution)/shard_map/ppermute | solution.py:46
  231.7 7.2 %collective-permute-start.37 = (f32[3,256]{1,0:T(4,128)S(1)}, f32[3,256]{1,0:T(4,128)S(1)}, u32[]{:S(2)}, u32[]{:S(2)}) collective-permute-start(f32[3,256]{1,0:T(4,128)S(1)} %pad_maximum_fusion.12), channel_id=1, source_target_pairs={{0,1},{1,0},{2,3},{3,2},{4,5},{5,4},{6,7},{7,6},{8,9},{9,8},{10,11... | collective-permute-start | bytes 9224 | tf_op jit(solution)/shard_map/ppermute | solution.py:46
  234.0 10.1 %collective-permute-start.41 = (bf16[432,256]{1,0:T(8,128)(2,1)S(1)}, bf16[432,256]{1,0:T(8,128)(2,1)S(1)}, u32[]{:S(2)}, u32[]{:S(2)}) collective-permute-start(bf16[432,256]{1,0:T(8,128)(2,1)S(1)} %bitcast.350), channel_id=1, source_target_pairs={{0,0},{1,1},{2,4},{3,5},{4,2},{5,3},{6,6},{7,7},{8,8},{9,9},{10,12... | collective-permute-start | bytes 663560 | tf_op jit(solution)/shard_map/ppermute | solution.py:46
  250.3 4.4 collective-permute-start.48
  250.7 4.2 collective-permute-start.47
  264.5 4.6 collective-permute-start.49
  269.8 3.5 collective-permute-start.52
  275.0 3.8 collective-permute-start.55
  277.3 3.5 collective-permute-start.54
  287.1 17.8 %collective-permute-start.56 = (bf16[432,1024]{1,0:T(8,128)(2,1)S(1)}, bf16[432,1024]{1,0:T(8,128)(2,1)S(1)}, u32[]{:S(2)}, u32[]{:S(2)}) collective-permute-start(bf16[432,1024]{1,0:T(8,128)(2,1)S(1)} %pad_maximum_fusion.3.refs_2_.refs_5_), channel_id=1, source_target_pairs={{0,1},{1,0},{2,3},{3,2},{4,5},{5,4},{6,7},{7,6},{8,9},{9,8},{10,11... | collective-permute-start | bytes 2654216 | tf_op jit(solution)/shard_map/ppermute | solution.py:46
  287.2 31.1 %collective-permute-start.57 = (bf16[432,1024]{1,0:T(8,128)(2,1)S(1)}, bf16[432,1024]{1,0:T(8,128)(2,1)}, u32[]{:S(2)}, u32[]{:S(2)}) collective-permute-start(bf16[432,1024]{1,0:T(8,128)(2,1)S(1)} %pad_maximum_fusion.3.refs_2_.refs_5_), channel_id=1, source_target_pairs={{0,4},{1,5},{2,6},{3,7},{4,0},{5,1},{6,2},{7,3},{8,12},{9,13},{10,... | collective-permute-start | bytes 2654216 | tf_op jit(solution)/shard_map/ppermute | solution.py:46
  304.9 13.5 %collective-permute-start.58 = (bf16[432,1024]{1,0:T(8,128)(2,1)S(1)}, bf16[432,1024]{1,0:T(8,128)(2,1)}, u32[]{:S(2)}, u32[]{:S(2)}) collective-permute-start(bf16[432,1024]{1,0:T(8,128)(2,1)S(1)} %collective-permute-done.56.refs_3_.refs_6_), channel_id=1, source_target_pairs={{0,4},{1,5},{2,6},{3,7},{4,0},{5,1},{6,2},{7,3},{8,12},{9,13},{10,... | collective-permute-start | bytes 2654216 | tf_op jit(solution)/shard_map/ppermute | solution.py:46
  311.4 58.4 %collective-permute-start.40 = (bf16[432,256]{1,0:T(8,128)(2,1)}, bf16[432,256]{1,0:T(8,128)(2,1)S(1)}, u32[]{:S(2)}, u32[]{:S(2)}) collective-permute-start(bf16[432,256]{1,0:T(8,128)(2,1)} %get-tuple-element.161), channel_id=1, source_target_pairs={{0,0},{1,1},{2,4},{3,5},{4,2},{5,3},{6,6},{7,7},{8,8},{9,9},{10,12... | collective-permute-start | bytes 663560 | tf_op jit(solution)/shard_map/ppermute | solution.py:46
  316.8 80.7 %reduce-scatter.7.cloned.1.call-start = ((), (), s32[]{:S(2)}) async-start(), calls=%async_computation.3 | async-start | bytes 163840
  343.6 26.3 %collective-permute-start.63 = (bf16[58,64,128]{2,1,0:T(8,128)(2,1)}, bf16[58,64,128]{2,1,0:T(8,128)(2,1)}, u32[]{:S(2)}, u32[]{:S(2)}) collective-permute-start(bf16[58,64,128]{2,1,0:T(8,128)(2,1)} %get-tuple-element.46), channel_id=1, source_target_pairs={{0,16},{1,17},{2,18},{3,19},{4,20},{5,21},{6,22},{7,23},{8,24},{9,... | collective-permute-start | bytes 2850824 | tf_op jit(solution)/shard_map/ppermute | solution.py:46
  344.0 47.6 %collective-permute-start.68 = (bf16[58,64,128]{2,1,0:T(8,128)(2,1)}, bf16[58,64,128]{2,1,0:T(8,128)(2,1)S(1)}, u32[]{:S(2)}, u32[]{:S(2)}) collective-permute-start(bf16[58,64,128]{2,1,0:T(8,128)(2,1)} %get-tuple-element.51), channel_id=1, source_target_pairs={{0,8},{1,9},{2,10},{3,11},{4,12},{5,13},{6,14},{7,15},{8,0},{9,1},... | collective-permute-start | bytes 2850824 | tf_op jit(solution)/shard_map/ppermute | solution.py:46
  365.6 25.5 %collective-permute-start.59 = (bf16[432,512]{1,0:T(8,128)(2,1)}, bf16[432,512]{1,0:T(8,128)(2,1)S(1)}, u32[]{:S(2)}, u32[]{:S(2)}) collective-permute-start(bf16[432,512]{1,0:T(8,128)(2,1)} %get-tuple-element.39), channel_id=1, source_target_pairs={{0,3},{1,2},{2,7},{3,6},{4,1},{5,0},{6,5},{7,4},{8,11},{9,10},{10,... | collective-permute-start | bytes 1327112 | tf_op jit(solution)/shard_map/ppermute | solution.py:46
  368.0 31.4 %collective-permute-start.60 = (bf16[432,512]{1,0:T(8,128)(2,1)}, bf16[432,512]{1,0:T(8,128)(2,1)}, u32[]{:S(2)}, u32[]{:S(2)}) collective-permute-start(bf16[432,512]{1,0:T(8,128)(2,1)} %get-tuple-element.40), channel_id=1, source_target_pairs={{0,2},{1,3},{2,6},{3,7},{4,0},{5,1},{6,4},{7,5},{8,10},{9,11},{10,... | collective-permute-start | bytes 1327112 | tf_op jit(solution)/shard_map/ppermute | solution.py:46
  369.7 32.3 %collective-permute-start.61 = (bf16[432,512]{1,0:T(8,128)(2,1)}, bf16[432,512]{1,0:T(8,128)(2,1)}, u32[]{:S(2)}, u32[]{:S(2)}) collective-permute-start(bf16[432,512]{1,0:T(8,128)(2,1)} %get-tuple-element.41), channel_id=1, source_target_pairs={{0,1},{1,0},{2,5},{3,4},{4,3},{5,2},{6,7},{7,6},{8,9},{9,8},{10,13... | collective-permute-start | bytes 1327112 | tf_op jit(solution)/shard_map/ppermute | solution.py:46
  369.9 38.5 %collective-permute-start.62 = (bf16[432,512]{1,0:T(8,128)(2,1)}, bf16[432,512]{1,0:T(8,128)(2,1)}, u32[]{:S(2)}, u32[]{:S(2)}) collective-permute-start(bf16[432,512]{1,0:T(8,128)(2,1)} %get-tuple-element.42), channel_id=1, source_target_pairs={{0,0},{1,1},{2,4},{3,5},{4,2},{5,3},{6,6},{7,7},{8,8},{9,9},{10,12... | collective-permute-start | bytes 1327112 | tf_op jit(solution)/shard_map/ppermute | solution.py:46
  391.1 25.9 %collective-permute-start.65 = (bf16[58,64,128]{2,1,0:T(8,128)(2,1)}, bf16[58,64,128]{2,1,0:T(8,128)(2,1)}, u32[]{:S(2)}, u32[]{:S(2)}) collective-permute-start(bf16[58,64,128]{2,1,0:T(8,128)(2,1)} %get-tuple-element.47), channel_id=1, source_target_pairs={{0,16},{1,17},{2,18},{3,19},{4,20},{5,21},{6,22},{7,23},{8,24},{9,... | collective-permute-start | bytes 2850824 | tf_op jit(solution)/shard_map/ppermute | solution.py:46
  391.6 25.4 %collective-permute-start.64 = (bf16[58,64,128]{2,1,0:T(8,128)(2,1)}, bf16[58,64,128]{2,1,0:T(8,128)(2,1)}, u32[]{:S(2)}, u32[]{:S(2)}) collective-permute-start(bf16[58,64,128]{2,1,0:T(8,128)(2,1)} %add_convert_fusion.3), channel_id=1, source_target_pairs={{0,8},{1,9},{2,10},{3,11},{4,12},{5,13},{6,14},{7,15},{8,0},{9,1},... | collective-permute-start | bytes 2850824 | tf_op jit(solution)/shard_map/ppermute | solution.py:46
  399.4 29.4 %collective-permute-start.67 = (bf16[58,64,128]{2,1,0:T(8,128)(2,1)}, bf16[58,64,128]{2,1,0:T(8,128)(2,1)}, u32[]{:S(2)}, u32[]{:S(2)}) collective-permute-start(bf16[58,64,128]{2,1,0:T(8,128)(2,1)} %get-tuple-element.49), channel_id=1, source_target_pairs={{0,8},{1,9},{2,10},{3,11},{4,12},{5,13},{6,14},{7,15},{8,0},{9,1},... | collective-permute-start | bytes 2850824 | tf_op jit(solution)/shard_map/ppermute | solution.py:46
  402.1 26.8 %collective-permute-start.69 = (bf16[58,64,128]{2,1,0:T(8,128)(2,1)S(1)}, bf16[58,64,128]{2,1,0:T(8,128)(2,1)}, u32[]{:S(2)}, u32[]{:S(2)}) collective-permute-start(bf16[58,64,128]{2,1,0:T(8,128)(2,1)S(1)} %add_convert_fusion.1), channel_id=1, source_target_pairs={{0,16},{1,17},{2,18},{3,19},{4,20},{5,21},{6,22},{7,23},{8,24},{9,... | collective-permute-start | bytes 2850824 | tf_op jit(solution)/shard_map/ppermute | solution.py:46
  419.4 44.1 %collective-permute-start.66 = (bf16[16,64,128]{2,1,0:T(8,128)(2,1)S(1)}, bf16[16,64,128]{2,1,0:T(8,128)(2,1)S(1)}, u32[]{:S(2)}, u32[]{:S(2)}) collective-permute-start(bf16[16,64,128]{2,1,0:T(8,128)(2,1)S(1)} %slice.602), channel_id=1, source_target_pairs={{0,1},{1,0},{2,3},{3,2},{4,5},{5,4},{6,7},{7,6},{8,9},{9,8},{10,11... | collective-permute-start | bytes 786440 | tf_op jit(solution)/shard_map/ppermute | solution.py:46
  420.7 16.2 %collective-permute-start.74 = (bf16[13,64,128]{2,1,0:T(8,128)(2,1)S(1)}, bf16[13,64,128]{2,1,0:T(8,128)(2,1)S(1)}, u32[]{:S(2)}, u32[]{:S(2)}) collective-permute-start(bf16[13,64,128]{2,1,0:T(8,128)(2,1)S(1)} %get-tuple-element.143), channel_id=1, source_target_pairs={{0,4},{1,5},{2,6},{3,7},{4,0},{5,1},{6,2},{7,3},{8,12},{9,13},{10,... | collective-permute-start | bytes 638984 | tf_op jit(solution)/shard_map/ppermute | solution.py:46
  424.6 15.7 %collective-permute-start.72 = (bf16[13,64,128]{2,1,0:T(8,128)(2,1)S(1)}, bf16[13,64,128]{2,1,0:T(8,128)(2,1)S(1)}, u32[]{:S(2)}, u32[]{:S(2)}) collective-permute-start(bf16[13,64,128]{2,1,0:T(8,128)(2,1)S(1)} %get-tuple-element.144), channel_id=1, source_target_pairs={{0,5},{1,4},{2,7},{3,6},{4,1},{5,0},{6,3},{7,2},{8,13},{9,12},{10,... | collective-permute-start | bytes 638984 | tf_op jit(solution)/shard_map/ppermute | solution.py:46
  430.9 9.4 %collective-permute-start.75 = (bf16[13,64,128]{2,1,0:T(8,128)(2,1)S(1)}, bf16[13,64,128]{2,1,0:T(8,128)(2,1)S(1)}, u32[]{:S(2)}, u32[]{:S(2)}) collective-permute-start(bf16[13,64,128]{2,1,0:T(8,128)(2,1)S(1)} %get-tuple-element.145), channel_id=1, source_target_pairs={{0,6},{1,7},{2,4},{3,5},{4,2},{5,3},{6,0},{7,1},{8,14},{9,15},{10,... | collective-permute-start | bytes 638984 | tf_op jit(solution)/shard_map/ppermute | solution.py:46
  431.5 31.8 %collective-permute-start.73 = (bf16[13,64,128]{2,1,0:T(8,128)(2,1)S(1)}, bf16[13,64,128]{2,1,0:T(8,128)(2,1)S(1)}, u32[]{:S(2)}, u32[]{:S(2)}) collective-permute-start(bf16[13,64,128]{2,1,0:T(8,128)(2,1)S(1)} %get-tuple-element.146), channel_id=1, source_target_pairs={{0,7},{1,6},{2,5},{3,4},{4,3},{5,2},{6,1},{7,0},{8,15},{9,14},{10,... | collective-permute-start | bytes 638984 | tf_op jit(solution)/shard_map/ppermute | solution.py:46
  437.0 27.8 %collective-permute-start.71 = (bf16[16,64,128]{2,1,0:T(8,128)(2,1)S(1)}, bf16[16,64,128]{2,1,0:T(8,128)(2,1)S(1)}, u32[]{:S(2)}, u32[]{:S(2)}) collective-permute-start(bf16[16,64,128]{2,1,0:T(8,128)(2,1)S(1)} %get-tuple-element.147), channel_id=1, source_target_pairs={{0,2},{1,3},{2,0},{3,1},{4,6},{5,7},{6,4},{7,5},{8,10},{9,11},{10,... | collective-permute-start | bytes 786440 | tf_op jit(solution)/shard_map/ppermute | solution.py:46
  440.3 34.2 %collective-permute-start.70 = (bf16[16,64,128]{2,1,0:T(8,128)(2,1)S(1)}, bf16[16,64,128]{2,1,0:T(8,128)(2,1)S(1)}, u32[]{:S(2)}, u32[]{:S(2)}) collective-permute-start(bf16[16,64,128]{2,1,0:T(8,128)(2,1)S(1)} %get-tuple-element.148), channel_id=1, source_target_pairs={{0,3},{1,2},{2,1},{3,0},{4,7},{5,6},{6,5},{7,4},{8,11},{9,10},{10,... | collective-permute-start | bytes 786440 | tf_op jit(solution)/shard_map/ppermute | solution.py:46
  (87 other events, 1747.7 us)
Sparse Core Ops, SparseCore 0:
  316.9 34.4 reduce-scatter.4
  368.2 29.2 reduce-scatter.6

commit v2 on v1

v2 whole, which is shorter than its diff:
```python
import jax
import jax.numpy as jnp
from jax import lax
from jax.experimental import pallas as pl
from jax.experimental.pallas import tpu as pltpu
from jax.sharding import PartitionSpec as P

epsilon = 1e-05
dilations = (6, 12, 18)
LANES = 128
BLOCK_ROWS = 6
AXES = ("dp", "rows")
FULL, SHORT, PER_CHIP = 14, 13, 27
SLOTS = FULL + 2 + SHORT
CUT = 15
NT = (((1,), (1,)), ((), ()))
TN = (((0,), (0,)), ((), ()))
NN = (((1,), (0,)), ((), ()))


def dot(first, second, dims):
    return lax.dot_general(first, second, dims, preferred_element_type=jnp.float32)


def after(x, *first):
    return lax.optimization_barrier((x, first))[0]


def silu_slope(values):
    sigma = jax.nn.sigmoid(values)
    return sigma * (1.0 + values * (1.0 - sigma))


class Place:
    def __init__(self):
        self.nd, self.nr = lax.axis_size("dp"), lax.axis_size("rows")
        self.nzl = self.nr // 2
        d, z = lax.axis_index("dp"), lax.axis_index("rows")
        self.d, self.z = d, z
        self.m, self.c = d // 2, d % 2
        self.zh, self.zl = z // self.nzl, z % self.nzl
        self.part = self.c * self.nzl + self.zl
        self.image = 2 * self.m + self.zh

    def swap(self, x, m=0, c=0, zh=0, zl=0):
        nzl = self.nzl
        pairs = []
        for flat in range(self.nd * self.nr):
            d, z = divmod(flat, self.nr)
            pairs.append((flat, (d ^ (2 * m + c)) * self.nr + (z ^ (zh * nzl + zl))))
        return lax.ppermute(x, AXES, pairs)


def by_xor(items, index):
    items = list(items)
    bit = 1
    while bit < len(items):
        flip = (index & bit) != 0
        pick = lambda a, b: jnp.where(flip, a, b)
        items = [jax.tree.map(pick, items[k ^ bit], items[k]) for k in range(len(items))]
        bit *= 2
    return items


def tree(items):
    items = list(items)
    while len(items) > 1:
        items = [items[i] + items[i + 1] for i in range(0, len(items), 2)]
    return items[0]


def exchange_stages(place):
    return (
        [dict(c=1)],
        [dict(m=k) for k in range(1, place.nd // 2)],
        [dict(zh=k // place.nzl, zl=k % place.nzl) for k in range(1, place.nr)],
    )


def total(place, x):
    for stage in exchange_stages(place):
        x = tree([x] + [place.swap(x, **s) for s in stage])
    return x


def moments(place, sums, squares, count, extra=None):
    width = sums.shape[1]
    k = sums.shape[0]
    rows = [sums, squares, jnp.full((1, width), count, jnp.float32)]
    if extra is not None:
        rows.append(extra)
    x = jnp.concatenate(rows, axis=0)
    for stage in exchange_stages(place):
        xs = [x] + [place.swap(x, **s) for s in stage]
        whole = tree(xs)
        n = whole[2 * k : 2 * k + 1]
        mean = whole[:k] / jnp.maximum(n, 1.0)
        between = []
        for y in xs:
            own = y[2 * k : 2 * k + 1]
            gap = y[:k] / jnp.maximum(own, 1.0) - mean
            between.append(own * gap * gap)
        x = jnp.concatenate([whole[:k], whole[k : 2 * k] + tree(between), whole[2 * k :]], axis=0)
    n = x[2 * k : 2 * k + 1]
    return x[:k] / n, x[k : 2 * k] / n, n, x[2 * k + 1 :]


def local_moments(values, mask, count):
    sums = jnp.sum(values * mask, axis=0, keepdims=True)
    centred = (values - sums / jnp.maximum(count, 1.0)) * mask
    return sums, jnp.sum(centred * centred, axis=0, keepdims=True)


def line_pieces(place, dilated, pointwise, pooling):
    tiles = lambda w: jnp.transpose(w.T.reshape(w.shape[1], w.shape[0] // LANES, LANES), (1, 0, 2))
    dil, one, pool = tiles(dilated), tiles(pointwise), tiles(pooling)
    other = [dil[2 + r :: 4][:SHORT] for r in range(2)]
    got = place.swap(jnp.concatenate(other, axis=0), c=1)
    same = [jnp.concatenate([dil[r::4][:FULL], one[r : r + 1], pool[r : r + 1]], axis=0) for r in range(2)]
    whole = [jnp.concatenate([same[r], got[r * SHORT : (r + 1) * SHORT]], axis=0) for r in range(2)]
    return by_xor(whole, place.zl)


def plane_direct(place, half):
    return place.swap(half, m=1), place.swap(half, m=2)


def plane_diagonal(place, by_x, by_y):
    return place.swap(by_x[:CUT], m=2), place.swap(by_y[CUT:], m=1)


def add_low(first, *others):
    out = first.astype(jnp.float32)
    for o in others:
        out = out + o.astype(jnp.float32)
    return out.astype(jnp.bfloat16)


def plane_scatter(place, pieces):
    first_d, second_d = place.swap(pieces[3][0], m=2), place.swap(pieces[3][1], m=1)
    to_x = jnp.stack([add_low(pieces[1][0], first_d), pieces[1][1]])
    to_y = jnp.stack([pieces[2][0], add_low(pieces[2][1], second_d)])
    by_x, by_y = place.swap(to_x, m=1), place.swap(to_y, m=2)
    return [add_low(pieces[0][q], by_x[q], by_y[q]) for q in range(2)]


def line_back(place, quarters):
    by_kl = by_xor(quarters, place.zl)
    by_part = by_xor([by_kl[0], place.swap(by_kl[1], zl=1)], place.zl)
    same = [p[: FULL + 2] for p in by_part]
    got = place.swap(jnp.concatenate([p[FULL + 2 :] for p in by_part], axis=0), c=1)
    other = [got[r * SHORT : (r + 1) * SHORT] for r in range(2)]
    gap = jnp.zeros((FULL - SHORT,) + other[0].shape[1:], other[0].dtype)
    dil = jnp.stack([s[:FULL] for s in same] + [jnp.concatenate([o, gap], axis=0) for o in other], axis=1)
    dil = dil.reshape((4 * FULL,) + dil.shape[2:])[: 2 * PER_CHIP]
    rows = lambda t: jnp.transpose(t, (1, 0, 2)).reshape(t.shape[1], t.shape[0] * LANES).astype(jnp.float32).T
    one = jnp.stack([s[FULL] for s in same])
    pool = jnp.stack([s[FULL + 1] for s in same])
    return rows(dil), rows(one), rows(pool)


def gathered_tiles(place, dilated, pointwise, pooling):
    whole = []
    for w in (dilated, pointwise, pooling):
        w = lax.all_gather(w, "rows", axis=1, tiled=True)
        w = lax.all_gather(w, "dp", axis=0, tiled=True)
        channels = pointwise.shape[0] * place.nd
        taps = w.shape[0] // channels
        w = w.reshape(taps, channels // (LANES * place.nr), place.nr, LANES, w.shape[1])
        w = lax.dynamic_index_in_dim(w, place.part, 2, keepdims=False)
        whole.append(jnp.transpose(w.reshape(taps, channels // place.nr, w.shape[-1]), (0, 2, 1)))
    return jnp.concatenate(whole, axis=0)


def scattered_tiles(place, gradients):
    outs = []
    taps, half, width = gradients.shape
    for g in (gradients[: taps - 2], gradients[taps - 2 : taps - 1], gradients[taps - 1 :]):
        g = jnp.transpose(g, (0, 2, 1)).reshape(g.shape[0], width // LANES, 1, LANES, half)
        spread = jnp.zeros((g.shape[0], width // LANES, place.nr, LANES, 2 * half), g.dtype)
        g = lax.dynamic_update_slice(spread, g, (0, 0, place.part, 0, place.zh * half)).reshape(-1, 2 * half)
        g = lax.psum_scatter(g, "dp", scatter_dimension=0, tiled=True)
        outs.append(lax.psum_scatter(g, "rows", scatter_dimension=1, tiled=True).astype(jnp.float32))
    return outs


def doubling(place):
    steps = []
    for name, index, size in (("zl", place.zl, place.nzl), ("zh", place.zh, 2), ("c", place.c, 2), ("m", place.m, place.nd // 2)):
        bit = 1
        while bit < size:
            steps.append(({name: bit}, (index & bit) != 0))
            bit *= 2
    return steps


def joined(place, x, step):
    swap, upper = step
    return jnp.stack(by_xor([x, place.swap(x, **swap)], upper.astype(jnp.int32)))


def halved(place, x, step):
    swap, upper = step
    mine = by_xor([x[0], x[1]], upper.astype(jnp.int32))
    return add_low(mine[0], place.swap(mine[1], **swap))


class Shape:
    def __init__(self, band_rows, columns, nr, width, out, pieces):
        self.band_rows, self.columns, self.nr, self.width, self.out = band_rows, columns, nr, width, out
        self.rows = band_rows * nr
        self.band, self.pixels = band_rows * columns, band_rows * columns * nr
        self.block = BLOCK_ROWS * columns
        self.blocks = self.rows // BLOCK_ROWS
        self.pieces = pieces
        self.quarter = out // 4

    def regions(self, dilation):
        cuts = sorted({0, min(dilation, self.rows), max(self.rows - dilation, 0), self.rows})
        for lo, hi in zip(cuts, cuts[1:]):
            yield lo, hi, [r for r in range(3) if 0 <= lo + (r - 1) * dilation and hi + (r - 1) * dilation <= self.rows]


ANY = pl.BlockSpec(memory_space=pl.ANY)
SMEM = pl.BlockSpec(memory_space=pltpu.SMEM)
VMEM = pl.BlockSpec(memory_space=pltpu.VMEM)
PARAMS = pltpu.CompilerParams(vmem_limit_bytes=58 * 2**20)


LIGHT = pl.CostEstimate(flops=0, bytes_accessed=0, transcendentals=0)


def lanes_at(start, size=LANES):
    return pl.ds(pl.multiple_of(start, LANES), size)


def start_bands(shape, refs, scratch, sem, part):
    for k, ref in enumerate(refs):
        pltpu.make_async_copy(ref, scratch.at[pl.ds((part ^ k) * shape.band, shape.band), :], sem.at[k]).start()


def start_cuts(shape, refs, scratch, sem, part):
    for k, cuts in enumerate(refs):
        first = 0
        for ref in cuts:
            place = scratch.at[pl.ds((part ^ k) * shape.band + first, ref.shape[0]), :]
            pltpu.make_async_copy(ref, place, sem.at[k]).start()
            first += ref.shape[0]


def wait_bands(shape, refs, scratch, sem):
    for k, ref in enumerate(refs):
        pltpu.make_async_copy(ref, scratch.at[pl.ds(k * shape.band, shape.band), :], sem.at[k]).wait()


def split_features(shape, features, mask, c):
    tiles, n = shape.width // LANES, shape.nr // 2

    def kernel(info, x, mask_ref, *outs):
        valid = mask_ref[...].astype(jnp.bfloat16)
        for k, out in enumerate(outs):
            for q in range(n):
                for i in range(tiles):
                    at = (i * shape.nr + (info[0] ^ k) * n + q) * LANES
                    out[q, :, i * LANES : (i + 1) * LANES] = x[:, lanes_at(at)] * valid

    return pl.pallas_call(
        kernel,
        out_shape=[jax.ShapeDtypeStruct((n, shape.band, shape.width), jnp.bfloat16)] * 2,
        in_specs=[SMEM, VMEM, VMEM],
        out_specs=[VMEM] * 2,
        compiler_params=PARAMS,
        cost_estimate=LIGHT,
        name="split_features",
    )(c.reshape(1), features, mask)


def join_features(shape, own, other, c, zl):
    tiles, n = shape.width // LANES, shape.nr // 2

    def kernel(info, *refs):
        for k, part in enumerate(refs[: 2 * n]):
            core, q = info[0] ^ (k // n), info[1] ^ (k % n)
            for i in range(tiles):
                at = (i * shape.nr + core * n + q) * LANES
                refs[2 * n][:, lanes_at(at)] = part[:, i * LANES : (i + 1) * LANES]

    return pl.pallas_call(
        kernel,
        out_shape=jax.ShapeDtypeStruct((shape.band, shape.width * shape.nr), jnp.bfloat16),
        in_specs=[SMEM] + [VMEM] * shape.nr,
        out_specs=VMEM,
        compiler_params=PARAMS,
        cost_estimate=LIGHT,
        name="join_features",
    )(jnp.stack([c, zl]).astype(jnp.int32), *own, *other)


def packed_half(shape, zl, pieces):
    size = shape.quarter

    def kernel(info, *refs):
        for kl, ref in enumerate(refs[:2]):
            refs[2][:, pl.ds(pl.multiple_of((info[0] ^ kl) * size, size), size), :] = ref[...]

    return pl.pallas_call(
        kernel,
        out_shape=jax.ShapeDtypeStruct((SLOTS, 2 * size, LANES), jnp.bfloat16),
        in_specs=[SMEM] + [VMEM] * 2,
        out_specs=VMEM,
        compiler_params=PARAMS,
        cost_estimate=LIGHT,
        name="packed_half",
    )(zl.reshape(1), *pieces)


def chip_slot(t, c):
    return jnp.where(jnp.where(c == 0, t < FULL, t >= SHORT), t - SHORT * c, FULL + 2 + t - FULL * (1 - c))


def assembled_weights(shape, info, own, by_x, by_y, diagonal):
    def kernel(info, *refs):
        ins, out, sem = refs[:5], refs[5], refs[6]
        m, c = info[0], info[1]

        def copy(ref, slot, tap, lane):
            pltpu.make_async_copy(ref.at[slot], out.at[tap, :, lanes_at(lane)], sem).start()

        def place(rel, slot, tap, lane):
            if rel < 3:
                copy(ins[rel], slot, tap, lane)
            else:

                @pl.when(slot < CUT)
                def _():
                    copy(ins[3], slot, tap, lane)

                @pl.when(slot >= CUT)
                def _():
                    copy(ins[4], slot - CUT, tap, lane)

        for rel in range(4):
            chip = m ^ rel

            def body(t, carry):
                v = chip * PER_CHIP + t
                place(rel, chip_slot(t, c), v // 4, (v % 4) * LANES)
                return carry

            lax.fori_loop(0, PER_CHIP, body, 0)
            for extra in range(2):
                place(rel, FULL + extra, 27 + extra, chip * LANES)
        pltpu.make_async_copy(out, out, sem).wait()

    return pl.pallas_call(
        kernel,
        out_shape=jax.ShapeDtypeStruct((29, shape.out // 2, shape.width), jnp.bfloat16),
        in_specs=[SMEM] + [ANY] * 5,
        out_specs=VMEM,
        scratch_shapes=[pltpu.SemaphoreType.DMA],
        compiler_params=PARAMS,
        cost_estimate=LIGHT,
        name="assembled_weights",
    )(info, own, by_x, by_y, *diagonal)


def shifted(values, by, columns):
    if by == 0:
        return values
    pixels = values.shape[0]
    source = lax.broadcasted_iota(jnp.int32, (pixels, 1), 0) % columns - by
    return jnp.where((source >= 0) & (source < columns), pltpu.roll(values, by % pixels, 0), 0.0)


def put_halves(shape, c, blk, value, keep, sent, lane):
    half = shape.blocks // 2
    rows, lanes = pl.ds((blk % half) * shape.block, shape.block), slice(lane, lane + shape.out)

    @pl.when(c == blk // half)
    def _():
        keep[rows, lanes] = value

    @pl.when(c != blk // half)
    def _():
        sent[rows, lanes] = value.astype(sent.dtype)


def half_shapes(shape, n):
    half = shape.pixels // 2
    return [
        jax.ShapeDtypeStruct((half, n * shape.out), jnp.float32),
        jax.ShapeDtypeStruct((half, n * shape.out), jnp.bfloat16),
    ]


def start_taps(weights, scratch, sem, taps, zh):
    half = weights[0].shape[1]
    for n, tap in enumerate(taps):
        for kh, ref in enumerate(weights):
            columns = pl.ds(pl.multiple_of((zh ^ kh) * half, half), half)
            pltpu.make_async_copy(ref.at[tap], scratch.at[n, columns], sem.at[n]).start()


def wait_taps(scratch, sem, some):
    for n in some:
        pltpu.make_async_copy(scratch.at[n], scratch.at[n], sem.at[n]).wait()


def dilated_products(shape, branch, x, w, first, y):
    dilation, columns = dilations[branch], shape.columns
    for s in range(3):
        for lo, hi, rs in shape.regions(dilation):
            pixels = jnp.concatenate(
                [x[(lo + (r - 1) * dilation) * columns : (hi + (r - 1) * dilation) * columns, :] for r in rs], axis=1
            )
            taps = jnp.concatenate([w[first + 3 * s + r] for r in rs], axis=1)
            y[s, lo * columns : hi * columns, :] = dot(pixels, taps, NT)


def put_dilated(shape, branch, y, c, keep, sent, lane):
    dilation, columns = dilations[branch], shape.columns
    for blk in range(shape.blocks):
        at = slice(blk * shape.block, (blk + 1) * shape.block)
        z = y[1, at, :] + shifted(y[0, at, :], dilation, columns) + shifted(y[2, at, :], -dilation, columns)
        put_halves(shape, c, blk, z, keep, sent, lane)


def taps_of(branch):
    return [9 * branch + 3 * r + s for s in range(3) for r in range(3)]


def far_sums(shape, info, bands, weights):
    nr = shape.nr

    def kernel(info, *refs):
        ins, weights = refs[:nr], refs[nr : nr + 2]
        keep, sent, x, w, y, band_sem, w_sem = refs[nr + 2 :]
        start_bands(shape, ins, x, band_sem, info[5])
        start_taps(weights, w, w_sem, taps_of(2) + taps_of(1), info[2])
        wait_bands(shape, ins, x, band_sem)
        for n, branch in enumerate((2, 1)):
            wait_taps(w, w_sem, range(9 * n, 9 * n + 9))
            dilated_products(shape, branch, x, w, 9 * n, y)
            put_dilated(shape, branch, y, info[1], keep, sent, n * shape.out)

    return pl.pallas_call(
        kernel,
        out_shape=half_shapes(shape, 2),
        in_specs=[SMEM] + [ANY] * (nr + 2),
        out_specs=[VMEM] * 2,
        scratch_shapes=[
            pltpu.VMEM((shape.pixels, shape.width), jnp.bfloat16),
            pltpu.VMEM((18, shape.out, shape.width), jnp.bfloat16),
            pltpu.VMEM((3, shape.pixels, shape.out), jnp.float32),
            pltpu.SemaphoreType.DMA((nr,)),
            pltpu.SemaphoreType.DMA((18,)),
        ],
        compiler_params=PARAMS,
        cost_estimate=LIGHT,
        name="far_sums",
    )(info, *bands, *weights)


def near_sums(shape, info, area, bands, weights):
    nr = shape.nr

    def kernel(info, area, *refs):
        ins, weights = refs[:nr], refs[nr : nr + 2]
        keep, sent, pooled, lifted, x, w, y, band_sem, w_sem = refs[nr + 2 :]
        start_bands(shape, ins, x, band_sem, info[5])
        start_taps(weights, w, w_sem, taps_of(0) + [27, 28], info[2])
        wait_bands(shape, ins, x, band_sem)
        wait_taps(w, w_sem, range(11))
        dilated_products(shape, 0, x, w, 0, y)
        put_dilated(shape, 0, y, info[1], keep, sent, 0)
        sums = jnp.zeros((1, shape.width), jnp.float32)
        for blk in range(shape.blocks):
            values = x[blk * shape.block : (blk + 1) * shape.block, :]
            sums = sums + jnp.sum(values.astype(jnp.float32), axis=0, keepdims=True)
            put_halves(shape, info[1], blk, dot(values, w[9], NT), keep, sent, shape.out)
        low = jnp.broadcast_to(sums / area[0], pooled.shape).astype(jnp.bfloat16)
        first = lax.broadcasted_iota(jnp.int32, pooled.shape, 0) == 0
        pooled[...] = jnp.where(first, low.astype(jnp.float32), 0.0).astype(jnp.bfloat16)
        lifted[...] = dot(pooled[...], w[10], NT)

    return pl.pallas_call(
        kernel,
        out_shape=half_shapes(shape, 2)
        + [jax.ShapeDtypeStruct((16, shape.width), jnp.bfloat16), jax.ShapeDtypeStruct((16, shape.out), jnp.float32)],
        in_specs=[SMEM, SMEM] + [ANY] * (nr + 2),
        out_specs=[VMEM] * 4,
        scratch_shapes=[
            pltpu.VMEM((shape.pixels, shape.width), jnp.bfloat16),
            pltpu.VMEM((11, shape.out, shape.width), jnp.bfloat16),
            pltpu.VMEM((3, shape.pixels, shape.out), jnp.float32),
            pltpu.SemaphoreType.DMA((nr,)),
            pltpu.SemaphoreType.DMA((11,)),
        ],
        compiler_params=PARAMS,
        cost_estimate=LIGHT,
        name="near_sums",
    )(info, area, *bands, *weights)


def moved_columns(shape, delta, lane, lanes, branch, moved):
    for blk in range(shape.blocks):
        at = slice(blk * shape.block, (blk + 1) * shape.block)
        values = delta[at, lanes_at(lane, lanes)].astype(jnp.float32)
        for s in range(3):
            moved[at, s * lanes : (s + 1) * lanes] = shifted(
                values, (s - 1) * dilations[branch], shape.columns
            ).astype(jnp.bfloat16)


def input_gradient(shape, info, area, deltas, pool_delta, mask, weights):
    nr, columns = shape.nr, shape.columns

    def kernel(info, area, *refs):
        ins, pool_delta, mask, weights = refs[:nr], refs[nr], refs[nr + 1], refs[nr + 2 : nr + 4]
        outs = refs[nr + 4 : 2 * nr + 4]
        delta, moved, w, acc, delta_sem, w_sem = refs[2 * nr + 4 :]
        start_bands(shape, ins, delta, delta_sem, info[4])
        start_taps(weights, w, w_sem, range(29), info[2])
        wait_bands(shape, ins, delta, delta_sem)
        wait_taps(w, w_sem, range(29))
        pool = dot(pool_delta[...], w[28], NN)[0:1] / area[0]
        acc[...] = dot(delta[:, : shape.out], w[27], NN) + pool
        for branch in range(3):
            dilation = dilations[branch]
            moved_columns(shape, delta, (branch + 1) * shape.out, shape.out, branch, moved)
            for lo, hi, rs in shape.regions(dilation):
                rows = [2 - r for r in rs]
                pixels = jnp.concatenate(
                    [moved[(lo - (r - 1) * dilation) * columns : (hi - (r - 1) * dilation) * columns, :] for r in rows],
                    axis=1,
                )
                taps = jnp.concatenate([w[9 * branch + 3 * r + s] for r in rows for s in range(3)], axis=0)
                acc[lo * columns : hi * columns, :] += dot(pixels, taps, NN)
        for k in range(nr):
            at = pl.ds(pl.multiple_of((info[5] ^ k) * shape.band, shape.band), shape.band)
            outs[k][...] = (acc[at, :] * mask[at, :]).astype(jnp.bfloat16)

    return pl.pallas_call(
        kernel,
        out_shape=[jax.ShapeDtypeStruct((shape.band, shape.width), jnp.bfloat16)] * nr,
        in_specs=[SMEM, SMEM] + [ANY] * nr + [VMEM] * 2 + [ANY] * 2,
        out_specs=[VMEM] * nr,
        scratch_shapes=[
            pltpu.VMEM((shape.pixels, 4 * shape.out), jnp.bfloat16),
            pltpu.VMEM((shape.pixels, 3 * shape.out), jnp.bfloat16),
            pltpu.VMEM((29, shape.out, shape.width), jnp.bfloat16),
            pltpu.VMEM((shape.pixels, shape.width), jnp.float32),
            pltpu.SemaphoreType.DMA((nr,)),
            pltpu.SemaphoreType.DMA((29,)),
        ],
        compiler_params=PARAMS,
        cost_estimate=pl.CostEstimate(
            flops=44 * shape.pixels * shape.width * shape.out, bytes_accessed=2**24, transcendentals=0
        ),
        name="input_gradient",
    )(info, area, *deltas, pool_delta, mask, *weights)


def weight_gradients(shape, info, bands, far_bands, deltas, far_deltas, pool_deltas, pooled):
    nr, columns, half = shape.nr, shape.columns, shape.out // 2
    n_outs = 8 if shape.pieces else 1
    flat_far = [cut for cuts in far_bands for cut in cuts]
    n_far = len(flat_far)

    def kernel(info, *refs):
        ins, delta_ins, far_delta_ins = (refs[n * nr : (n + 1) * nr] for n in range(3))
        refs = refs[3 * nr :]
        far_flat, refs = refs[:n_far], refs[n_far:]
        flat = iter(far_flat)
        far_ins = [[next(flat) for _ in cuts] for cuts in far_bands]
        pool_deltas, pooled, outs = refs[0], refs[1], refs[2 : 2 + n_outs]
        x, far_x, delta, far_delta, moved, far_moved, sem = refs[2 + n_outs :]
        m, c, zh, part, z = info[0], info[1], info[2], info[4], info[5]
        start_bands(shape, delta_ins, delta, sem.at[0], part)
        start_bands(shape, ins, x, sem.at[1], z)
        start_bands(shape, far_delta_ins, far_delta, sem.at[2], part)
        start_cuts(shape, far_ins, far_x, sem.at[3], z)
        for n, target in enumerate((delta, x, far_delta, far_x)):
            for k in range(nr):
                some = target.at[pl.ds(k * shape.band, shape.band)]
                pltpu.make_async_copy(some, some, sem.at[n, k]).wait()

        def put(tap, value):
            value = value.astype(jnp.bfloat16)
            if not shape.pieces:
                outs[0][tap] = value
                return
            for i in range(4):
                if tap < 27:
                    v = 4 * tap + i
                    chip, slot = v // PER_CHIP, chip_slot(v % PER_CHIP, c)
                else:
                    chip, slot = i, FULL + tap - 27
                for rel in range(4):

                    @pl.when((m ^ rel) == chip)
                    def _():
                        for q in range(2):
                            rows = slice(q * shape.quarter, (q + 1) * shape.quarter)
                            outs[2 * rel + q][slot] = value[rows, i * LANES : (i + 1) * LANES]

        for branch in range(3):
            dilation = dilations[branch]
            move = dilation * columns
            moved_columns(shape, delta, (branch + 1) * shape.out + zh * half, half, branch, moved)
            moved_columns(shape, far_delta, (branch + 1) * half, half, branch, far_moved)
            for r in range(3):
                to = slice(max(0, 1 - r) * move, shape.pixels - max(0, r - 1) * move)
                of = slice(max(0, r - 1) * move, shape.pixels - max(0, 1 - r) * move)
                value = dot(moved[to, :], x[of, :], TN) + dot(far_moved[to, :], far_x[of, :], TN)
                for s in range(3):
                    put(9 * branch + 3 * r + s, value[s * half : (s + 1) * half])
        own = delta[:, lanes_at(zh * half, half)]
        put(27, dot(own, x[...], TN) + dot(far_delta[:, :half], far_x[...], TN))
        put(28, dot(pool_deltas[...], pooled[...], TN))

    if shape.pieces:
        out_shape = [jax.ShapeDtypeStruct((SLOTS, shape.quarter, LANES), jnp.bfloat16)] * 8
    else:
        out_shape = [jax.ShapeDtypeStruct((29, half, shape.width), jnp.bfloat16)]
    return pl.pallas_call(
        kernel,
        out_shape=out_shape,
        in_specs=[SMEM] + [ANY] * (3 * nr + n_far) + [VMEM] * 2,
        out_specs=[VMEM] * n_outs,
        scratch_shapes=[
            pltpu.VMEM((shape.pixels, shape.width), jnp.bfloat16),
            pltpu.VMEM((shape.pixels, shape.width), jnp.bfloat16),
            pltpu.VMEM((shape.pixels, 4 * shape.out), jnp.bfloat16),
            pltpu.VMEM((shape.pixels, 2 * shape.out), jnp.bfloat16),
            pltpu.VMEM((shape.pixels, 3 * half), jnp.bfloat16),
            pltpu.VMEM((shape.pixels, 3 * half), jnp.bfloat16),
            pltpu.SemaphoreType.DMA((4, nr)),
        ],
        compiler_params=PARAMS,
        cost_estimate=pl.CostEstimate(
            flops=44 * shape.pixels * shape.width * shape.out, bytes_accessed=2**24, transcendentals=0
        ),
        name="weight_gradients",
    )(info, *bands, *deltas, *far_deltas, *flat_far, pool_deltas, pooled)


def valid_pixels(extent, first_row, rows, columns):
    r = first_row + lax.broadcasted_iota(jnp.int32, (rows, columns), 0)
    w = lax.broadcasted_iota(jnp.int32, (rows, columns), 1)
    return ((r < extent[0]) & (w < extent[1])).astype(jnp.float32).reshape(rows * columns, 1)


def to_logical(place, x):
    return jnp.where(place.zh == place.c, x, place.swap(x, c=1, zh=1))


def on_device(
    features, extent, pointwise_weight, pooling_weight, dilated_weight, projection_weight, norm_gain, norm_bias, cotangent
):
    place = Place()
    nr, nzl = place.nr, place.nzl
    _, band_rows, columns, channels = features.shape
    width, out = channels // nr, norm_gain.shape[1]
    band = band_rows * columns
    pieces = nr == 4 and place.nd == 8 and dilated_weight.shape[0] == 2 * PER_CHIP * LANES
    shape = Shape(band_rows, columns, nr, width, out, pieces)
    images = place.nd

    partner = place.swap(extent, c=1)
    extent_here = jnp.where(place.zh == place.c, extent, partner)[0]
    area = (extent_here[0] * extent_here[1]).astype(jnp.float32)
    mask = valid_pixels(extent_here, place.part * band_rows, band_rows, columns)
    own_mask = valid_pixels(extent[0], place.z * band_rows, band_rows, columns)
    info = jnp.stack([place.m, place.c, place.zh, place.zl, place.part, place.z]).astype(jnp.int32)
    areas = area.reshape(1)

    if pieces:
        sources = line_pieces(place, dilated_weight, pointwise_weight, pooling_weight)
        crossed = place.swap(sources[0], zh=1)
        neighbour = after(place.swap(sources[1], zl=1), crossed)
        near = packed_half(shape, place.zl, [sources[0], neighbour])
        features, near = after((features, near), near)
    own_parts, other_parts = split_features(shape, features.reshape(band, channels), own_mask, place.c)
    held = by_xor([own_parts, place.swap(other_parts, c=1)], place.c)
    held = [by_xor([v[q] for q in range(nzl)], place.zl) for v in by_xor(held, place.zh)]
    line = [divmod(k, nzl) for k in range(nr)]

    def sent(image, k, some=slice(None), first=()):
        kh, kl = divmod(k, nzl)
        v = held[kh ^ image][kl][some]
        return place.swap(after(v, first), zh=kh, zl=kl) if k else v

    middle = band // 32 * 16
    cuts = [slice(0, middle), slice(middle, band)]
    steps = doubling(place)
    nd_bits = (place.nd // 2).bit_length() - 1
    projection = projection_weight.T
    if pieces:
        neighbour = place.swap(neighbour, zh=1)
        near_x, near_y = plane_direct(place, near)
        bands = [sent(0, k) for k in range(nzl)]
        projection = joined(place, projection, steps[0])
        far = packed_half(shape, place.zl, [crossed, after(neighbour, near_x, near_y, bands, projection)])
        near_d = plane_diagonal(place, near_x, near_y)
        bands.append(sent(0, nzl, first=neighbour))
        far_x, far_y = plane_direct(place, far)
        near = assembled_weights(shape, info, near, near_x, near_y, near_d)
        far_d = plane_diagonal(place, after(far_x, bands, near), far_y)
        bands.append(sent(0, nzl + 1, first=bands))
        weights = [near, assembled_weights(shape, info, far, far_x, far_y, far_d)]
    else:
        projection = joined(place, projection, steps[0])
        bands = [sent(0, k) for k in range(nr)]
        weights = gathered_tiles(place, dilated_weight, pointwise_weight, pooling_weight)
        weights = by_xor([weights[:, : out // 2], weights[:, out // 2 :]], place.zh)

    def reduce(keep, got):
        half = keep + got.astype(jnp.float32)
        rows = half.reshape(nzl, band, half.shape[1])
        mine = lax.dynamic_index_in_dim(rows, place.zl, 0, keepdims=False)
        for k in range(1, nzl):
            other = lax.dynamic_index_in_dim(rows, place.zl ^ k, 0, keepdims=False).astype(jnp.bfloat16)
            mine = mine + place.swap(other, zl=k).astype(jnp.float32)
        return mine

    whole_mask = after(valid_pixels(extent_here, 0, shape.rows, columns), bands)
    ready = (bands, weights)
    keep, given = far_sums(shape, info, bands, weights)
    far_bands = [[sent(1, k, first=ready)] for k in range(nzl)] + [[sent(1, nzl, cuts[0], ready)]]
    for step in steps[1:-nd_bits]:
        projection = joined(place, after(projection, ready), step)
    got = place.swap(after(given, far_bands), c=1)
    wide = reduce(keep, got)
    upstream_low = to_logical(place, after(cotangent.reshape(band, out), got))
    keep, given, pooled, lifted = near_sums(shape, info, areas, after(bands, got, projection, whole_mask), weights)
    for step in steps[-nd_bits:-1]:
        projection = joined(place, after(projection, got), step)
    got = place.swap(after(given, projection, upstream_low), c=1)
    projection = joined(place, after(projection, got), steps[-1])
    far_bands += [[sent(1, k, cuts[0], got)] for k in range(nzl + 1, nr)]
    narrow = after(reduce(keep, got), projection, far_bands)
    projection = projection.reshape((place.nd, nr) + projection_weight.shape[::-1])
    projection = jnp.transpose(projection, (1, 2, 0, 3)).reshape(out, -1)
    z = [narrow[:, out:], narrow[:, :out], wide[:, out:], wide[:, :out]]

    local_count = jnp.sum(mask)
    stats = [local_moments(v, mask, local_count) for v in z]
    table = (lax.broadcasted_iota(jnp.int32, (images, 1), 0) == place.image).astype(jnp.float32) * lifted[0:1]
    average, spread, count, pool_pre = moments(
        place,
        jnp.concatenate([s for s, _ in stats], axis=0),
        jnp.concatenate([q for _, q in stats], axis=0),
        local_count,
        table,
    )
    inv_std = lax.rsqrt(spread + epsilon)
    normed = [(z[k] - average[k : k + 1]) * inv_std[k : k + 1] for k in range(4)]
    pre_act = [norm_gain[k : k + 1] * normed[k] + norm_bias[k : k + 1] for k in range(4)]

    pool_average = jnp.mean(pool_pre, axis=0, keepdims=True)
    pool_centred = pool_pre - pool_average
    pool_inv = lax.rsqrt(jnp.mean(pool_centred * pool_centred, axis=0, keepdims=True) + epsilon)
    pool_normed = pool_centred * pool_inv
    pool_lift = norm_gain[4:5] * pool_normed + norm_bias[4:5]
    here = lambda rows: lax.dynamic_slice_in_dim(rows, place.image, 1, axis=0)
    pool_act = here(jax.nn.silu(pool_lift))

    concat = jnp.concatenate([jax.nn.silu(u) * mask for u in pre_act] + [pool_act * mask], axis=1).astype(jnp.bfloat16)
    pooled_far = place.swap(pooled, zh=1)
    proj_pre = dot(concat, projection, NT)
    proj_sums, proj_squares = local_moments(proj_pre, mask, local_count)
    proj_average, proj_spread, _, _ = moments(place, proj_sums, proj_squares, local_count)
    proj_inv = lax.rsqrt(proj_spread + epsilon)
    proj_normed = (proj_pre - proj_average) * proj_inv
    proj_lift = norm_gain[5:6] * proj_normed + norm_bias[5:6]
    output = to_logical(place, (jax.nn.silu(proj_lift) * mask).astype(jnp.bfloat16))

    upstream = upstream_low.astype(jnp.float32) * mask * silu_slope(proj_lift)
    sums = jnp.concatenate(
        [jnp.sum(upstream * proj_normed, axis=0, keepdims=True), jnp.sum(upstream, axis=0, keepdims=True)], axis=0
    )
    proj_totals = total(place, sums)
    proj_gain_grad, proj_bias_grad = proj_totals[0:1], proj_totals[1:2]
    gain = norm_gain[5:6]
    proj_delta = (
        mask
        * proj_inv
        * (gain * upstream - gain * proj_bias_grad / count - proj_normed * gain * proj_gain_grad / count)
    ).astype(jnp.bfloat16)
    concat_grad = dot(proj_delta, projection, NN)
    projection_partial = lambda first: dot(after(proj_delta, first), concat, TN)
    branch_up = [
        concat_grad[:, k * out : (k + 1) * out] * mask * silu_slope(pre_act[k]) for k in range(4)
    ]
    pool_part = jnp.sum(concat_grad[:, 4 * out :] * mask, axis=0, keepdims=True)
    table = (lax.broadcasted_iota(jnp.int32, (images, 1), 0) == place.image).astype(jnp.float32) * pool_part
    totals = total(
        place,
        after(jnp.concatenate(
            [jnp.sum(branch_up[k] * normed[k], axis=0, keepdims=True) for k in range(4)]
            + [jnp.sum(branch_up[k], axis=0, keepdims=True) for k in range(4)]
            + [table],
            axis=0,
        ), output, pooled_far),
    )
    branch_gain_grad, branch_bias_grad = totals[:4], totals[4:8]
    pool_up = totals[8:] * silu_slope(pool_lift)
    pool_gain_grad = jnp.sum(pool_up * pool_normed, axis=0, keepdims=True)
    pool_bias_grad = jnp.sum(pool_up, axis=0, keepdims=True)
    pool_deltas = pool_inv * (
        norm_gain[4:5] * pool_up
        - norm_gain[4:5] * pool_bias_grad / images
        - pool_normed * norm_gain[4:5] * pool_gain_grad / images
    )
    low_rows = lambda rows: jnp.pad(rows, ((0, 16 - rows.shape[0]), (0, 0))).astype(jnp.bfloat16)
    pool_pair = lax.dynamic_slice_in_dim(pool_deltas, 2 * place.m, 2, axis=0)
    halves = lambda v, n: by_xor([v[:, n * out : n * out + out // 2], v[:, n * out + out // 2 : (n + 1) * out]], place.zh)
    deltas = []
    for k in range(4):
        gain = norm_gain[k : k + 1]
        deltas.append(
            mask
            * inv_std[k : k + 1]
            * (
                gain * branch_up[k]
                - gain * branch_bias_grad[k : k + 1] / count
                - normed[k] * gain * branch_gain_grad[k : k + 1] / count
            )
        )
    delta = jnp.concatenate(deltas, axis=1).astype(jnp.bfloat16)
    crossing = jnp.concatenate([halves(delta, k)[1] for k in range(4)], axis=1)

    def over_group(v, first):
        near = [v] + [after(place.swap(v, zl=k), first) for k in range(1, nzl)]
        return near + [place.swap(n, c=1) for n in near]

    crossing = place.swap(crossing, zh=1)
    spread_deltas = over_group(delta, crossing)
    far_deltas = [crossing] + [place.swap(crossing, zl=k) for k in range(1, nzl)]
    inputs = input_gradient(shape, info, areas, spread_deltas, low_rows(here(pool_deltas)), whole_mask, weights)

    for k in range(nzl, nr):
        far_bands[k].append(sent(1, k, cuts[1], spread_deltas))
    rows = projection_weight.shape[0]
    part = projection_partial(spread_deltas).astype(jnp.bfloat16).reshape(nr, out // nr, images * rows)
    mine = by_xor([part[k] for k in range(nr)], place.z)
    part = add_low(mine[0], *[place.swap(mine[k], zh=k // nzl, zl=k % nzl) for k in range(1, nr)])
    crossing = after(far_deltas, inputs, part, far_bands)
    part = jnp.transpose(part.reshape(out // nr, images, rows), (1, 0, 2)).reshape(-1, 2, out // nr, rows)
    part = halved(place, [part[:, k] for k in range(2)], steps[-nd_bits - 1])

    pooled_pair = pooled + jnp.roll(pooled_far, 1, axis=0)
    pool_pair = jnp.concatenate([pool_pair[i : i + 1] for i in range(2)], axis=0)
    pool_pair = jnp.concatenate(by_xor([pool_pair[0:1], pool_pair[1:2]], place.zh), axis=0)
    pool_pair = halves(low_rows(pool_pair), 0)[0]
    far_deltas = crossing + [place.swap(n, c=1) for n in crossing]
    grads = weight_gradients(shape, info, bands, far_bands, spread_deltas, far_deltas, pool_pair, pooled_pair)

    returned = [place.swap(inputs[k], zh=kh, zl=kl) if k else inputs[0] for k, (kh, kl) in enumerate(line)]
    returned = by_xor(by_xor([returned[:nzl], returned[nzl:]], place.zh), place.c)
    traded = place.swap(jnp.stack(returned[1]), c=1)
    feature_gradient = join_features(shape, returned[0], [traded[k] for k in range(nzl)], place.c, place.zl)

    if pieces:
        pairs = [[grads[2 * rel], grads[2 * rel + 1]] for rel in range(4)]
        quarters = plane_scatter(place, pairs)
        dilated_gradient, pointwise_gradient, pooling_gradient = line_back(place, quarters)
    else:
        dilated_gradient, pointwise_gradient, pooling_gradient = scattered_tiles(place, grads[0])

    if pieces:
        part = after(part, quarters)
    for step in steps[-nd_bits:]:
        part = part.reshape(-1, 2, out // nr, rows)
        part = halved(place, [part[:, k] for k in range(2)], step)
    projection_gradient = part.reshape(out // nr, rows).astype(jnp.float32).T

    return (
        output.reshape(cotangent.shape),
        feature_gradient.reshape(features.shape),
        pointwise_gradient,
        pooling_gradient,
        dilated_gradient,
        projection_gradient,
        jnp.concatenate([branch_gain_grad, pool_gain_grad, proj_gain_grad], axis=0),
        jnp.concatenate([branch_bias_grad, pool_bias_grad, proj_bias_grad], axis=0),
    )


def solution(mesh):
    banded = P("dp", "rows", None, None)
    blocks = P("dp", "rows")
    return jax.shard_map(
        on_device,
        mesh=mesh,
        in_specs=(banded, P("dp", None), blocks, blocks, blocks, blocks, P(), P(), banded),
        out_specs=(banded, banded, blocks, blocks, blocks, blocks, P(), P()),
        check_vma=False,
    )
```

time: 494 us -> 452 us (0.915)
  the two profiles are of different devices: /device:TPU:9 before, /device:TPU:0 now
where the time goes in v2:
time: 452 us; the launch traced here: 443 us
  waiting for transfers between devices  190 us (42%)
  starting transfers between devices  93.9 us (21%)
  Pallas kernels  88.6 us (20%)
  other arithmetic  38.6 us (9%)
  local copies, waits for them, and re-layouts  26.5 us (6%)
  between operations  4.82 us (1%)
    ppermute x85, waiting for transfers between devices, swap(): return lax.ppermute(x, AXES, pairs)  190 us
    ppermute x85, starting transfers between devices, swap(): return lax.ppermute(x, AXES, pairs)  93.9 us
    pallas_call x1, Pallas kernels, weight_gradients(): pl.pallas_call(kernel, out_shape=out_shape, in_specs=[SMEM] + [ANY] * (3...  22.9 us
    pallas_call x1, Pallas kernels, input_gradient(): pl.pallas_call(kernel, out_shape=[jax.ShapeDtypeStruct((shape.band, shape...  17.9 us
    pallas_call x1, Pallas kernels, far_sums(): pl.pallas_call(kernel, out_shape=half_shapes(shape, 2), in_specs=[SMEM] +...  14.1 us
    pallas_call x1, Pallas kernels, near_sums(): pl.pallas_call(kernel, out_shape=half_shapes(shape, 2) + [jax.ShapeDtypeS...  11.9 us
    pallas_call x2, Pallas kernels, assembled_weights(): pl.pallas_call(kernel, out_shape=jax.ShapeDtypeStruct((29, shape.out // 2...  10.9 us
  transfers between devices with their start and end apart: 85, of which 43 were waited for; matrix products, arithmetic and copies ran while one was open for 10% of the time, Pallas kernels for 13%

profile of v2, /device:TPU:0, one launch (start us, length us, event | category | flops | bytes accessed | tf_op | source)
XLA Modules:
  0.0 443.5 jit_solution(156173131154346250)
XLA Ops:
  4.2 4.0 collective-permute-start.3
  8.3 1.6 collective-permute-start.2
  12.7 17.1 %collective-permute-done.3.refs_0_ = bf16[29,64,128]{2,1,0:T(8,128)(2,1)S(1)} collective-permute-done((bf16[29,64,128]{2,1,0:T(8,128)(2,1)S(1)}, bf16[29,64,128]{2,1,0:T(8,128)(2,1)S(1)}, u32[]{:S(2)}, u32[]{:S(2)}) %collective-permute-start.3) | collective-permute-done | bytes 475168 | tf_op jit(solution)/shard_map/ppermute | solution.py:51
  30.5 2.2 packed_half.2.refs_0_
  32.7 3.3 split_features.1
  35.9 1.6 collective-permute-start.10
  41.3 3.2 collective-permute-start.5
  45.1 19.4 %collective-permute-done.13 = bf16[64,160]{1,0:T(8,128)(2,1)S(1)} collective-permute-done((bf16[64,160]{1,0:T(8,128)(2,1)S(1)}, bf16[64,160]{1,0:T(8,128)(2,1)S(1)}, u32[]{:S(2)}, u32[]{:S(2)}) %collective-permute-start.13) | collective-permute-done | bytes 20512 | tf_op jit(solution)/shard_map/ppermute | solution.py:51
  64.6 2.3 packed_half.3.refs_0_
  67.9 1.9 slice.730
  69.8 1.6 collective-permute-start.11
  71.3 1.8 slice.731
  76.6 22.5 %collective-permute-done.12.refs_4_ = bf16[14,128,128]{2,1,0:T(8,128)(2,1)} collective-permute-done((bf16[14,128,128]{2,1,0:T(8,128)(2,1)}, bf16[14,128,128]{2,1,0:T(8,128)(2,1)}, u32[]{:S(2)}, u32[]{:S(2)}) %collective-permute-start.12) | collective-permute-done | bytes 458784 | tf_op jit(solution)/shard_map/ppermute | solution.py:51
  100.0 5.5 %assembled_weights.2.refs_4_.refs_6_ = bf16[29,128,512]{2,1,0:T(8,128)(2,1)} custom-call(s32[6]{0:T(128)} %stack.125.info, bf16[29,128,128]{2,1,0:T(8,128)(2,1)} %packed_half.2.refs_0_, bf16[29,128,128]{2,1,0:T(8,128)(2,1)} %collective-permute-done.9.refs_1_, bf16[29,128,128]{2,1,0:T(8,128)(2,1)} %collective-permute-done.10.refs_2_, ...), custom_call_target="tpu_custom_call" | custom-call | tf_op jit(solution)/shard_map/assembled_weights/pallas_call | solution.py:355
  107.1 1.6 collective-permute-start.17
  108.8 3.3 collective-permute-start.8
  114.7 4.6 %collective-permute-done.17.refs_4_ = bf16[14,128,128]{2,1,0:T(8,128)(2,1)S(1)} collective-permute-done((bf16[14,128,128]{2,1,0:T(8,128)(2,1)S(1)}, bf16[14,128,128]{2,1,0:T(8,128)(2,1)S(1)}, u32[]{:S(2)}, u32[]{:S(2)}) %collective-permute-start.17) | collective-permute-done | bytes 458784 | tf_op jit(solution)/shard_map/ppermute | solution.py:51
  120.8 5.4 %assembled_weights.3.refs_5_.refs_7_ = bf16[29,128,512]{2,1,0:T(8,128)(2,1)} custom-call(s32[6]{0:T(128)} %stack.125.info, bf16[29,128,128]{2,1,0:T(8,128)(2,1)} %packed_half.3.refs_0_, bf16[29,128,128]{2,1,0:T(8,128)(2,1)} %copy-done.5, bf16[29,128,128]{2,1,0:T(8,128)(2,1)} %collective-permute-done.15.refs_2_, bf16[15,128,128]{2,1,0:T(8,128)(2,1)} %copy-done.15, ...), custom_call_target="tpu_custom_call" | custom-call | tf_op jit(solution)/shard_map/assembled_weights/pallas_call | solution.py:355
  126.3 3.3 collective-permute-start.18
  130.9 1.7 collective-permute-start.21
  132.6 14.1 %far_sums.1 = (f32[864,512]{1,0:T(8,128)}, bf16[864,512]{1,0:T(8,128)(2,1)}) custom-call(s32[6]{0:T(128)} %stack.125.info, bf16[432,512]{1,0:T(8,128)(2,1)} %bitcast.291, bf16[432,512]{1,0:T(8,128)(2,1)} %copy-done.10, bf16[432,512]{1,0:T(8,128)(2,1)} %copy-done.11, bf16[432,512]{1,0:T(8,128)(2,1)} %copy-done.12, ...), custom_call_target="tpu_custom_call" | custom-call | tf_op jit(solution)/shard_map/far_sums/pallas_call | solution.py:446
  151.1 1.8 convert_add_fusion
  153.3 2.0 collective-permute-start.24
  155.3 11.9 %near_sums.1 = (f32[864,512]{1,0:T(8,128)}, bf16[864,512]{1,0:T(8,128)(2,1)}, bf16[16,512]{1,0:T(8,128)(2,1)}, f32[16,256]{1,0:T(8,128)}) custom-call(s32[6]{0:T(128)} %stack.125.info, f32[1]{0:T(128)} %bitcast.10.area, bf16[432,512]{1,0:T(8,128)(2,1)} %bitcast.292, bf16[432,512]{1,0:T(8,128)(2,1)} %copy-done.10, bf16[432,512]{1,0:T(8,128)(2,1)} %copy-done.11, ...), custom_call_target="tpu_custom_call" | custom-call | tf_op jit(solution)/shard_map/near_sums/pallas_call | solution.py:486
  172.7 1.6 collective-permute-start.26
  175.5 10.2 %collective-permute-done.27 = bf16[2,2,2,2,64,160]{5,4,3,2,1,0:T(8,128)(2,1)S(1)} collective-permute-done((bf16[2,2,2,2,64,160]{5,4,3,2,1,0:T(8,128)(2,1)S(1)}, bf16[2,2,2,2,64,160]{5,4,3,2,1,0:T(8,128)(2,1)S(1)}, u32[]{:S(2)}, u32[]{:S(2)}) %collective-permute-start.27) | collective-permute-done | bytes 327712 | tf_op jit(solution)/shard_map/ppermute | solution.py:51
  186.2 4.0 collective-permute-done.28.refs_16_
  200.6 2.2 collective-permute-done.33
  204.5 3.2 collective-permute-start.35
  210.5 1.6 copy.79
  212.1 2.4 reshape.318
  223.3 2.2 collective-permute-start.40
  226.2 1.6 collective-permute-done.40
  228.0 3.2 collective-permute-start.42
  232.7 3.8 collective-permute-done.43
  244.0 2.2 collective-permute-done.48
  246.3 1.7 collective-permute-start.50
  248.0 2.6 collective-permute-start.51
  250.8 2.6 collective-permute-done.51
  257.7 5.7 %collective-permute-done.44 = bf16[432,256]{1,0:T(8,128)(2,1)S(1)} collective-permute-done((bf16[432,256]{1,0:T(8,128)(2,1)}, bf16[432,256]{1,0:T(8,128)(2,1)S(1)}, u32[]{:S(2)}, u32[]{:S(2)}) %collective-permute-start.44) | collective-permute-done | bytes 221216 | tf_op jit(solution)/shard_map/ppermute | solution.py:51
  263.4 1.6 broadcast_select_fusion.18
  267.5 2.2 collective-permute-start.56
  270.5 1.6 collective-permute-done.56
  272.2 2.6 collective-permute-start.58
  274.9 1.7 collective-permute-start.59
  276.9 3.5 collective-permute-done.59
  283.6 2.4 collective-permute-start.61
  285.9 23.4 %collective-permute-done.61.refs_8_ = bf16[432,512]{1,0:T(8,128)(2,1)S(1)} collective-permute-done((bf16[432,512]{1,0:T(8,128)(2,1)S(1)}, bf16[432,512]{1,0:T(8,128)(2,1)S(1)}, u32[]{:S(2)}, u32[]{:S(2)}) %collective-permute-start.61) | collective-permute-done | bytes 442400 | tf_op jit(solution)/shard_map/ppermute | solution.py:51
  316.4 1.9 collective-permute-start.70
  318.3 1.7 collective-permute-start.71
  319.9 2.2 collective-permute-start.73
  322.1 17.9 %input_gradient.1 = (bf16[432,512]{1,0:T(8,128)(2,1)}, bf16[432,512]{1,0:T(8,128)(2,1)}, bf16[432,512]{1,0:T(8,128)(2,1)}, bf16[432,512]{1,0:T(8,128)(2,1)}) custom-call(s32[6]{0:T(128)} %stack.125.info, f32[1]{0:T(128)} %bitcast.10.area, bf16[432,1024]{1,0:T(8,128)(2,1)} %pad_maximum_fusion.4.refs_0_.refs_4_, ...), custom_call_target="tpu_custom_call" | custom-call | flops 9965666304 | bytes 16777216 | tf_op jit(solution)/shard_map/input_gradient/pallas_call | solution.py:543
  340.3 3.4 collective-permute-done.73.refs_17_
  343.7 9.9 %collective-permute-done.72.refs_15_ = bf16[224,512]{1,0:T(8,128)(2,1)S(1)} collective-permute-done((bf16[224,512]{1,0:T(8,128)(2,1)S(1)}, bf16[224,512]{1,0:T(8,128)(2,1)S(1)}, u32[]{:S(2)}, u32[]{:S(2)}) %collective-permute-start.72) | collective-permute-done | bytes 229408 | tf_op jit(solution)/shard_map/ppermute | solution.py:51
  357.0 22.9 %weight_gradients.1 = (bf16[29,64,128]{2,1,0:T(8,128)(2,1)}, bf16[29,64,128]{2,1,0:T(8,128)(2,1)}, bf16[29,64,128]{2,1,0:T(8,128)(2,1)}, bf16[29,64,128]{2,1,0:T...) custom-call(s32[6]{0:T(128)} %stack.125.info, ...), custom_call_target="tpu_custom_call" | custom-call | flops 9965666304 | bytes 16777216 | tf_op jit(solution)/shard_map/weight_gradients/pallas_call | solution.py:626
  383.8 9.2 %collective-permute-done.76 = bf16[29,64,128]{2,1,0:T(8,128)(2,1)S(1)} collective-permute-done((bf16[29,64,128]{2,1,0:T(8,128)(2,1)}, bf16[29,64,128]{2,1,0:T(8,128)(2,1)S(1)}, u32[]{:S(2)}, u32[]{:S(2)}) %collective-permute-start.76) | collective-permute-done | bytes 475168 | tf_op jit(solution)/shard_map/ppermute | solution.py:51
  397.6 2.2 collective-permute-start.65
  399.7 1.8 collective-permute-start.66
  401.6 1.9 collective-permute-done.64
  404.4 17.9 %collective-permute-done.65 = bf16[432,512]{1,0:T(8,128)(2,1)S(1)} collective-permute-done((bf16[432,512]{1,0:T(8,128)(2,1)S(1)}, bf16[432,512]{1,0:T(8,128)(2,1)S(1)}, u32[]{:S(2)}, u32[]{:S(2)}) %collective-permute-start.65) | collective-permute-done | bytes 442400 | tf_op jit(solution)/shard_map/ppermute | solution.py:51
  424.1 1.6 collective-permute-start.83
  426.9 1.8 collective-permute-done.83
  430.5 3.1 join_features.1
  434.3 5.0 %collective-permute-done.80 = bf16[29,64,128]{2,1,0:T(8,128)(2,1)S(1)} collective-permute-done((bf16[29,64,128]{2,1,0:T(8,128)(2,1)S(1)}, bf16[29,64,128]{2,1,0:T(8,128)(2,1)S(1)}, u32[]{:S(2)}, u32[]{:S(2)}) %collective-permute-start.80) | collective-permute-done | bytes 475168 | tf_op jit(solution)/shard_map/ppermute | solution.py:51
  (453 shorter events, 106.8 us)
Async XLA Ops:
  4.2 25.5 %collective-permute-start.3 = (bf16[29,64,128]{2,1,0:T(8,128)(2,1)S(1)}, bf16[29,64,128]{2,1,0:T(8,128)(2,1)S(1)}, u32[]{:S(2)}, u32[]{:S(2)}) collective-permute-start(bf16[29,64,128]{2,1,0:T(8,128)(2,1)S(1)} %get-tuple-element.151.refs_0_), channel_id=1, source_target_pairs={{0,2},{1,3},{2,0},{3,1},{4,6},{5,7},{6,4},{7,5},{8,10},{9,11},{10,... | collective-permute-start | bytes 1425416 | tf_op jit(solution)/shard_map/ppermute | solution.py:51
  8.3 21.8 %collective-permute-start.2 = (bf16[29,64,128]{2,1,0:T(8,128)(2,1)S(1)}, bf16[29,64,128]{2,1,0:T(8,128)(2,1)}, u32[]{:S(2)}, u32[]{:S(2)}) collective-permute-start(bf16[29,64,128]{2,1,0:T(8,128)(2,1)S(1)} %get-tuple-element.150), channel_id=1, source_target_pairs={{0,1},{1,0},{2,3},{3,2},{4,5},{5,4},{6,7},{7,6},{8,9},{9,8},{10,11... | collective-permute-start | bytes 1425416 | tf_op jit(solution)/shard_map/ppermute | solution.py:51
  35.9 28.6 %collective-permute-start.10 = (bf16[29,128,128]{2,1,0:T(8,128)(2,1)S(1)}, bf16[29,128,128]{2,1,0:T(8,128)(2,1)}, u32[]{:S(2)}, u32[]{:S(2)}) collective-permute-start(bf16[29,128,128]{2,1,0:T(8,128)(2,1)S(1)} %copy-done.4), channel_id=1, source_target_pairs={{0,16},{1,17},{2,18},{3,19},{4,20},{5,21},{6,22},{7,23},{8,24},{9,... | collective-permute-start | bytes 2850824 | tf_op jit(solution)/shard_map/ppermute | solution.py:51
  37.5 27.0 %collective-permute-start.9 = (bf16[29,128,128]{2,1,0:T(8,128)(2,1)S(1)}, bf16[29,128,128]{2,1,0:T(8,128)(2,1)}, u32[]{:S(2)}, u32[]{:S(2)}) collective-permute-start(bf16[29,128,128]{2,1,0:T(8,128)(2,1)S(1)} %copy-done.4), channel_id=1, source_target_pairs={{0,8},{1,9},{2,10},{3,11},{4,12},{5,13},{6,14},{7,15},{8,0},{9,1},... | collective-permute-start | bytes 2850824 | tf_op jit(solution)/shard_map/ppermute | solution.py:51
  39.0 25.5 %collective-permute-start.6 = (bf16[29,64,128]{2,1,0:T(8,128)(2,1)}, bf16[29,64,128]{2,1,0:T(8,128)(2,1)}, u32[]{:S(2)}, u32[]{:S(2)}) collective-permute-start(bf16[29,64,128]{2,1,0:T(8,128)(2,1)} %collective-permute-done.2.refs_1_), channel_id=1, source_target_pairs={{0,2},{1,3},{2,0},{3,1},{4,6},{5,7},{6,4},{7,5},{8,10},{9,11},{10,... | collective-permute-start | bytes 1425416 | tf_op jit(solution)/shard_map/ppermute | solution.py:51
  41.3 23.3 %collective-permute-start.5 = (bf16[432,512]{1,0:T(8,128)(2,1)S(1)}, bf16[432,512]{1,0:T(8,128)(2,1)S(1)}, u32[]{:S(2)}, u32[]{:S(2)}) collective-permute-start(bf16[432,512]{1,0:T(8,128)(2,1)S(1)} %bitcast.305), channel_id=1, source_target_pairs={{0,1},{1,0},{2,3},{3,2},{4,5},{5,4},{6,7},{7,6},{8,9},{9,8},{10,11... | collective-permute-start | bytes 1327112 | tf_op jit(solution)/shard_map/ppermute | solution.py:51
  44.5 20.0 %collective-permute-start.13 = (bf16[64,160]{1,0:T(8,128)(2,1)S(1)}, bf16[64,160]{1,0:T(8,128)(2,1)S(1)}, u32[]{:S(2)}, u32[]{:S(2)}) collective-permute-start(bf16[64,160]{1,0:T(8,128)(2,1)S(1)} %bitcast.313), channel_id=1, source_target_pairs={{0,1},{1,0},{2,3},{3,2},{4,5},{5,4},{6,7},{7,6},{8,9},{9,8},{10,11... | collective-permute-start | bytes 61448 | tf_op jit(solution)/shard_map/ppermute | solution.py:51
  66.9 38.6 %collective-permute-start.14 = (bf16[29,128,128]{2,1,0:T(8,128)(2,1)}, bf16[29,128,128]{2,1,0:T(8,128)(2,1)S(1)}, u32[]{:S(2)}, u32[]{:S(2)}) collective-permute-start(bf16[29,128,128]{2,1,0:T(8,128)(2,1)} %packed_half.3.refs_0_), channel_id=1, source_target_pairs={{0,8},{1,9},{2,10},{3,11},{4,12},{5,13},{6,14},{7,15},{8,0},{9,1},... | collective-permute-start | bytes 2850824 | tf_op jit(solution)/shard_map/ppermute | solution.py:51
  67.4 38.7 %collective-permute-start.15 = (bf16[29,128,128]{2,1,0:T(8,128)(2,1)}, bf16[29,128,128]{2,1,0:T(8,128)(2,1)}, u32[]{:S(2)}, u32[]{:S(2)}) collective-permute-start(bf16[29,128,128]{2,1,0:T(8,128)(2,1)} %packed_half.3.refs_0_), channel_id=1, source_target_pairs={{0,16},{1,17},{2,18},{3,19},{4,20},{5,21},{6,22},{7,23},{8,24},{9,... | collective-permute-start | bytes 2850824 | tf_op jit(solution)/shard_map/ppermute | solution.py:51
  69.8 30.2 %collective-permute-start.11 = (bf16[15,128,128]{2,1,0:T(8,128)(2,1)}, bf16[15,128,128]{2,1,0:T(8,128)(2,1)}, u32[]{:S(2)}, u32[]{:S(2)}) collective-permute-start(bf16[15,128,128]{2,1,0:T(8,128)(2,1)} %slice.730), channel_id=1, source_target_pairs={{0,16},{1,17},{2,18},{3,19},{4,20},{5,21},{6,22},{7,23},{8,24},{9,... | collective-permute-start | bytes 1474568 | tf_op jit(solution)/shard_map/ppermute | solution.py:51
  73.2 25.9 %collective-permute-start.12 = (bf16[14,128,128]{2,1,0:T(8,128)(2,1)}, bf16[14,128,128]{2,1,0:T(8,128)(2,1)}, u32[]{:S(2)}, u32[]{:S(2)}) collective-permute-start(bf16[14,128,128]{2,1,0:T(8,128)(2,1)} %slice.731), channel_id=1, source_target_pairs={{0,8},{1,9},{2,10},{3,11},{4,12},{5,13},{6,14},{7,15},{8,0},{9,1},... | collective-permute-start | bytes 1376264 | tf_op jit(solution)/shard_map/ppermute | solution.py:51
  75.6 29.8 %collective-permute-start.7 = (bf16[432,512]{1,0:T(8,128)(2,1)}, bf16[432,512]{1,0:T(8,128)(2,1)S(1)}, u32[]{:S(2)}, u32[]{:S(2)}) collective-permute-start(bf16[432,512]{1,0:T(8,128)(2,1)} %get-tuple-element.63.refs_12_), channel_id=1, source_target_pairs={{0,2},{1,3},{2,0},{3,1},{4,6},{5,7},{6,4},{7,5},{8,10},{9,11},{10,... | collective-permute-start | bytes 1327112 | tf_op jit(solution)/shard_map/ppermute | solution.py:51
  99.0 9.7 %collective-permute-start = (s32[1,2]{1,0:T(1,128)S(1)}, s32[1,2]{1,0:T(1,128)S(1)}, u32[]{:S(2)}, u32[]{:S(2)}) collective-permute-start(s32[1,2]{1,0:T(1,128)S(1)} %copy-done.54), channel_id=1, source_target_pairs={{0,4},{1,5},{2,6},{3,7},{4,0},{5,1},{6,2},{7,3},{8,12},{9,13},{10,... | collective-permute-start | bytes 32 | tf_op jit(solution)/shard_map/ppermute | solution.py:51
  105.6 13.6 %collective-permute-start.16 = (bf16[15,128,128]{2,1,0:T(8,128)(2,1)S(1)}, bf16[15,128,128]{2,1,0:T(8,128)(2,1)S(1)}, u32[]{:S(2)}, u32[]{:S(2)}) collective-permute-start(bf16[15,128,128]{2,1,0:T(8,128)(2,1)S(1)} %slice.579), channel_id=1, source_target_pairs={{0,16},{1,17},{2,18},{3,19},{4,20},{5,21},{6,22},{7,23},{8,24},{9,... | collective-permute-start | bytes 1474568 | tf_op jit(solution)/shard_map/ppermute | solution.py:51
  107.1 12.1 %collective-permute-start.17 = (bf16[14,128,128]{2,1,0:T(8,128)(2,1)S(1)}, bf16[14,128,128]{2,1,0:T(8,128)(2,1)S(1)}, u32[]{:S(2)}, u32[]{:S(2)}) collective-permute-start(bf16[14,128,128]{2,1,0:T(8,128)(2,1)S(1)} %slice.732), channel_id=1, source_target_pairs={{0,8},{1,9},{2,10},{3,11},{4,12},{5,13},{6,14},{7,15},{8,0},{9,1},... | collective-permute-start | bytes 1376264 | tf_op jit(solution)/shard_map/ppermute | solution.py:51
  108.8 17.5 %collective-permute-start.8 = (bf16[432,512]{1,0:T(8,128)(2,1)S(1)}, bf16[432,512]{1,0:T(8,128)(2,1)S(1)}, u32[]{:S(2)}, u32[]{:S(2)}) collective-permute-start(bf16[432,512]{1,0:T(8,128)(2,1)S(1)} %copy-done.24), channel_id=1, source_target_pairs={{0,3},{1,2},{2,1},{3,0},{4,7},{5,6},{6,5},{7,4},{8,11},{9,10},{10,... | collective-permute-start | bytes 1327112 | tf_op jit(solution)/shard_map/ppermute | solution.py:51
  126.3 20.5 %collective-permute-start.18 = (bf16[432,512]{1,0:T(8,128)(2,1)S(1)}, bf16[432,512]{1,0:T(8,128)(2,1)S(1)}, u32[]{:S(2)}, u32[]{:S(2)}) collective-permute-start(bf16[432,512]{1,0:T(8,128)(2,1)S(1)} %copy-done.24), channel_id=1, source_target_pairs={{0,1},{1,0},{2,3},{3,2},{4,5},{5,4},{6,7},{7,6},{8,9},{9,8},{10,11... | collective-permute-start | bytes 1327112 | tf_op jit(solution)/shard_map/ppermute | solution.py:51
  129.6 17.2 %collective-permute-start.19 = (bf16[208,512]{1,0:T(8,128)(2,1)S(1)}, bf16[208,512]{1,0:T(8,128)(2,1)S(1)}, u32[]{:S(2)}, u32[]{:S(2)}) collective-permute-start(bf16[208,512]{1,0:T(8,128)(2,1)S(1)} %slice_bitcast_fusion.11), channel_id=1, source_target_pairs={{0,2},{1,3},{2,0},{3,1},{4,6},{5,7},{6,4},{7,5},{8,10},{9,11},{10,... | collective-permute-start | bytes 638984 | tf_op jit(solution)/shard_map/ppermute | solution.py:51
  130.9 17.6 %collective-permute-start.21 = (bf16[2,64,160]{2,1,0:T(8,128)(2,1)S(1)}, bf16[2,64,160]{2,1,0:T(8,128)(2,1)S(1)}, u32[]{:S(2)}, u32[]{:S(2)}) collective-permute-start(bf16[2,64,160]{2,1,0:T(8,128)(2,1)S(1)} %pad_maximum_fusion.14), channel_id=1, source_target_pairs={{0,2},{1,3},{2,0},{3,1},{4,6},{5,7},{6,4},{7,5},{8,10},{9,11},{10,... | collective-permute-start | bytes 122888 | tf_op jit(solution)/shard_map/ppermute | solution.py:51
  150.5 16.8 %collective-permute-start.23 = (bf16[2,2,2,64,160]{4,3,2,1,0:T(8,128)(2,1)S(1)}, bf16[2,2,2,64,160]{4,3,2,1,0:T(8,128)(2,1)S(1)}, u32[]{:S(2)}, u32[]{:S(2)}) collective-permute-start(bf16[2,2,2,64,160]{4,3,2,1,0:T(8,128)(2,1)S(1)} %pad_maximum_fusion.12), channel_id=1, source_target_pairs={{0,8},{1,9},{2,10},{3,11},{4,12},{5,13},{6,14},{7,15},{8,0},{9,1},... | collective-permute-start | bytes 491528 | tf_op jit(solution)/shard_map/ppermute | solution.py:51
  153.0 17.3 %collective-permute-start.29 = (bf16[432,512]{1,0:T(8,128)(2,1)S(1)}, bf16[432,512]{1,0:T(8,128)(2,1)S(1)}, u32[]{:S(2)}, u32[]{:S(2)}) collective-permute-start(bf16[432,512]{1,0:T(8,128)(2,1)S(1)} %fusion.5), channel_id=1, source_target_pairs={{0,1},{1,0},{2,3},{3,2},{4,5},{5,4},{6,7},{7,6},{8,9},{9,8},{10,11... | collective-permute-start | bytes 1327112 | tf_op jit(solution)/shard_map/ppermute | solution.py:51
  153.3 14.1 %collective-permute-start.24 = (bf16[432,256]{1,0:T(8,128)(2,1)S(1)}, bf16[432,256]{1,0:T(8,128)(2,1)S(1)}, u32[]{:S(2)}, u32[]{:S(2)}) collective-permute-start(bf16[432,256]{1,0:T(8,128)(2,1)S(1)} %bitcast.310), channel_id=1, source_target_pairs={{0,6},{1,7},{2,4},{3,5},{4,2},{5,3},{6,0},{7,1},{8,14},{9,15},{10,... | collective-permute-start | bytes 663560 | tf_op jit(solution)/shard_map/ppermute | solution.py:51
  171.5 14.2 %collective-permute-start.27 = (bf16[2,2,2,2,64,160]{5,4,3,2,1,0:T(8,128)(2,1)S(1)}, bf16[2,2,2,2,64,160]{5,4,3,2,1,0:T(8,128)(2,1)S(1)}, u32[]{:S(2)}, u32[]{:S(2)}) collective-permute-start(bf16[2,2,2,2,64,160]{5,4,3,2,1,0:T(8,128)(2,1)S(1)} %pad_maximum_fusion.6), channel_id=1, source_target_pairs={{0,16},{1,17},{2,18},{3,19},{4,20},{5,21},{6,22},{7,23},{8,24},{9,... | collective-permute-start | bytes 983048 | tf_op jit(solution)/shard_map/ppermute | solution.py:51
  172.7 13.3 %collective-permute-start.26 = (bf16[432,512]{1,0:T(8,128)(2,1)S(1)}, bf16[432,512]{1,0:T(8,128)(2,1)S(1)}, u32[]{:S(2)}, u32[]{:S(2)}) collective-permute-start(bf16[432,512]{1,0:T(8,128)(2,1)S(1)} %fusion.4), channel_id=1, source_target_pairs={{0,1},{1,0},{2,3},{3,2},{4,5},{5,4},{6,7},{7,6},{8,9},{9,8},{10,11... | collective-permute-start | bytes 1327112 | tf_op jit(solution)/shard_map/ppermute | solution.py:51
  174.3 15.9 %collective-permute-start.28 = (bf16[208,512]{1,0:T(8,128)(2,1)S(1)}, bf16[208,512]{1,0:T(8,128)(2,1)S(1)}, u32[]{:S(2)}, u32[]{:S(2)}) collective-permute-start(bf16[208,512]{1,0:T(8,128)(2,1)S(1)} %slice_bitcast_fusion.10), channel_id=1, source_target_pairs={{0,3},{1,2},{2,1},{3,0},{4,7},{5,6},{6,5},{7,4},{8,11},{9,10},{10,... | collective-permute-start | bytes 638984 | tf_op jit(solution)/shard_map/ppermute | solution.py:51
  198.1 4.7 %collective-permute-start.33 = (f32[17,256]{1,0:T(8,128)S(1)}, f32[17,256]{1,0:T(8,128)S(1)}, u32[]{:S(2)}, u32[]{:S(2)}) collective-permute-start(f32[17,256]{1,0:T(8,128)S(1)} %pad_maximum_fusion.15), channel_id=1, source_target_pairs={{0,24},{1,25},{2,26},{3,27},{4,28},{5,29},{6,30},{7,31},{8,16},{9,... | collective-permute-start | bytes 52232 | tf_op jit(solution)/shard_map/ppermute | solution.py:51
  204.5 10.0 %collective-permute-start.34 = (f32[17,256]{1,0:T(8,128)}, f32[17,256]{1,0:T(8,128)}, u32[]{:S(2)}, u32[]{:S(2)}) collective-permute-start(f32[17,256]{1,0:T(8,128)} %pad_maximum_fusion.16), channel_id=1, source_target_pairs={{0,1},{1,0},{2,3},{3,2},{4,5},{5,4},{6,7},{7,6},{8,9},{9,8},{10,11... | collective-permute-start | bytes 52232 | tf_op jit(solution)/shard_map/ppermute | solution.py:51
  204.5 10.0 %collective-permute-start.35 = (f32[17,256]{1,0:T(8,128)}, f32[17,256]{1,0:T(8,128)}, u32[]{:S(2)}, u32[]{:S(2)}) collective-permute-start(f32[17,256]{1,0:T(8,128)} %pad_maximum_fusion.16), channel_id=1, source_target_pairs={{0,2},{1,3},{2,0},{3,1},{4,6},{5,7},{6,4},{7,5},{8,10},{9,11},{10,... | collective-permute-start | bytes 52232 | tf_op jit(solution)/shard_map/ppermute | solution.py:51
  207.7 6.8 %collective-permute-start.36 = (f32[17,256]{1,0:T(8,128)}, f32[17,256]{1,0:T(8,128)}, u32[]{:S(2)}, u32[]{:S(2)}) collective-permute-start(f32[17,256]{1,0:T(8,128)} %pad_maximum_fusion.16), channel_id=1, source_target_pairs={{0,3},{1,2},{2,1},{3,0},{4,7},{5,6},{6,5},{7,4},{8,11},{9,10},{10,... | collective-permute-start | bytes 52232 | tf_op jit(solution)/shard_map/ppermute | solution.py:51
  223.3 4.5 %collective-permute-start.40 = (f32[3,256]{1,0:T(4,128)S(1)}, f32[3,256]{1,0:T(4,128)S(1)}, u32[]{:S(2)}, u32[]{:S(2)}) collective-permute-start(f32[3,256]{1,0:T(4,128)S(1)} %pad_maximum_fusion.20), channel_id=1, source_target_pairs={{0,24},{1,25},{2,26},{3,27},{4,28},{5,29},{6,30},{7,31},{8,16},{9,... | collective-permute-start | bytes 9224 | tf_op jit(solution)/shard_map/ppermute | solution.py:51
  227.9 4.5 %collective-permute-start.41 = (f32[3,256]{1,0:T(4,128)S(1)}, f32[3,256]{1,0:T(4,128)S(1)}, u32[]{:S(2)}, u32[]{:S(2)}) collective-permute-start(f32[3,256]{1,0:T(4,128)S(1)} %pad_maximum_fusion.21), channel_id=1, source_target_pairs={{0,1},{1,0},{2,3},{3,2},{4,5},{5,4},{6,7},{7,6},{8,9},{9,8},{10,11... | collective-permute-start | bytes 9224 | tf_op jit(solution)/shard_map/ppermute | solution.py:51
  228.0 4.8 %collective-permute-start.42 = (f32[3,256]{1,0:T(4,128)S(1)}, f32[3,256]{1,0:T(4,128)S(1)}, u32[]{:S(2)}, u32[]{:S(2)}) collective-permute-start(f32[3,256]{1,0:T(4,128)S(1)} %pad_maximum_fusion.21), channel_id=1, source_target_pairs={{0,2},{1,3},{2,0},{3,1},{4,6},{5,7},{6,4},{7,5},{8,10},{9,11},{10,... | collective-permute-start | bytes 9224 | tf_op jit(solution)/shard_map/ppermute | solution.py:51
  231.1 5.4 %collective-permute-start.43 = (f32[3,256]{1,0:T(4,128)S(1)}, f32[3,256]{1,0:T(4,128)S(1)}, u32[]{:S(2)}, u32[]{:S(2)}) collective-permute-start(f32[3,256]{1,0:T(4,128)S(1)} %pad_maximum_fusion.21), channel_id=1, source_target_pairs={{0,3},{1,2},{2,1},{3,0},{4,7},{5,6},{6,5},{7,4},{8,11},{9,10},{10,... | collective-permute-start | bytes 9224 | tf_op jit(solution)/shard_map/ppermute | solution.py:51
  241.7 4.5 %collective-permute-start.48 = (f32[2,256]{1,0:T(2,128)S(1)}, f32[2,256]{1,0:T(2,128)S(1)}, u32[]{:S(2)}, u32[]{:S(2)}) collective-permute-start(f32[2,256]{1,0:T(2,128)S(1)} %fusion.70), channel_id=1, source_target_pairs={{0,24},{1,25},{2,26},{3,27},{4,28},{5,29},{6,30},{7,31},{8,16},{9,... | collective-permute-start | bytes 6152 | tf_op jit(solution)/shard_map/ppermute | solution.py:51
  246.2 4.5 %collective-permute-start.49 = (f32[2,256]{1,0:T(2,128)S(1)}, f32[2,256]{1,0:T(2,128)S(1)}, u32[]{:S(2)}, u32[]{:S(2)}) collective-permute-start(f32[2,256]{1,0:T(2,128)S(1)} %add_add_fusion.7), channel_id=1, source_target_pairs={{0,1},{1,0},{2,3},{3,2},{4,5},{5,4},{6,7},{7,6},{8,9},{9,8},{10,11... | collective-permute-start | bytes 6152 | tf_op jit(solution)/shard_map/ppermute | solution.py:51
  246.3 4.5 %collective-permute-start.50 = (f32[2,256]{1,0:T(2,128)S(1)}, f32[2,256]{1,0:T(2,128)S(1)}, u32[]{:S(2)}, u32[]{:S(2)}) collective-permute-start(f32[2,256]{1,0:T(2,128)S(1)} %add_add_fusion.7), channel_id=1, source_target_pairs={{0,2},{1,3},{2,0},{3,1},{4,6},{5,7},{6,4},{7,5},{8,10},{9,11},{10,... | collective-permute-start | bytes 6152 | tf_op jit(solution)/shard_map/ppermute | solution.py:51
  248.0 5.4 %collective-permute-start.51 = (f32[2,256]{1,0:T(2,128)S(1)}, f32[2,256]{1,0:T(2,128)S(1)}, u32[]{:S(2)}, u32[]{:S(2)}) collective-permute-start(f32[2,256]{1,0:T(2,128)S(1)} %add_add_fusion.7), channel_id=1, source_target_pairs={{0,3},{1,2},{2,1},{3,0},{4,7},{5,6},{6,5},{7,4},{8,11},{9,10},{10,... | collective-permute-start | bytes 6152 | tf_op jit(solution)/shard_map/ppermute | solution.py:51
  250.7 14.4 %collective-permute-start.52 = (bf16[16,512]{1,0:T(8,128)(2,1)S(1)}, bf16[16,512]{1,0:T(8,128)(2,1)S(1)}, u32[]{:S(2)}, u32[]{:S(2)}) collective-permute-start(bf16[16,512]{1,0:T(8,128)(2,1)S(1)} %copy-done.33), channel_id=1, source_target_pairs={{0,2},{1,3},{2,0},{3,1},{4,6},{5,7},{6,4},{7,5},{8,10},{9,11},{10,... | collective-permute-start | bytes 49160 | tf_op jit(solution)/shard_map/ppermute | solution.py:51
  250.7 12.7 %collective-permute-start.44 = (bf16[432,256]{1,0:T(8,128)(2,1)}, bf16[432,256]{1,0:T(8,128)(2,1)S(1)}, u32[]{:S(2)}, u32[]{:S(2)}) collective-permute-start(bf16[432,256]{1,0:T(8,128)(2,1)} %get-tuple-element.179), channel_id=1, source_target_pairs={{0,6},{1,7},{2,4},{3,5},{4,2},{5,3},{6,0},{7,1},{8,14},{9,15},{10,... | collective-permute-start | bytes 663560 | tf_op jit(solution)/shard_map/ppermute | solution.py:51
  267.5 4.6 %collective-permute-start.56 = (f32[16,256]{1,0:T(8,128)S(1)}, f32[16,256]{1,0:T(8,128)S(1)}, u32[]{:S(2)}, u32[]{:S(2)}) collective-permute-start(f32[16,256]{1,0:T(8,128)S(1)} %add.456), channel_id=1, source_target_pairs={{0,24},{1,25},{2,26},{3,27},{4,28},{5,29},{6,30},{7,31},{8,16},{9,... | collective-permute-start | bytes 49160 | tf_op jit(solution)/shard_map/ppermute | solution.py:51
  272.2 4.5 %collective-permute-start.57 = (f32[16,256]{1,0:T(8,128)S(1)}, f32[16,256]{1,0:T(8,128)S(1)}, u32[]{:S(2)}, u32[]{:S(2)}) collective-permute-start(f32[16,256]{1,0:T(8,128)S(1)} %add_add_fusion.3), channel_id=1, source_target_pairs={{0,1},{1,0},{2,3},{3,2},{4,5},{5,4},{6,7},{7,6},{8,9},{9,8},{10,11... | collective-permute-start | bytes 49160 | tf_op jit(solution)/shard_map/ppermute | solution.py:51
  272.2 4.7 %collective-permute-start.58 = (f32[16,256]{1,0:T(8,128)S(1)}, f32[16,256]{1,0:T(8,128)S(1)}, u32[]{:S(2)}, u32[]{:S(2)}) collective-permute-start(f32[16,256]{1,0:T(8,128)S(1)} %add_add_fusion.3), channel_id=1, source_target_pairs={{0,2},{1,3},{2,0},{3,1},{4,6},{5,7},{6,4},{7,5},{8,10},{9,11},{10,... | collective-permute-start | bytes 49160 | tf_op jit(solution)/shard_map/ppermute | solution.py:51
  274.9 5.5 %collective-permute-start.59 = (f32[16,256]{1,0:T(8,128)S(1)}, f32[16,256]{1,0:T(8,128)S(1)}, u32[]{:S(2)}, u32[]{:S(2)}) collective-permute-start(f32[16,256]{1,0:T(8,128)S(1)} %add_add_fusion.3), channel_id=1, source_target_pairs={{0,3},{1,2},{2,1},{3,0},{4,7},{5,6},{6,5},{7,4},{8,11},{9,10},{10,... | collective-permute-start | bytes 49160 | tf_op jit(solution)/shard_map/ppermute | solution.py:51
  283.4 28.3 %collective-permute-start.60 = (bf16[432,1024]{1,0:T(8,128)(2,1)}, bf16[432,1024]{1,0:T(8,128)(2,1)}, u32[]{:S(2)}, u32[]{:S(2)}) collective-permute-start(bf16[432,1024]{1,0:T(8,128)(2,1)} %pad_maximum_fusion.4.refs_0_.refs_4_), channel_id=1, source_target_pairs={{0,1},{1,0},{2,3},{3,2},{4,5},{5,4},{6,7},{7,6},{8,9},{9,8},{10,11... | collective-permute-start | bytes 2654216 | tf_op jit(solution)/shard_map/ppermute | solution.py:51
  283.6 25.8 %collective-permute-start.61 = (bf16[432,512]{1,0:T(8,128)(2,1)S(1)}, bf16[432,512]{1,0:T(8,128)(2,1)S(1)}, u32[]{:S(2)}, u32[]{:S(2)}) collective-permute-start(bf16[432,512]{1,0:T(8,128)(2,1)S(1)} %pad_maximum_fusion.9), channel_id=1, source_target_pairs={{0,2},{1,3},{2,0},{3,1},{4,6},{5,7},{6,4},{7,5},{8,10},{9,11},{10,... | collective-permute-start | bytes 1327112 | tf_op jit(solution)/shard_map/ppermute | solution.py:51
  285.9 28.9 %collective-permute-start.62 = (bf16[432,1024]{1,0:T(8,128)(2,1)}, bf16[432,1024]{1,0:T(8,128)(2,1)}, u32[]{:S(2)}, u32[]{:S(2)}) collective-permute-start(bf16[432,1024]{1,0:T(8,128)(2,1)} %pad_maximum_fusion.4.refs_0_.refs_4_), channel_id=1, source_target_pairs={{0,4},{1,5},{2,6},{3,7},{4,0},{5,1},{6,2},{7,3},{8,12},{9,13},{10,... | collective-permute-start | bytes 2654216 | tf_op jit(solution)/shard_map/ppermute | solution.py:51
  313.7 26.6 %collective-permute-start.68 = (bf16[432,512]{1,0:T(8,128)(2,1)}, bf16[432,512]{1,0:T(8,128)(2,1)S(1)}, u32[]{:S(2)}, u32[]{:S(2)}) collective-permute-start(bf16[432,512]{1,0:T(8,128)(2,1)} %copy-done.64), channel_id=1, source_target_pairs={{0,1},{1,0},{2,3},{3,2},{4,5},{5,4},{6,7},{7,6},{8,9},{9,8},{10,11... | collective-permute-start | bytes 1327112 | tf_op jit(solution)/shard_map/ppermute | solution.py:51
  315.5 24.5 %collective-permute-start.69 = (bf16[64,1280]{1,0:T(8,128)(2,1)S(1)}, bf16[64,1280]{1,0:T(8,128)(2,1)S(1)}, u32[]{:S(2)}, u32[]{:S(2)}) collective-permute-start(bf16[64,1280]{1,0:T(8,128)(2,1)S(1)} %get-tuple-element.170), channel_id=1, source_target_pairs={{0,1},{1,0},{2,3},{3,2},{4,5},{5,4},{6,7},{7,6},{8,9},{9,8},{10,11... | collective-permute-start | bytes 491528 | tf_op jit(solution)/shard_map/ppermute | solution.py:51
  316.4 23.7 %collective-permute-start.70 = (bf16[64,1280]{1,0:T(8,128)(2,1)S(1)}, bf16[64,1280]{1,0:T(8,128)(2,1)S(1)}, u32[]{:S(2)}, u32[]{:S(2)}) collective-permute-start(bf16[64,1280]{1,0:T(8,128)(2,1)S(1)} %get-tuple-element.171), channel_id=1, source_target_pairs={{0,2},{1,3},{2,0},{3,1},{4,6},{5,7},{6,4},{7,5},{8,10},{9,11},{10,... | collective-permute-start | bytes 491528 | tf_op jit(solution)/shard_map/ppermute | solution.py:51
  318.3 21.8 %collective-permute-start.71 = (bf16[64,1280]{1,0:T(8,128)(2,1)S(1)}, bf16[64,1280]{1,0:T(8,128)(2,1)S(1)}, u32[]{:S(2)}, u32[]{:S(2)}) collective-permute-start(bf16[64,1280]{1,0:T(8,128)(2,1)S(1)} %get-tuple-element.172), channel_id=1, source_target_pairs={{0,3},{1,2},{2,1},{3,0},{4,7},{5,6},{6,5},{7,4},{8,11},{9,10},{10,... | collective-permute-start | bytes 491528 | tf_op jit(solution)/shard_map/ppermute | solution.py:51
  319.9 23.8 %collective-permute-start.73 = (bf16[224,512]{1,0:T(8,128)(2,1)S(1)}, bf16[224,512]{1,0:T(8,128)(2,1)S(1)}, u32[]{:S(2)}, u32[]{:S(2)}) collective-permute-start(bf16[224,512]{1,0:T(8,128)(2,1)S(1)} %get-tuple-element.98), channel_id=1, source_target_pairs={{0,3},{1,2},{2,1},{3,0},{4,7},{5,6},{6,5},{7,4},{8,11},{9,10},{10,... | collective-permute-start | bytes 688136 | tf_op jit(solution)/shard_map/ppermute | solution.py:51
  340.0 13.6 %collective-permute-start.72 = (bf16[224,512]{1,0:T(8,128)(2,1)S(1)}, bf16[224,512]{1,0:T(8,128)(2,1)S(1)}, u32[]{:S(2)}, u32[]{:S(2)}) collective-permute-start(bf16[224,512]{1,0:T(8,128)(2,1)S(1)} %get-tuple-element.97), channel_id=1, source_target_pairs={{0,2},{1,3},{2,0},{3,1},{4,6},{5,7},{6,4},{7,5},{8,10},{9,11},{10,... | collective-permute-start | bytes 688136 | tf_op jit(solution)/shard_map/ppermute | solution.py:51
  379.9 13.2 %collective-permute-start.76 = (bf16[29,64,128]{2,1,0:T(8,128)(2,1)}, bf16[29,64,128]{2,1,0:T(8,128)(2,1)S(1)}, u32[]{:S(2)}, u32[]{:S(2)}) collective-permute-start(bf16[29,64,128]{2,1,0:T(8,128)(2,1)} %get-tuple-element.103), channel_id=1, source_target_pairs={{0,16},{1,17},{2,18},{3,19},{4,20},{5,21},{6,22},{7,23},{8,24},{9,... | collective-permute-start | bytes 1425416 | tf_op jit(solution)/shard_map/ppermute | solution.py:51
  381.8 21.8 %collective-permute-start.64 = (bf16[432,512]{1,0:T(8,128)(2,1)S(1)}, bf16[432,512]{1,0:T(8,128)(2,1)S(1)}, u32[]{:S(2)}, u32[]{:S(2)}) collective-permute-start(bf16[432,512]{1,0:T(8,128)(2,1)S(1)} %copy-done.68), channel_id=1, source_target_pairs={{0,2},{1,3},{2,0},{3,1},{4,6},{5,7},{6,4},{7,5},{8,10},{9,11},{10,... | collective-permute-start | bytes 1327112 | tf_op jit(solution)/shard_map/ppermute | solution.py:51
  382.2 13.7 %collective-permute-start.78 = (bf16[29,64,128]{2,1,0:T(8,128)(2,1)}, bf16[29,64,128]{2,1,0:T(8,128)(2,1)S(1)}, u32[]{:S(2)}, u32[]{:S(2)}) collective-permute-start(bf16[29,64,128]{2,1,0:T(8,128)(2,1)} %get-tuple-element.107), channel_id=1, source_target_pairs={{0,8},{1,9},{2,10},{3,11},{4,12},{5,13},{6,14},{7,15},{8,0},{9,1},... | collective-permute-start | bytes 1425416 | tf_op jit(solution)/shard_map/ppermute | solution.py:51
  383.7 16.0 %collective-permute-start.82 = (bf16[4,64,160]{2,1,0:T(8,128)(2,1)S(1)}, bf16[4,64,160]{2,1,0:T(8,128)(2,1)S(1)}, u32[]{:S(2)}, u32[]{:S(2)}) collective-permute-start(bf16[4,64,160]{2,1,0:T(8,128)(2,1)S(1)} %select_bitcast_fusion.8), channel_id=1, source_target_pairs={{0,4},{1,5},{2,6},{3,7},{4,0},{5,1},{6,2},{7,3},{8,12},{9,13},{10,... | collective-permute-start | bytes 245768 | tf_op jit(solution)/shard_map/ppermute | solution.py:51
  394.4 29.1 %collective-permute-start.77 = (bf16[2,29,64,128]{3,2,1,0:T(8,128)(2,1)S(1)}, bf16[2,29,64,128]{3,2,1,0:T(8,128)(2,1)S(1)}, u32[]{:S(2)}, u32[]{:S(2)}) collective-permute-start(bf16[2,29,64,128]{3,2,1,0:T(8,128)(2,1)S(1)} %pad_maximum_fusion.1), channel_id=1, source_target_pairs={{0,8},{1,9},{2,10},{3,11},{4,12},{5,13},{6,14},{7,15},{8,0},{9,1},... | collective-permute-start | bytes 2850824 | tf_op jit(solution)/shard_map/ppermute | solution.py:51
  396.2 27.2 %collective-permute-start.79 = (bf16[2,29,64,128]{3,2,1,0:T(8,128)(2,1)S(1)}, bf16[2,29,64,128]{3,2,1,0:T(8,128)(2,1)S(1)}, u32[]{:S(2)}, u32[]{:S(2)}) collective-permute-start(bf16[2,29,64,128]{3,2,1,0:T(8,128)(2,1)S(1)} %pad_maximum_fusion.2), channel_id=1, source_target_pairs={{0,16},{1,17},{2,18},{3,19},{4,20},{5,21},{6,22},{7,23},{8,24},{9,... | collective-permute-start | bytes 2850824 | tf_op jit(solution)/shard_map/ppermute | solution.py:51
  397.6 24.8 %collective-permute-start.65 = (bf16[432,512]{1,0:T(8,128)(2,1)S(1)}, bf16[432,512]{1,0:T(8,128)(2,1)S(1)}, u32[]{:S(2)}, u32[]{:S(2)}) collective-permute-start(bf16[432,512]{1,0:T(8,128)(2,1)S(1)} %copy-done.67), channel_id=1, source_target_pairs={{0,1},{1,0},{2,3},{3,2},{4,5},{5,4},{6,7},{7,6},{8,9},{9,8},{10,11... | collective-permute-start | bytes 1327112 | tf_op jit(solution)/shard_map/ppermute | solution.py:51
  399.7 22.6 %collective-permute-start.66 = (bf16[432,512]{1,0:T(8,128)(2,1)S(1)}, bf16[432,512]{1,0:T(8,128)(2,1)S(1)}, u32[]{:S(2)}, u32[]{:S(2)}) collective-permute-start(bf16[432,512]{1,0:T(8,128)(2,1)S(1)} %copy-done.66), channel_id=1, source_target_pairs={{0,3},{1,2},{2,1},{3,0},{4,7},{5,6},{6,5},{7,4},{8,11},{9,10},{10,... | collective-permute-start | bytes 1327112 | tf_op jit(solution)/shard_map/ppermute | solution.py:51
  423.3 6.2 %collective-permute-start.67 = (bf16[2,432,512]{2,1,0:T(8,128)(2,1)S(1)}, bf16[2,432,512]{2,1,0:T(8,128)(2,1)S(1)}, u32[]{:S(2)}, u32[]{:S(2)}) collective-permute-start(bf16[2,432,512]{2,1,0:T(8,128)(2,1)S(1)} %pad_maximum_fusion.5), channel_id=1, source_target_pairs={{0,4},{1,5},{2,6},{3,7},{4,0},{5,1},{6,2},{7,3},{8,12},{9,13},{10,... | collective-permute-start | bytes 2654216 | tf_op jit(solution)/shard_map/ppermute | solution.py:51
  424.1 4.5 %collective-permute-start.83 = (bf16[2,64,160]{2,1,0:T(8,128)(2,1)S(1)}, bf16[2,64,160]{2,1,0:T(8,128)(2,1)S(1)}, u32[]{:S(2)}, u32[]{:S(2)}) collective-permute-start(bf16[2,64,160]{2,1,0:T(8,128)(2,1)S(1)} %fusion.24), channel_id=1, source_target_pairs={{0,8},{1,9},{2,10},{3,11},{4,12},{5,13},{6,14},{7,15},{8,0},{9,1},... | collective-permute-start | bytes 122888 | tf_op jit(solution)/shard_map/ppermute | solution.py:51
  426.3 13.0 %collective-permute-start.80 = (bf16[29,64,128]{2,1,0:T(8,128)(2,1)S(1)}, bf16[29,64,128]{2,1,0:T(8,128)(2,1)S(1)}, u32[]{:S(2)}, u32[]{:S(2)}) collective-permute-start(bf16[29,64,128]{2,1,0:T(8,128)(2,1)S(1)} %get-tuple-element.132), channel_id=1, source_target_pairs={{0,1},{1,0},{2,3},{3,2},{4,5},{5,4},{6,7},{7,6},{8,9},{9,8},{10,11... | collective-permute-start | bytes 1425416 | tf_op jit(solution)/shard_map/ppermute | solution.py:51
  428.7 4.9 %collective-permute-start.84 = (bf16[1,64,160]{2,1,0:T(8,128)(2,1)S(1)}, bf16[1,64,160]{2,1,0:T(8,128)(2,1)S(1)}, u32[]{:S(2)}, u32[]{:S(2)}) collective-permute-start(bf16[1,64,160]{2,1,0:T(8,128)(2,1)S(1)} %select_bitcast_fusion.13), channel_id=1, source_target_pairs={{0,16},{1,17},{2,18},{3,19},{4,20},{5,21},{6,22},{7,23},{8,24},{9,... | collective-permute-start | bytes 61448 | tf_op jit(solution)/shard_map/ppermute | solution.py:51
  (97 other events, 1023.9 us)
